TPU v7x, 32 devices: a whole 2x2x4 slice. The times are simulated.
32 devices in a mesh: gx: 16 (over z, x, core), gy: 2 (over y).
Axes of the slice: x: 2, y: 2, z: 4, core: 2. Of those that a mesh axis runs over, the one named last changes fastest.
Arguments:
- velocity: float32 [3, 32, 1024, 128], P(None, 'gx', 'gy'), may hold values from -4 to 4.5, as said below
- previous: float32 [3, 32, 1024, 128], P(None, 'gx', 'gy'), may hold values from -1800 to 1800
Outputs:
- advanced: float32 [3, 32, 1024, 128], P(None, 'gx', 'gy')
Inputs may be any that keep to these rules, and one draw needn't show every extreme that they name: `velocity`: each component is zero on the two walls, the first and the last wall-normal point.
All inputs are finite; a program needn't handle non-finite values.
Results may differ from a plain program's by a relative error of at most 0.0003.
Values sent between devices are 32-bit elements; how exact they have to be, the bound alone decides.
No kernel may reach another device: no remote copies, remote signals or barrier semaphores. Data moves between devices by JAX's collectives and lax.ppermute only.
A program may use at most 64 MiB of HBM per device.

v0:
```python
import jax
import jax.numpy as jnp
from jax import lax
from jax.sharding import PartitionSpec as P

NY = 1024


LENGTH_SPACING = 8.0 * 3.141592653589793 / 4096.0
SPAN_SPACING = 3.0 * 3.141592653589793 / 3072.0
VISCOSITY = 1.0 / 2000.0
TIME_STEP = 0.003
GAMMA_NOW = 5.0 / 12.0
ZETA_PAST = -17.0 / 60.0


def padded(cells, sides, width):
    for axis, dim in sides:
        count = lax.axis_size(axis)
        head = lax.slice_in_dim(cells, 0, width, axis=dim)
        tail = lax.slice_in_dim(cells, cells.shape[dim] - width, cells.shape[dim], axis=dim)
        cells = jnp.concatenate(
            [
                lax.ppermute(tail, axis, [(i, (i + 1) % count) for i in range(count)]),
                cells,
                lax.ppermute(head, axis, [((i + 1) % count, i) for i in range(count)]),
            ],
            axis=dim,
        )
    return cells


def chebyshev_rows(total, offset, count):
    row_ids = offset + jnp.arange(count, dtype=jnp.int32)
    col_ids = jnp.arange(total, dtype=jnp.int32)
    row_angle = jnp.pi * row_ids.astype(jnp.float32) / (total - 1)
    col_angle = jnp.pi * col_ids.astype(jnp.float32) / (total - 1)
    on_diagonal = row_ids[:, None] == col_ids[None, :]
    parity = (row_ids[:, None] + col_ids[None, :]) % 2
    signs = 1.0 - 2.0 * parity.astype(jnp.float32)
    row_half = jnp.where((row_ids == 0) | (row_ids == total - 1), 0.5, 1.0).astype(jnp.float32)
    col_half = jnp.where((col_ids == 0) | (col_ids == total - 1), 0.5, 1.0).astype(jnp.float32)
    weight_ratio = signs * col_half[None, :] / row_half[:, None]
    spacing = (
        -2.0
        * jnp.sin(0.5 * (row_angle[:, None] + col_angle[None, :]))
        * jnp.sin(0.5 * (row_angle[:, None] - col_angle[None, :]))
    )
    spacing_safe = jnp.where(on_diagonal, 1.0, spacing)
    first_off = jnp.where(on_diagonal, 0.0, weight_ratio / spacing_safe)
    first_diag = -jnp.sum(first_off, axis=1)
    first = first_off + jnp.where(on_diagonal, first_diag[:, None], 0.0)
    second_off = jnp.where(
        on_diagonal, 0.0, 2.0 * first_off * (first_diag[:, None] - 1.0 / spacing_safe)
    )
    second = second_off + jnp.where(on_diagonal, -jnp.sum(second_off, axis=1)[:, None], 0.0)
    return (first, second)


def central(center, plus_one, minus_one, plus_two, minus_two, spacing):
    first = (8.0 * (plus_one - minus_one) - (plus_two - minus_two)) / (12.0 * spacing)
    second = (16.0 * (plus_one + minus_one) - (plus_two + minus_two) - 30.0 * center) / (
        12.0 * spacing * spacing
    )
    return (first, second)


def shards(velocity, previous):
    widened = padded(velocity, (("gx", 1),), 2)
    along_x, across_x = central(
        widened[:, 2:-2],
        widened[:, 3:-1],
        widened[:, 1:-3],
        widened[:, 4:],
        widened[:, :-4],
        LENGTH_SPACING,
    )
    along_z, across_z = central(
        velocity,
        jnp.roll(velocity, -1, 3),
        jnp.roll(velocity, 1, 3),
        jnp.roll(velocity, -2, 3),
        jnp.roll(velocity, 2, 3),
        SPAN_SPACING,
    )
    plane_term = (
        VISCOSITY * (across_x + across_z) - velocity[0:1] * along_x - velocity[2:3] * along_z
    )
    local_rows = velocity.shape[2]
    offset = lax.axis_index("gy") * local_rows
    first_rows, second_rows = chebyshev_rows(NY, offset, local_rows)
    operators = jnp.concatenate([first_rows, second_rows], axis=0)
    added = jnp.einsum(
        "ky,cxyz->cxkz",
        operators,
        lax.all_gather(velocity, "gy", axis=2, tiled=True),
        precision=lax.Precision.HIGHEST,
    )
    wall_first = added[:, :, :local_rows]
    wall_second = added[:, :, local_rows:]
    wall_term = VISCOSITY * wall_second - velocity[1:2] * wall_first
    tendency = plane_term + wall_term
    return velocity + TIME_STEP * (GAMMA_NOW * tendency + ZETA_PAST * previous)


def solution(mesh):
    in_specs = (P(None, "gx", "gy", None), P(None, "gx", "gy", None))
    out_specs = P(None, "gx", "gy", None)
    return jax.shard_map(shards, mesh=mesh, in_specs=in_specs, out_specs=out_specs, check_vma=False)
```

profile of v0, /device:TPU:0, one launch (start us, length us, event | category | flops | bytes accessed | tf_op | source)
XLA Modules:
  0.0 97.7 jit_solution(611484043620523764)
XLA Ops:
  6.5 0.0 copy-start
  6.5 0.0 all-gather.2.cloned.1.call-start
  6.5 0.7 all-gather.2.cloned.1.call-update
  7.3 5.5 %collective-permute-start = (f32[3,2,512,128]{3,2,1,0:T(8,128)}, f32[3,2,512,128]{3,2,1,0:T(8,128)}, u32[]{:S(2)}, u32[]{:S(2)}) collective-permute-start(f32[3,2,512,128]{3,2,1,0:T(8,128)} %param.2), channel_id=1, source_target_pairs={{2,0},{4,2},{6,4},{8,6},{10,8},{12,10},{14,12},{16,14},{18,16},{20... | collective-permute-start | bytes 4718600 | tf_op jit(solution)/shard_map/ppermute | solution.py:26
  12.7 0.0 collective-permute-start.1
  12.8 0.0 copy-done
  12.8 1.7 %fusion.30 = (f32[3,2,512,1]{3,2,1,0:T(8,128)S(1)}, f32[3,2,512,1]{3,2,1,0:T(8,128)}) fusion(f32[3,2,512,128]{3,2,1,0:T(8,128)S(1)} %copy-done), kind=kLoop, calls=%fused_computation.55 | loop fusion | bytes 49152 | tf_op jit(solution)/shard_map/jit(_roll_static)/slice | solution.py:80
  14.4 16.0 %fusion.20 = f32[512]{0:T(512)S(1)} fusion(f32[1024]{0:T(1024)S(1)} %get-tuple-element.20, f32[512]{0:T(512)S(1)} %get-tuple-element.18, f32[512]{0:T(512)S(1)} %get-tuple-element.19, f32[1024]{0:T(1024)S(1)} %get-tuple-element.21, s32[512]{0:T(512)S(1)} %iota_add_fusion), kind=kLoop, calls=%fused_computation.37 | loop fusion | flops 14679552 | bytes 16384 | tf_op jit(solution)/shard_map/reduce_sum | solution.py:51
  30.5 2.2 %fusion.31 = (f32[3,2,512,126]{3,2,1,0:T(8,128)}, f32[3,2,512,126]{3,2,1,0:T(8,128)}) fusion(f32[3,2,512,128]{3,2,1,0:T(8,128)S(1)} %copy-done), kind=kLoop, calls=%fused_computation.56 | loop fusion | bytes 6193152 | tf_op jit(solution)/shard_map/jit(_roll_static)/slice | solution.py:82
  32.6 2.2 %fusion.32 = (f32[3,2,512,2]{3,2,1,0:T(8,128)}, f32[3,2,512,2]{3,2,1,0:T(8,128)}) fusion(f32[3,2,512,128]{3,2,1,0:T(8,128)S(1)} %copy-done), kind=kLoop, calls=%fused_computation.57 | loop fusion | bytes 98304 | tf_op jit(solution)/shard_map/jit(_roll_static)/slice | solution.py:82
  34.8 2.2 %fusion.29 = (f32[3,2,512,127]{3,2,1,0:T(8,128)}, f32[3,2,512,127]{3,2,1,0:T(8,128)}) fusion(f32[3,2,512,128]{3,2,1,0:T(8,128)S(1)} %copy-done), kind=kLoop, calls=%fused_computation.54 | loop fusion | bytes 6242304 | tf_op jit(solution)/shard_map/jit(_roll_static)/slice | solution.py:80
  37.0 16.4 %fusion.21 = f32[512]{0:T(512)S(1)} fusion(f32[512]{0:T(512)S(1)} %neg.15, f32[1024]{0:T(1024)S(1)} %get-tuple-element.20, f32[512]{0:T(512)S(1)} %get-tuple-element.18, f32[512]{0:T(512)S(1)} %get-tuple-element.19, f32[1024]{0:T(1024)S(1)} %get-tuple-element.21, s32[512]{0:T(512)S(1)} %iota_add_fusion), kind=kLoop, calls=%fused_computation.38 | loop fusion | flops 17300992 | bytes 18432 | tf_op jit(solution)/shard_map/reduce_sum | solution.py:56
  53.4 1.2 %multiply_bitcast_fusion.1 = (f32[2,512,128]{2,1,0:T(8,128)}, f32[2,512,128]{2,1,0:T(8,128)}, f32[2,512,128]{2,1,0:T(8,128)}) fusion(f32[3,2,512,128]{3,2,1,0:T(8,128)S(1)} %copy-done), kind=kLoop, calls=%fused_computation.41 | loop fusion | flops 262144 | bytes 3145728 | tf_op jit(solution)/shard_map/mul | solution.py:87
  54.6 17.8 %select_add_fusion.1 = (f32[512,1024]{1,0:T(8,128)}, f32[512,1024]{1,0:T(8,128)}) fusion(f32[512]{0:T(512)S(1)} %neg.15, s32[512]{0:T(512)S(1)} %iota_add_fusion, f32[1024]{0:T(1024)S(1)} %get-tuple-element.20, f32[512]{0:T(512)S(1)} %get-tuple-element.18, f32[512]{0:T(512)S(1)} %get-tuple-element.19, f32[1024]{0:T(1024)S(1)} %get-tuple-element.21, ...), kind=kLoop, calls=%fused_computation.16 | loop fusion | flops 18874368 | bytes 4212736 | tf_op jit(solution)/shard_map/add | solution.py:52
  72.4 0.0 all-gather.2.cloned.1.call-done
  72.4 0.0 copy-start.1
  72.4 0.0 copy-start.2
  72.4 0.0 copy-start.3
  72.4 0.0 copy-start.4
  72.4 0.0 copy-start.5
  72.4 0.0 copy-start.6
  72.4 0.0 copy-start.7
  72.5 0.0 copy-start.8
  72.5 0.0 copy-start.9
  72.5 0.0 copy-start.10
  72.5 12.7 %fusion.13 = f32[3,2,1024,128]{3,2,1,0:T(8,128)S(1)} fusion(f32[3,2,1024,128]{3,2,1,0:T(8,128)} %all-gather.2.cloned.1.call-done, f32[512,1024]{1,0:T(8,128)} %get-tuple-element.17, f32[512,1024]{1,0:T(8,128)} %get-tuple-element.16), kind=kOutput, calls=%fused_computation.22 | convolution fusion | flops 9664724992 | bytes 10485760 | tf_op jit(solution)/shard_map/ky,cxyz->cxkz/dot_general | solution.py:93
  85.2 0.0 collective-permute-done
  85.2 0.0 collective-permute-done.1
  85.2 0.0 copy-done.1
  85.2 0.0 copy-done.2
  85.2 0.0 copy-done.3
  85.2 0.0 copy-done.4
  85.2 0.0 copy-done.5
  85.2 0.0 copy-done.6
  85.3 0.0 copy-done.7
  85.3 0.0 copy-done.8
  85.3 0.0 copy-done.9
  85.3 0.0 copy-done.10
  85.3 5.6 %fusion.19 = f32[3,2,512,128]{3,2,1,0:T(8,128)} fusion(f32[3,2,512,128]{3,2,1,0:T(8,128)S(1)} %copy-done, f32[3,2,1024,128]{3,2,1,0:T(8,128)S(1)} %fusion.13, f32[3,2,512,128]{3,2,1,0:T(8,128)} %param.3, f32[3,2,512,128]{3,2,1,0:T(8,128)} %collective-permute-done, f32[3,2,512,128]{3,2,1,0:T(8,128)} %collective-permute-done.1, ...), kind=kLoop, calls=%fused_computation.29 | loop fusion | flops 16515072 | bytes 18874368 | tf_op jit(solution)/shard_map/add | solution.py:103
  (5 shorter events, 0.0 us)
Async XLA Ops:
  6.5 6.2 %copy-start = (f32[3,2,512,128]{3,2,1,0:T(8,128)S(1)}, f32[3,2,512,128]{3,2,1,0:T(8,128)}, u32[]{:S(2)}) copy-start(f32[3,2,512,128]{3,2,1,0:T(8,128)} %param.2) | copy-start | bytes 4718596
  6.5 65.9 %all-gather.2.cloned.1.call-start = ((), (), s32[]{:S(2)}) async-start(), calls=%async_computation | async-start | bytes 4718592 | tf_op jit(solution)/shard_map/all_gather | solution.py:96
  7.3 77.9 %collective-permute-start = (f32[3,2,512,128]{3,2,1,0:T(8,128)}, f32[3,2,512,128]{3,2,1,0:T(8,128)}, u32[]{:S(2)}, u32[]{:S(2)}) collective-permute-start(f32[3,2,512,128]{3,2,1,0:T(8,128)} %param.2), channel_id=1, source_target_pairs={{2,0},{4,2},{6,4},{8,6},{10,8},{12,10},{14,12},{16,14},{18,16},{20... | collective-permute-start | bytes 4718600 | tf_op jit(solution)/shard_map/ppermute | solution.py:26
  12.7 72.5 %collective-permute-start.1 = (f32[3,2,512,128]{3,2,1,0:T(8,128)}, f32[3,2,512,128]{3,2,1,0:T(8,128)}, u32[]{:S(2)}, u32[]{:S(2)}) collective-permute-start(f32[3,2,512,128]{3,2,1,0:T(8,128)} %param.2), channel_id=1, source_target_pairs={{0,2},{2,4},{4,6},{6,8},{8,10},{10,12},{12,14},{14,16},{16,18},{18... | collective-permute-start | bytes 4718600 | tf_op jit(solution)/shard_map/ppermute | solution.py:24
  72.4 12.8 %copy-start.1 = (f32[3,2,512,1]{3,2,1,0:T(8,128)S(1)}, f32[3,2,512,1]{3,2,1,0:T(8,128)}, u32[]{:S(2)}) copy-start(f32[3,2,512,1]{3,2,1,0:T(8,128)} %get-tuple-element.11) | copy-start | bytes 36868
  72.4 12.8 %copy-start.2 = (f32[3,2,512,126]{3,2,1,0:T(8,128)S(1)}, f32[3,2,512,126]{3,2,1,0:T(8,128)}, u32[]{:S(2)}) copy-start(f32[3,2,512,126]{3,2,1,0:T(8,128)} %get-tuple-element.12) | copy-start | bytes 4644868
  72.4 12.8 %copy-start.3 = (f32[3,2,512,126]{3,2,1,0:T(8,128)S(1)}, f32[3,2,512,126]{3,2,1,0:T(8,128)}, u32[]{:S(2)}) copy-start(f32[3,2,512,126]{3,2,1,0:T(8,128)} %get-tuple-element.13) | copy-start | bytes 4644868
  72.4 12.8 %copy-start.4 = (f32[3,2,512,2]{3,2,1,0:T(8,128)S(1)}, f32[3,2,512,2]{3,2,1,0:T(8,128)}, u32[]{:S(2)}) copy-start(f32[3,2,512,2]{3,2,1,0:T(8,128)} %get-tuple-element.14) | copy-start | bytes 73732
  72.4 12.8 %copy-start.5 = (f32[3,2,512,2]{3,2,1,0:T(8,128)S(1)}, f32[3,2,512,2]{3,2,1,0:T(8,128)}, u32[]{:S(2)}) copy-start(f32[3,2,512,2]{3,2,1,0:T(8,128)} %get-tuple-element.15) | copy-start | bytes 73732
  72.4 12.8 %copy-start.6 = (f32[3,2,512,127]{3,2,1,0:T(8,128)S(1)}, f32[3,2,512,127]{3,2,1,0:T(8,128)}, u32[]{:S(2)}) copy-start(f32[3,2,512,127]{3,2,1,0:T(8,128)} %get-tuple-element.8) | copy-start | bytes 4681732
  72.4 12.8 %copy-start.7 = (f32[3,2,512,127]{3,2,1,0:T(8,128)S(1)}, f32[3,2,512,127]{3,2,1,0:T(8,128)}, u32[]{:S(2)}) copy-start(f32[3,2,512,127]{3,2,1,0:T(8,128)} %get-tuple-element.9) | copy-start | bytes 4681732
  72.5 12.8 %copy-start.8 = (f32[2,512,128]{2,1,0:T(8,128)S(1)}, f32[2,512,128]{2,1,0:T(8,128)}, u32[]{:S(2)}) copy-start(f32[2,512,128]{2,1,0:T(8,128)} %get-tuple-element.5) | copy-start | bytes 1572868
  72.5 12.8 %copy-start.9 = (f32[2,512,128]{2,1,0:T(8,128)S(1)}, f32[2,512,128]{2,1,0:T(8,128)}, u32[]{:S(2)}) copy-start(f32[2,512,128]{2,1,0:T(8,128)} %get-tuple-element.6) | copy-start | bytes 1572868
  72.5 12.8 %copy-start.10 = (f32[2,512,128]{2,1,0:T(8,128)S(1)}, f32[2,512,128]{2,1,0:T(8,128)}, u32[]{:S(2)}) copy-start(f32[2,512,128]{2,1,0:T(8,128)} %get-tuple-element.7) | copy-start | bytes 1572868
Sparse Core Ops, SparseCore 0:
  8.9 47.6 all-gather.1
where the time goes:
time: 97.9 us; the launch traced here: 97.7 us
  other arithmetic  57 us (58%)
  between operations  13.6 us (14%)
  matrix products  12.7 us (13%)
  local copies, waits for them, and re-layouts  8.25 us (8%)
  starting transfers between devices  5.47 us (6%)
    add x1, other arithmetic, chebyshev_rows(): first = first_off + jnp.where(on_diagonal, first_diag[:, None], 0.0)  17.8 us
    reduce_sum x1, other arithmetic, chebyshev_rows(): jnp.sum(second_off, axis=1)[:, None]  16.4 us
    reduce_sum x1, other arithmetic, chebyshev_rows(): first_diag = -jnp.sum(first_off, axis=1)  16 us
    dot_general x1, matrix products, shards(): jnp.einsum('ky,cxyz->cxkz', operators, lax.all_gather(velocity, 'gy', axi...  12.7 us
    add x1, other arithmetic, shards(): return velocity + TIME_STEP * (GAMMA_NOW * tendency + ZETA_PAST * previous)  5.57 us
    ppermute x1, starting transfers between devices, padded(): lax.ppermute(head, axis, [((i + 1) % count, i) for i in range(count)])  5.47 us
    slice x2, local copies, waits for them, and re-layouts, shards(): jnp.roll(velocity, -2, 3)  4.39 us
    slice x2, local copies, waits for them, and re-layouts, shards(): jnp.roll(velocity, -1, 3)  3.82 us
  transfers between devices with their start and end apart: 3, of which 0 were waited for; matrix products, arithmetic and copies ran while one was open for 74% of the time, Pallas kernels for 0%

commit v1 on v0

v1 whole, which is shorter than its diff:
```python
import functools

import jax
import jax.numpy as jnp
import numpy as np
from jax import lax
from jax.experimental import pallas as pl
from jax.experimental.pallas import tpu as pltpu
from jax.sharding import PartitionSpec as P

NY = 1024


LENGTH_SPACING = 8.0 * 3.141592653589793 / 4096.0
SPAN_SPACING = 3.0 * 3.141592653589793 / 3072.0
VISCOSITY = 1.0 / 2000.0
TIME_STEP = 0.003
GAMMA_NOW = 5.0 / 12.0
ZETA_PAST = -17.0 / 60.0

SCALE = TIME_STEP * GAMMA_NOW
X_FIRST = SCALE / (12.0 * LENGTH_SPACING)
X_SECOND = SCALE * VISCOSITY / (12.0 * LENGTH_SPACING * LENGTH_SPACING)
Z_FIRST = SCALE / (12.0 * SPAN_SPACING)
Z_SECOND = SCALE * VISCOSITY / (12.0 * SPAN_SPACING * SPAN_SPACING)
PAST = TIME_STEP * ZETA_PAST

VMEM_LIMIT = 48 * 1024 * 1024


def chebyshev_matrices(total):
    one = np.float32(1.0)
    ids = np.arange(total, dtype=np.int32)
    angle = np.float32(np.pi) * ids.astype(np.float32) / np.float32(total - 1)
    on_diagonal = ids[:, None] == ids[None, :]
    signs = one - np.float32(2.0) * ((ids[:, None] + ids[None, :]) % 2).astype(np.float32)
    half = np.where((ids == 0) | (ids == total - 1), 0.5, 1.0).astype(np.float32)
    weight_ratio = signs * half[None, :] / half[:, None]
    spacing = (
        np.float32(-2.0)
        * np.sin(np.float32(0.5) * (angle[:, None] + angle[None, :]))
        * np.sin(np.float32(0.5) * (angle[:, None] - angle[None, :]))
    )
    spacing = np.where(on_diagonal, one, spacing)
    first = np.where(on_diagonal, np.float32(0.0), weight_ratio / spacing)
    first_diag = -np.sum(first, axis=1, dtype=np.float32)
    second = np.where(
        on_diagonal,
        np.float32(0.0),
        np.float32(2.0) * first * (first_diag[:, None] - one / spacing),
    )
    second_diag = -np.sum(second, axis=1, dtype=np.float32)
    first[ids, ids] = first_diag
    second[ids, ids] = second_diag
    return first, second


def operator_blocks(total, parts):
    first, second = chebyshev_matrices(total)
    rows = total // parts
    stacked = np.stack(
        [first.astype(np.float64) * SCALE, second.astype(np.float64) * (SCALE * VISCOSITY)]
    ).astype(np.float32)
    blocks = stacked.reshape(2, parts, rows, parts, rows).transpose(1, 3, 0, 2, 4)
    blocks = blocks.reshape(parts, parts, 2 * rows, rows)
    high = blocks.astype(jnp.bfloat16)
    low = (blocks - high.astype(np.float32)).astype(jnp.bfloat16)
    return np.stack([high, low], axis=2)


def wall(operators, fields, v):
    rows = v.shape[1]
    side = jnp.concatenate([fields[0], fields[1]], axis=1)
    high = side.astype(jnp.bfloat16)
    low = (side - high.astype(jnp.float32)).astype(jnp.bfloat16)
    dot = functools.partial(jnp.dot, preferred_element_type=jnp.float32)
    product = dot(operators[0, 0, 0], high) + (
        dot(operators[0, 0, 1], high) + dot(operators[0, 0, 0], low)
    )
    first, second = product[:rows], product[rows:]
    return second - jnp.concatenate([v[0], v[1]], axis=1) * first


def local_kernel(where, operators, velocity, previous, out):
    q = pl.program_id(0)
    field = velocity[pl.ds(q, 1)][0]
    width = field.shape[2]
    added = wall(operators, field, velocity[1])
    parity = where[2]
    along = jnp.where(parity == 0, X_FIRST, -X_FIRST).astype(jnp.float32)
    roll = lambda f, k: pltpu.roll(f, k % width, 1)
    for plane in range(2):
        f, other = field[plane], field[1 - plane]
        u, w = velocity[0, plane], velocity[2, plane]
        step = X_FIRST if plane == 0 else -X_FIRST
        total = X_SECOND * (16.0 * other - 30.0 * f) - u * ((8.0 * step) * other)
        p1, m1, p2, m2 = roll(f, -1), roll(f, 1), roll(f, -2), roll(f, 2)
        total += Z_SECOND * (16.0 * (p1 + m1) - (p2 + m2) - 30.0 * f)
        total -= w * (Z_FIRST * (8.0 * (p1 - m1) - (p2 - m2)))
        total += added[:, plane * width : (plane + 1) * width]
        out[0, plane] = f + PAST * previous[0, plane] + total


def near_kernel(where, velocity, near, base, out):
    parity = where[2]
    inner, outer = 1 - parity, parity
    along = jnp.where(parity == 0, X_FIRST, -X_FIRST).astype(jnp.float32)
    first, second = near[0, parity], near[0, 1 - parity]
    out[0, outer] = base[0, outer] - X_SECOND * first + (along * velocity[0, outer]) * first
    out[0, inner] = (
        base[0, inner]
        + X_SECOND * (16.0 * first - second)
        - (along * velocity[0, inner]) * (8.0 * first - second)
    )


def far_kernel(where, velocity, far, base, out):
    parity = where[2]
    inner, outer = 1 - parity, parity
    along = jnp.where(parity == 0, X_FIRST, -X_FIRST).astype(jnp.float32)
    first, second = far[0, 1 - parity], far[0, parity]
    out[0, inner] = base[0, inner] - X_SECOND * first - (along * velocity[0, inner]) * first
    out[0, outer] = (
        base[0, outer]
        + X_SECOND * (16.0 * first - second)
        + (along * velocity[0, outer]) * (8.0 * first - second)
    )


def remote_kernel(where, operators, velocity, others, base, out):
    added = wall(operators, others[0], velocity[0])
    width = others.shape[3]
    for plane in range(2):
        out[0, plane] = base[0, plane] + added[:, plane * width : (plane + 1) * width]


def call(kernel, where, ins, specs, shape, flops, name):
    one = pl.BlockSpec((1,) + shape[1:], lambda q, where: (q, 0, 0, 0))
    size = int(np.prod(shape)) * 4
    return pl.pallas_call(
        kernel,
        grid_spec=pltpu.PrefetchScalarGridSpec(
            num_scalar_prefetch=1,
            grid=(shape[0],),
            in_specs=specs,
            out_specs=one,
        ),
        out_shape=jax.ShapeDtypeStruct(shape, jnp.float32),
        compiler_params=pltpu.CompilerParams(vmem_limit_bytes=VMEM_LIMIT),
        cost_estimate=pl.CostEstimate(flops=flops, bytes_accessed=4 * size, transcendentals=0),
        name=name,
    )(where, *ins)


def shards(parts, velocity, previous):
    count = lax.axis_size("gx")
    shape = velocity.shape
    assert shape[1] == 2 and count % 2 == 0
    rows = shape[2]
    me = lax.axis_index("gy")
    parity = lax.axis_index("gx") % 2

    outward = [(i, (i - 1) % count if i % 2 == 0 else (i + 1) % count) for i in range(count)]
    inward = [(i, i ^ 1) for i in range(count)]
    others = [
        lax.ppermute(velocity, "gy", [(i, (i + k) % parts) for i in range(parts)])
        for k in range(1, parts)
    ]
    far = lax.ppermute(velocity, "gx", outward)
    near = lax.ppermute(velocity, "gx", inward)

    blocks = jnp.asarray(operator_blocks(rows * parts, parts))

    def where(k):
        return jnp.stack([me, (me - k) % parts, parity]).astype(jnp.int32)

    one = pl.BlockSpec((1,) + shape[1:], lambda q, where: (q, 0, 0, 0))
    whole = pl.BlockSpec(shape, lambda q, where: (0, 0, 0, 0))
    u_only = pl.BlockSpec((1,) + shape[1:], lambda q, where: (0, 0, 0, 0))
    v_only = pl.BlockSpec((1,) + shape[1:], lambda q, where: (1, 0, 0, 0))
    block = pl.BlockSpec(
        (1, 1) + blocks.shape[2:], lambda q, where: (where[0], where[1], 0, 0, 0)
    )
    flops = 2 * 3 * 2 * rows * rows * 6 * shape[3]
    light = 20 * 6 * rows * shape[3]

    total = call(
        local_kernel, where(0), (blocks, velocity, previous), [block, whole, one], shape, flops, "local"
    )
    total = call(near_kernel, where(0), (velocity, near, total), [u_only, one, one], shape, light, "near")
    for k in range(1, parts):
        total = call(
            remote_kernel,
            where(k),
            (blocks, velocity, others[k - 1], total),
            [block, v_only, one, one],
            shape,
            flops,
            "remote",
        )
    return call(far_kernel, where(0), (velocity, far, total), [u_only, one, one], shape, light, "far")


def solution(mesh):
    spec = P(None, "gx", "gy", None)
    body = functools.partial(shards, mesh.shape["gy"])
    return jax.shard_map(body, mesh=mesh, in_specs=(spec, spec), out_specs=spec, check_vma=False)
```

time: 97.9 us -> 46.8 us (0.48)
  the two profiles are of different devices: /device:TPU:0 before, /device:TPU:1 now
where the time goes in v1:
time: 46.8 us; the launch traced here: 46 us
  waiting for transfers between devices  19.4 us (41%)
  Pallas kernels  17.3 us (37%)
  local copies, waits for them, and re-layouts  5.09 us (11%)
  starting transfers between devices  4.12 us (9%)
    ppermute x1, waiting for transfers between devices, shards(): lax.ppermute(velocity, 'gy', [(i, (i + k) % parts) for i in range(parts)])  19.4 us
    pallas_call x4, Pallas kernels, call(): pl.pallas_call(kernel, grid_spec=pltpu.PrefetchScalarGridSpec(num_scalar_...  17.3 us
    unnamed x10, local copies, waits for them, and re-layouts  5.09 us
    ppermute x1, starting transfers between devices, shards(): lax.ppermute(velocity, 'gy', [(i, (i + k) % parts) for i in range(parts)])  2.69 us
    ppermute x1, starting transfers between devices, shards(): far = lax.ppermute(velocity, 'gx', outward)  1.38 us
  transfers between devices with their start and end apart: 3, of which 1 were waited for; matrix products, arithmetic and copies ran while one was open for 0% of the time, Pallas kernels for 32%

profile of v1, /device:TPU:1, one launch (start us, length us, event | category | flops | bytes accessed | tf_op | source)
XLA Modules:
  0.0 46.0 jit_solution(16575905326900156260)
XLA Ops:
  0.0 0.1 collective-permute-start.2
  0.1 2.7 %collective-permute-start.1 = (f32[3,2,512,128]{3,2,1,0:T(8,128)}, f32[3,2,512,128]{3,2,1,0:T(8,128)}, u32[]{:S(2)}, u32[]{:S(2)}) collective-permute-start(f32[3,2,512,128]{3,2,1,0:T(8,128)} %velocity.7), channel_id=1, source_target_pairs={{0,1},{1,0},{2,3},{3,2},{4,5},{5,4},{6,7},{7,6},{8,9},{9,8},{10,11... | collective-permute-start | bytes 4718600 | tf_op jit(solution)/shard_map/ppermute | solution.py:166
  2.7 1.4 %collective-permute-start = (f32[3,2,512,128]{3,2,1,0:T(8,128)}, f32[3,2,512,128]{3,2,1,0:T(8,128)S(1)}, u32[]{:S(2)}, u32[]{:S(2)}) collective-permute-start(f32[3,2,512,128]{3,2,1,0:T(8,128)} %velocity.7), channel_id=1, source_target_pairs={{0,30},{2,4},{4,2},{6,8},{8,6},{10,12},{12,10},{14,16},{16,14},{18... | collective-permute-start | bytes 4718600 | tf_op jit(solution)/shard_map/ppermute | solution.py:169
  4.1 0.1 add_add_fusion
  4.2 0.0 copy-start
  4.2 1.4 %copy-done = f32[3,2,512,128]{3,2,1,0:T(8,128)S(1)} copy-done((f32[3,2,512,128]{3,2,1,0:T(8,128)S(1)}, f32[3,2,512,128]{3,2,1,0:T(8,128)}, u32[]{:S(2)}) %copy-start) | copy-done | bytes 1572888
  5.6 0.0 copy-start.4
  5.6 1.4 %copy-done.4 = f32[3,2,512,128]{3,2,1,0:T(8,128)S(1)} copy-done((f32[3,2,512,128]{3,2,1,0:T(8,128)S(1)}, f32[3,2,512,128]{3,2,1,0:T(8,128)}, u32[]{:S(2)}) %copy-start.4) | copy-done | bytes 1572888
  7.0 6.1 %local.1.base = f32[3,2,512,128]{3,2,1,0:T(8,128)S(1)} custom-call(s32[3]{0:T(128)S(1)} %get-tuple-element.5.where, bf16[2,2,2,1024,512]{4,3,2,1,0:T(8,128)(2,1)} %constant.38.clone.operators, f32[3,2,512,128]{3,2,1,0:T(8,128)S(1)} %copy-done, f32[3,2,512,128]{3,2,1,0:T(8,128)S(1)} %copy-done.4), custom_call_target="tpu_custom_call" | custom-call | flops 2415919104 | bytes 6291456 | tf_op jit(solution)/shard_map/local/pallas_call | solution.py:140
  13.2 0.0 copy-start.2
  13.2 1.1 %copy-done.2 = f32[3,2,512,128]{3,2,1,0:T(8,128)} copy-done((f32[3,2,512,128]{3,2,1,0:T(8,128)}, f32[3,2,512,128]{3,2,1,0:T(8,128)S(1)}, u32[]{:S(2)}) %copy-start.2) | copy-done | bytes 1572888
  14.3 0.0 copy-start.1
  14.3 0.0 collective-permute-done.2.near
  14.3 3.0 %near.1.base = f32[3,2,512,128]{3,2,1,0:T(8,128)S(1)} custom-call(s32[3]{0:T(128)S(1)} %get-tuple-element.5.where, f32[3,2,512,128]{3,2,1,0:T(8,128)S(1)} %copy-done, f32[3,2,512,128]{3,2,1,0:T(8,128)S(1)} %collective-permute-done.2.near, f32[3,2,512,128]{3,2,1,0:T(8,128)} %copy-done.2), custom_call_target="tpu_custom_call" | custom-call | flops 7864320 | bytes 6291456 | tf_op jit(solution)/shard_map/near/pallas_call | solution.py:140
  17.3 0.0 copy-start.3
  17.3 1.1 %copy-done.3 = f32[3,2,512,128]{3,2,1,0:T(8,128)} copy-done((f32[3,2,512,128]{3,2,1,0:T(8,128)}, f32[3,2,512,128]{3,2,1,0:T(8,128)S(1)}, u32[]{:S(2)}) %copy-start.3) | copy-done | bytes 1572888
  18.4 19.4 %collective-permute-done.1.others = f32[3,2,512,128]{3,2,1,0:T(8,128)} collective-permute-done((f32[3,2,512,128]{3,2,1,0:T(8,128)}, f32[3,2,512,128]{3,2,1,0:T(8,128)}, u32[]{:S(2)}, u32[]{:S(2)}) %collective-permute-start.1) | collective-permute-done | bytes 1572896 | tf_op jit(solution)/shard_map/ppermute | solution.py:166
  37.8 0.0 copy-done.1
  37.8 5.7 %remote.1.base = f32[3,2,512,128]{3,2,1,0:T(8,128)S(1)} custom-call(s32[3]{0:T(128)S(1)} %get-tuple-element.6.where, bf16[2,2,2,1024,512]{4,3,2,1,0:T(8,128)(2,1)} %constant.38.clone.operators, f32[3,2,512,128]{3,2,1,0:T(8,128)S(1)} %copy-done.1, f32[3,2,512,128]{3,2,1,0:T(8,128)} %collective-permute-done.1.others, f32[3,2,512,128]{3,2,1,0:T(8,128)} %copy-done.3), custom_call_target="tpu_custom_call" | custom-call | flops 2415919104 | bytes 6291456 | tf_op jit(solution)/shard_map/remote/pallas_call | solution.py:140
  43.5 0.0 collective-permute-done.far
  43.6 2.5 %far.1 = f32[3,2,512,128]{3,2,1,0:T(8,128)} custom-call(s32[3]{0:T(128)S(1)} %get-tuple-element.5.where, f32[3,2,512,128]{3,2,1,0:T(8,128)S(1)} %copy-done.1, f32[3,2,512,128]{3,2,1,0:T(8,128)S(1)} %collective-permute-done.far, f32[3,2,512,128]{3,2,1,0:T(8,128)S(1)} %remote.1.base), custom_call_target="tpu_custom_call" | custom-call | flops 7864320 | bytes 6291456 | tf_op jit(solution)/shard_map/far/pallas_call | solution.py:140
Async XLA Ops:
  0.0 14.3 %collective-permute-start.2 = (f32[3,2,512,128]{3,2,1,0:T(8,128)}, f32[3,2,512,128]{3,2,1,0:T(8,128)S(1)}, u32[]{:S(2)}, u32[]{:S(2)}) collective-permute-start(f32[3,2,512,128]{3,2,1,0:T(8,128)} %velocity.7), channel_id=1, source_target_pairs={{0,2},{2,0},{4,6},{6,4},{8,10},{10,8},{12,14},{14,12},{16,18},{18,... | collective-permute-start | bytes 4718600 | tf_op jit(solution)/shard_map/ppermute | solution.py:170
  0.1 37.8 %collective-permute-start.1 = (f32[3,2,512,128]{3,2,1,0:T(8,128)}, f32[3,2,512,128]{3,2,1,0:T(8,128)}, u32[]{:S(2)}, u32[]{:S(2)}) collective-permute-start(f32[3,2,512,128]{3,2,1,0:T(8,128)} %velocity.7), channel_id=1, source_target_pairs={{0,1},{1,0},{2,3},{3,2},{4,5},{5,4},{6,7},{7,6},{8,9},{9,8},{10,11... | collective-permute-start | bytes 4718600 | tf_op jit(solution)/shard_map/ppermute | solution.py:166
  2.7 40.8 %collective-permute-start = (f32[3,2,512,128]{3,2,1,0:T(8,128)}, f32[3,2,512,128]{3,2,1,0:T(8,128)S(1)}, u32[]{:S(2)}, u32[]{:S(2)}) collective-permute-start(f32[3,2,512,128]{3,2,1,0:T(8,128)} %velocity.7), channel_id=1, source_target_pairs={{0,30},{2,4},{4,2},{6,8},{8,6},{10,12},{12,10},{14,16},{16,14},{18... | collective-permute-start | bytes 4718600 | tf_op jit(solution)/shard_map/ppermute | solution.py:169
  4.2 1.4 %copy-start = (f32[3,2,512,128]{3,2,1,0:T(8,128)S(1)}, f32[3,2,512,128]{3,2,1,0:T(8,128)}, u32[]{:S(2)}) copy-start(f32[3,2,512,128]{3,2,1,0:T(8,128)} %velocity.7) | copy-start | bytes 4718596
  5.6 1.4 %copy-start.4 = (f32[3,2,512,128]{3,2,1,0:T(8,128)S(1)}, f32[3,2,512,128]{3,2,1,0:T(8,128)}, u32[]{:S(2)}) copy-start(f32[3,2,512,128]{3,2,1,0:T(8,128)} %previous.1) | copy-start | bytes 4718596
  13.2 1.1 %copy-start.2 = (f32[3,2,512,128]{3,2,1,0:T(8,128)}, f32[3,2,512,128]{3,2,1,0:T(8,128)S(1)}, u32[]{:S(2)}) copy-start(f32[3,2,512,128]{3,2,1,0:T(8,128)S(1)} %local.1.base) | copy-start | bytes 4718596
  14.3 23.5 %copy-start.1 = (f32[3,2,512,128]{3,2,1,0:T(8,128)S(1)}, f32[3,2,512,128]{3,2,1,0:T(8,128)}, u32[]{:S(2)}) copy-start(f32[3,2,512,128]{3,2,1,0:T(8,128)} %velocity.7) | copy-start | bytes 4718596
  17.3 1.1 %copy-start.3 = (f32[3,2,512,128]{3,2,1,0:T(8,128)}, f32[3,2,512,128]{3,2,1,0:T(8,128)S(1)}, u32[]{:S(2)}) copy-start(f32[3,2,512,128]{3,2,1,0:T(8,128)S(1)} %near.1.base) | copy-start | bytes 4718596

commit v2 on v1

v2 whole, which is shorter than its diff:
```python
import functools

import jax
import jax.numpy as jnp
import numpy as np
from jax import lax
from jax.experimental import pallas as pl
from jax.experimental.pallas import tpu as pltpu
from jax.sharding import PartitionSpec as P

NY = 1024


LENGTH_SPACING = 8.0 * 3.141592653589793 / 4096.0
SPAN_SPACING = 3.0 * 3.141592653589793 / 3072.0
VISCOSITY = 1.0 / 2000.0
TIME_STEP = 0.003
GAMMA_NOW = 5.0 / 12.0
ZETA_PAST = -17.0 / 60.0

SCALE = TIME_STEP * GAMMA_NOW
X_FIRST = SCALE / (12.0 * LENGTH_SPACING)
X_SECOND = SCALE * VISCOSITY / (12.0 * LENGTH_SPACING * LENGTH_SPACING)
Z_FIRST = SCALE / (12.0 * SPAN_SPACING)
Z_SECOND = SCALE * VISCOSITY / (12.0 * SPAN_SPACING * SPAN_SPACING)
PAST = TIME_STEP * ZETA_PAST

VMEM_LIMIT = 24 * 1024 * 1024


def chebyshev_matrices(total):
    one = np.float32(1.0)
    ids = np.arange(total, dtype=np.int32)
    angle = ids.astype(np.float32) * (np.float32(np.pi) / np.float32(total - 1))
    on_diagonal = ids[:, None] == ids[None, :]
    signs = one - np.float32(2.0) * ((ids[:, None] + ids[None, :]) % 2).astype(np.float32)
    half = np.where((ids == 0) | (ids == total - 1), 0.5, 1.0).astype(np.float32)
    weight_ratio = signs * half[None, :] / half[:, None]
    spacing = (
        np.float32(-2.0)
        * np.sin(np.float32(0.5) * (angle[:, None] + angle[None, :]))
        * np.sin(np.float32(0.5) * (angle[:, None] - angle[None, :]))
    )
    spacing = np.where(on_diagonal, one, spacing)
    first = np.where(on_diagonal, np.float32(0.0), weight_ratio / spacing)
    first_diag = -np.sum(first, axis=1, dtype=np.float32)
    second = np.where(
        on_diagonal,
        np.float32(0.0),
        np.float32(2.0) * first * (first_diag[:, None] - one / spacing),
    )
    second_diag = -np.sum(second, axis=1, dtype=np.float32)
    first[ids, ids] = first_diag
    second[ids, ids] = second_diag
    return first, second


def operator_blocks(total, parts):
    first, second = chebyshev_matrices(total)
    rows = total // parts
    stacked = np.stack(
        [first.astype(np.float64) * SCALE, second.astype(np.float64) * (SCALE * VISCOSITY)]
    ).astype(np.float32)
    blocks = stacked.reshape(2, parts, rows, parts, rows).transpose(1, 3, 0, 2, 4)
    blocks = blocks.reshape(parts, parts, 2 * rows, rows)
    high = blocks.astype(jnp.bfloat16)
    low = (blocks - high.astype(np.float32)).astype(jnp.bfloat16)
    return np.stack([high, low], axis=2)


def wall(operators, fields, v):
    rows = v.shape[1]
    side = jnp.concatenate([fields[0], fields[1]], axis=1)
    high = side.astype(jnp.bfloat16)
    low = (side - high.astype(jnp.float32)).astype(jnp.bfloat16)
    dot = functools.partial(jnp.dot, preferred_element_type=jnp.float32)
    product = dot(operators[0], high) + (dot(operators[1], high) + dot(operators[0], low))
    first, second = product[:rows], product[rows:]
    added = second - jnp.concatenate([v[0], v[1]], axis=1) * first
    return added[:, : v.shape[2]], added[:, v.shape[2] :]


def along_x(parity):
    return jnp.where(parity == 0, X_FIRST, -X_FIRST).astype(jnp.float32)


def local_kernel(operators, velocity, previous, *outs):
    width = velocity.shape[3]
    roll = lambda f, k: pltpu.roll(f, k % width, 1)
    for q in range(3):
        added = wall(operators, velocity[q], velocity[1])
        for plane in range(2):
            f, other = velocity[q, plane], velocity[q, 1 - plane]
            u, w = velocity[0, plane], velocity[2, plane]
            step = X_FIRST if plane == 0 else -X_FIRST
            total = X_SECOND * (16.0 * other - 30.0 * f) - u * ((8.0 * step) * other)
            p1, m1, p2, m2 = roll(f, -1), roll(f, 1), roll(f, -2), roll(f, 2)
            total += Z_SECOND * (16.0 * (p1 + m1) - (p2 + m2) - 30.0 * f)
            total -= w * (Z_FIRST * (8.0 * (p1 - m1) - (p2 - m2)))
            outs[q][plane] = f + PAST * previous[q, plane] + (total + added[plane])


def near_kernel(where, velocity, near, *refs):
    bases, outs, (slab, came) = refs[:3], refs[3:6], refs[6:]
    parity = where[0]
    inner, outer = 1 - parity, parity
    along = along_x(parity)
    fetches = [pltpu.make_async_copy(near.at[q], slab.at[q], came.at[q]) for q in range(3)]
    for fetch in fetches:
        fetch.start()
    for q in range(3):
        fetches[q].wait()
        base, out = bases[q], outs[q]
        first, second = slab[q, parity], slab[q, 1 - parity]
        out[outer] = base[outer] - X_SECOND * first + (along * velocity[0, outer]) * first
        out[inner] = (
            base[inner]
            + X_SECOND * (16.0 * first - second)
            - (along * velocity[0, inner]) * (8.0 * first - second)
        )


def remote_kernel(operators, velocity, others, *refs):
    for q in range(3):
        base, out = refs[q], refs[3 + q]
        added = wall(operators, others[q], velocity[1])
        for plane in range(2):
            out[plane] = base[plane] + added[plane]


def far_kernel(where, velocity, far, *refs):
    bases, (out, total, sent) = refs[:3], refs[3:]
    parity = where[0]
    inner, outer = 1 - parity, parity
    along = along_x(parity)
    stores = []
    for q in range(3):
        first, second = far[q, 1 - parity], far[q, parity]
        total[q, inner] = (
            bases[q][inner] - X_SECOND * first - (along * velocity[0, inner]) * first
        )
        total[q, outer] = (
            bases[q][outer]
            + X_SECOND * (16.0 * first - second)
            + (along * velocity[0, outer]) * (8.0 * first - second)
        )
        stores.append(pltpu.make_async_copy(total.at[q], out.at[q], sent.at[q]))
        stores[-1].start()
    for store in stores:
        store.wait()


VMEM = pl.BlockSpec(memory_space=pltpu.VMEM)
SMEM = pl.BlockSpec(memory_space=pltpu.SMEM)
ANY = pl.BlockSpec(memory_space=pl.ANY)


def vmem(array):
    return pltpu.with_memory_space_constraint(array, pltpu.VMEM)


def call(kernel, ins, in_specs, out_shape, flops, name, **kwargs):
    leaves = jax.tree.leaves(out_shape)
    kwargs.setdefault("out_specs", jax.tree.map(lambda _: VMEM, out_shape))
    size = sum(int(np.prod(x.shape)) * x.dtype.itemsize for x in (*ins, *leaves))
    return pl.pallas_call(
        kernel,
        in_specs=in_specs,
        out_shape=out_shape,
        compiler_params=pltpu.CompilerParams(vmem_limit_bytes=VMEM_LIMIT),
        cost_estimate=pl.CostEstimate(flops=flops, bytes_accessed=size, transcendentals=0),
        name=name,
        **kwargs,
    )(*ins)


def shards(parts, velocity, previous):
    count = lax.axis_size("gx")
    shape = velocity.shape
    assert shape[0] == 3 and shape[1] == 2 and count % 2 == 0
    rows = shape[2]
    me = lax.axis_index("gy")
    parity = (lax.axis_index("gx") % 2).astype(jnp.int32).reshape(1)

    outward = [(i, (i - 1) % count if i % 2 == 0 else (i + 1) % count) for i in range(count)]
    inward = [(i, i ^ 1) for i in range(count)]
    far = lax.ppermute(velocity, "gx", outward)
    near = lax.ppermute(velocity, "gx", inward)
    others = [
        lax.ppermute(velocity, "gy", [(i, (i + k) % parts) for i in range(parts)])
        for k in range(1, parts)
    ]

    blocks = jnp.asarray(operator_blocks(rows * parts, parts))
    mine = lax.dynamic_index_in_dim(blocks, me, 0, keepdims=False)
    operators = [
        lax.dynamic_index_in_dim(mine, (me - k) % parts, 0, keepdims=False) for k in range(parts)
    ]

    one = jax.ShapeDtypeStruct(shape[1:], jnp.float32)
    whole = jax.ShapeDtypeStruct(shape, jnp.float32)
    flops = 3 * 2 * 2 * 2 * rows * rows * 6 * shape[3]
    light = 20 * 6 * rows * shape[3]
    totals = call(
        local_kernel,
        (operators[0], velocity, previous),
        [VMEM] * 3,
        (one,) * 3,
        flops,
        "local",
    )
    totals = call(
        near_kernel,
        (parity, velocity, pltpu.with_memory_space_constraint(near, pltpu.HBM), *totals),
        [SMEM, VMEM, ANY] + [VMEM] * 3,
        (one,) * 3,
        light,
        "near",
        scratch_shapes=[pltpu.VMEM(shape, jnp.float32), pltpu.SemaphoreType.DMA((3,))],
    )
    for k in range(1, parts):
        totals = call(
            remote_kernel,
            (vmem(operators[k]), vmem(velocity), vmem(others[k - 1]), *totals),
            [VMEM] * 6,
            (one,) * 3,
            flops,
            "remote",
        )
    return call(
        far_kernel,
        (parity, vmem(velocity), vmem(far), *totals),
        [SMEM, VMEM, VMEM] + [VMEM] * 3,
        whole,
        light,
        "far",
        out_specs=ANY,
        scratch_shapes=[
            pltpu.VMEM(shape, jnp.float32),
            pltpu.SemaphoreType.DMA((3,)),
        ],
    )


def solution(mesh):
    spec = P(None, "gx", "gy", None)
    body = functools.partial(shards, mesh.shape["gy"])
    return jax.shard_map(body, mesh=mesh, in_specs=(spec, spec), out_specs=spec, check_vma=False)
```

time: 46.8 us -> 42.4 us (0.906)
  Pallas kernels: 17.3 us -> 9.31 us
  waiting for transfers between devices: 19.4 us -> 25.1 us
  local copies, waits for them, and re-layouts: 5.09 us -> 3.13 us
    pallas_call x4, Pallas kernels: 17.3 us -> 9.31 us  [call(): pl.pallas_call(kernel, in_specs=in_specs, out_shape=out_shape, compiler_p...]
    ppermute x1, waiting for transfers between devices: 19.4 us -> 25.1 us  [shards(): lax.ppermute(velocity, 'gy', [(i, (i + k) % parts) for i in range(parts)])]
    unnamed x10 -> x4, local copies, waits for them, and re-layouts: 5.09 us -> 0.48 us
    squeeze x0 -> x1, local copies, waits for them, and re-layouts: none -> 2.65 us  [shards(): lax.dynamic_index_in_dim(mine, (me - k) % parts, 0, keepdims=False)]
  transfers between devices with their start and end apart: 3 -> 3, of which waited for: 1 -> 1; matrix products, arithmetic and copies ran while one was open for 0% -> 6% of each run, Pallas kernels for 32% -> 19%
where the time goes in v2:
time: 42.4 us; the launch traced here: 41.8 us
  waiting for transfers between devices  25.1 us (59%)
  Pallas kernels  9.31 us (22%)
  starting transfers between devices  4.12 us (10%)
  local copies, waits for them, and re-layouts  3.13 us (7%)
    ppermute x1, waiting for transfers between devices, shards(): lax.ppermute(velocity, 'gy', [(i, (i + k) % parts) for i in range(parts)])  25.1 us
    pallas_call x4, Pallas kernels, call(): pl.pallas_call(kernel, in_specs=in_specs, out_shape=out_shape, compiler_p...  9.31 us
    ppermute x1, starting transfers between devices, shards(): lax.ppermute(velocity, 'gy', [(i, (i + k) % parts) for i in range(parts)])  2.69 us
    squeeze x1, local copies, waits for them, and re-layouts, shards(): lax.dynamic_index_in_dim(mine, (me - k) % parts, 0, keepdims=False)  2.65 us
    ppermute x1, starting transfers between devices, shards(): far = lax.ppermute(velocity, 'gx', outward)  1.38 us
  transfers between devices with their start and end apart: 3, of which 1 were waited for; matrix products, arithmetic and copies ran while one was open for 6% of the time, Pallas kernels for 19%

profile of v2, /device:TPU:1, one launch (start us, length us, event | category | flops | bytes accessed | tf_op | source)
XLA Modules:
  0.0 41.8 jit_solution(17797518111249288408)
XLA Ops:
  0.0 0.1 collective-permute-start.2
  0.1 2.7 %collective-permute-start.1 = (f32[3,2,512,128]{3,2,1,0:T(8,128)}, f32[3,2,512,128]{3,2,1,0:T(8,128)S(1)}, u32[]{:S(2)}, u32[]{:S(2)}) collective-permute-start(f32[3,2,512,128]{3,2,1,0:T(8,128)} %velocity.7), channel_id=1, source_target_pairs={{0,1},{1,0},{2,3},{3,2},{4,5},{5,4},{6,7},{7,6},{8,9},{9,8},{10,11... | collective-permute-start | bytes 4718600 | tf_op jit(solution)/shard_map/ppermute | solution.py:190
  2.7 1.4 %collective-permute-start = (f32[3,2,512,128]{3,2,1,0:T(8,128)}, f32[3,2,512,128]{3,2,1,0:T(8,128)S(1)}, u32[]{:S(2)}, u32[]{:S(2)}) collective-permute-start(f32[3,2,512,128]{3,2,1,0:T(8,128)} %velocity.7), channel_id=1, source_target_pairs={{0,30},{2,4},{4,2},{6,8},{8,6},{10,12},{12,10},{14,16},{16,14},{18... | collective-permute-start | bytes 4718600 | tf_op jit(solution)/shard_map/ppermute | solution.py:187
  4.1 0.0 copy-start
  4.1 0.0 copy-start.1
  4.1 2.7 %dynamic-slice_bitcast_fusion = (bf16[2,1024,512]{2,1,0:T(8,128)(2,1)S(1)}, bf16[2,1024,512]{2,1,0:T(8,128)(2,1)S(1)}) fusion(bf16[2,2,2,1024,512]{4,3,2,1,0:T(8,128)(2,1)} %constant.92.clone, s32[]{:T(128)S(6)} %select_n.34, s32[]{:T(128)S(6)} %select_n.40, s32[]{:T(128)S(6)} %select_n.37), kind=kLoop, calls=%fused_computation | loop fusion | bytes 8388620 | tf_op jit(solution)/shard_map/jit(dynamic_index_in_dim)/squeeze | solution.py:197
  6.8 0.0 copy-done
  6.8 0.5 %copy-done.1 = f32[3,2,512,128]{3,2,1,0:T(8,128)S(1)} copy-done((f32[3,2,512,128]{3,2,1,0:T(8,128)S(1)}, f32[3,2,512,128]{3,2,1,0:T(8,128)}, u32[]{:S(2)}) %copy-start.1) | copy-done | bytes 1572888
  7.3 3.7 %local.1 = (f32[2,512,128]{2,1,0:T(8,128)S(1)}, f32[2,512,128]{2,1,0:T(8,128)S(1)}, f32[2,512,128]{2,1,0:T(8,128)S(1)}) custom-call(bf16[2,1024,512]{2,1,0:T(8,128)(2,1)S(1)} %get-tuple-element.23.operators, f32[3,2,512,128]{3,2,1,0:T(8,128)S(1)} %copy-done, f32[3,2,512,128]{3,2,1,0:T(8,128)S(1)} %copy-done.1), custom_call_target="tpu_custom_call" | custom-call | flops 4831838208 | bytes 6815744 | tf_op jit(solution)/shard_map/local/pallas_call | solution.py:166
  11.0 0.0 collective-permute-done.2.near
  11.0 1.6 %near.1 = (f32[2,512,128]{2,1,0:T(8,128)S(1)}, f32[2,512,128]{2,1,0:T(8,128)S(1)}, f32[2,512,128]{2,1,0:T(8,128)S(1)}) custom-call(s32[1]{0:T(128)} %bitcast.where, f32[3,2,512,128]{3,2,1,0:T(8,128)S(1)} %copy-done, f32[3,2,512,128]{3,2,1,0:T(8,128)} %collective-permute-done.2.near, f32[2,512,128]{2,1,0:T(8,128)S(1)} %get-tuple-element.14.refs_0_, ...), custom_call_target="tpu_custom_call" | custom-call | flops 7864320 | bytes 6291460 | tf_op jit(solution)/shard_map/near/pallas_call | solution.py:166
  12.6 25.1 %collective-permute-done.1.others = f32[3,2,512,128]{3,2,1,0:T(8,128)S(1)} collective-permute-done((f32[3,2,512,128]{3,2,1,0:T(8,128)}, f32[3,2,512,128]{3,2,1,0:T(8,128)S(1)}, u32[]{:S(2)}, u32[]{:S(2)}) %collective-permute-start.1) | collective-permute-done | bytes 1572896 | tf_op jit(solution)/shard_map/ppermute | solution.py:190
  37.7 2.7 %remote.1 = (f32[2,512,128]{2,1,0:T(8,128)S(1)}, f32[2,512,128]{2,1,0:T(8,128)S(1)}, f32[2,512,128]{2,1,0:T(8,128)S(1)}) custom-call(bf16[2,1024,512]{2,1,0:T(8,128)(2,1)S(1)} %get-tuple-element.24.operators, f32[3,2,512,128]{3,2,1,0:T(8,128)S(1)} %copy-done, f32[3,2,512,128]{3,2,1,0:T(8,128)S(1)} %collective-permute-done.1.others, ...), custom_call_target="tpu_custom_call" | custom-call | flops 4831838208 | bytes 8388608 | tf_op jit(solution)/shard_map/remote/pallas_call | solution.py:166
  40.4 0.0 collective-permute-done.far
  40.4 1.4 %far.1 = f32[3,2,512,128]{3,2,1,0:T(8,128)} custom-call(s32[1]{0:T(128)} %bitcast.where, f32[3,2,512,128]{3,2,1,0:T(8,128)S(1)} %copy-done, f32[3,2,512,128]{3,2,1,0:T(8,128)S(1)} %collective-permute-done.far, f32[2,512,128]{2,1,0:T(8,128)S(1)} %get-tuple-element.20.refs_0_, f32[2,512,128]{2,1,0:T(8,128)S(1)} %get-tuple-element.21.refs_1_, ...), custom_call_target="tpu_custom_call" | custom-call | flops 7864320 | bytes 6291460 | tf_op jit(solution)/shard_map/far/pallas_call | solution.py:166
Async XLA Ops:
  0.0 11.0 %collective-permute-start.2 = (f32[3,2,512,128]{3,2,1,0:T(8,128)}, f32[3,2,512,128]{3,2,1,0:T(8,128)}, u32[]{:S(2)}, u32[]{:S(2)}) collective-permute-start(f32[3,2,512,128]{3,2,1,0:T(8,128)} %velocity.7), channel_id=1, source_target_pairs={{0,2},{2,0},{4,6},{6,4},{8,10},{10,8},{12,14},{14,12},{16,18},{18,... | collective-permute-start | bytes 4718600 | tf_op jit(solution)/shard_map/ppermute | solution.py:188
  0.1 37.7 %collective-permute-start.1 = (f32[3,2,512,128]{3,2,1,0:T(8,128)}, f32[3,2,512,128]{3,2,1,0:T(8,128)S(1)}, u32[]{:S(2)}, u32[]{:S(2)}) collective-permute-start(f32[3,2,512,128]{3,2,1,0:T(8,128)} %velocity.7), channel_id=1, source_target_pairs={{0,1},{1,0},{2,3},{3,2},{4,5},{5,4},{6,7},{7,6},{8,9},{9,8},{10,11... | collective-permute-start | bytes 4718600 | tf_op jit(solution)/shard_map/ppermute | solution.py:190
  2.7 37.7 %collective-permute-start = (f32[3,2,512,128]{3,2,1,0:T(8,128)}, f32[3,2,512,128]{3,2,1,0:T(8,128)S(1)}, u32[]{:S(2)}, u32[]{:S(2)}) collective-permute-start(f32[3,2,512,128]{3,2,1,0:T(8,128)} %velocity.7), channel_id=1, source_target_pairs={{0,30},{2,4},{4,2},{6,8},{8,6},{10,12},{12,10},{14,16},{16,14},{18... | collective-permute-start | bytes 4718600 | tf_op jit(solution)/shard_map/ppermute | solution.py:187
  4.1 2.7 %copy-start = (f32[3,2,512,128]{3,2,1,0:T(8,128)S(1)}, f32[3,2,512,128]{3,2,1,0:T(8,128)}, u32[]{:S(2)}) copy-start(f32[3,2,512,128]{3,2,1,0:T(8,128)} %velocity.7) | copy-start | bytes 4718596
  4.1 3.1 %copy-start.1 = (f32[3,2,512,128]{3,2,1,0:T(8,128)S(1)}, f32[3,2,512,128]{3,2,1,0:T(8,128)}, u32[]{:S(2)}) copy-start(f32[3,2,512,128]{3,2,1,0:T(8,128)} %previous.1) | copy-start | bytes 4718596

commit v3 on v2

--- a/solution.py
+++ b/solution.py
@@ -26,6 +26,7 @@
 PAST = TIME_STEP * ZETA_PAST
 
 VMEM_LIMIT = 24 * 1024 * 1024
+PIECES = ((0, 1), (2,))
 
 
 def chebyshev_matrices(total):
@@ -84,39 +85,67 @@
     return jnp.where(parity == 0, X_FIRST, -X_FIRST).astype(jnp.float32)
 
 
-def local_kernel(operators, velocity, previous, *outs):
-    width = velocity.shape[3]
+def local_kernel(blocks, velocity, previous, *refs):
+    outs, parted = refs[:3], refs[3 : 3 + len(PIECES)]
+    own, past, operators, came, sent = refs[3 + len(PIECES) :]
+    me = lax.axis_index("gy")
+    fetches = [
+        pltpu.make_async_copy(velocity, own, came.at[0]),
+        pltpu.make_async_copy(blocks.at[me, me], operators, came.at[1]),
+        pltpu.make_async_copy(previous, past, came.at[2]),
+    ]
+    for fetch in fetches:
+        fetch.start()
+    fetches[0].wait()
+    stores = [
+        pltpu.make_async_copy(own.at[c[0] : c[-1] + 1], part, sent.at[i])
+        for i, (c, part) in enumerate(zip(PIECES, parted))
+    ]
+    for store in stores:
+        store.start()
+    for fetch in fetches[1:]:
+        fetch.wait()
+    width = own.shape[3]
     roll = lambda f, k: pltpu.roll(f, k % width, 1)
     for q in range(3):
-        added = wall(operators, velocity[q], velocity[1])
+        added = wall(operators, own[q], own[1])
         for plane in range(2):
-            f, other = velocity[q, plane], velocity[q, 1 - plane]
-            u, w = velocity[0, plane], velocity[2, plane]
+            f, other = own[q, plane], own[q, 1 - plane]
+            u, w = own[0, plane], own[2, plane]
             step = X_FIRST if plane == 0 else -X_FIRST
             total = X_SECOND * (16.0 * other - 30.0 * f) - u * ((8.0 * step) * other)
             p1, m1, p2, m2 = roll(f, -1), roll(f, 1), roll(f, -2), roll(f, 2)
             total += Z_SECOND * (16.0 * (p1 + m1) - (p2 + m2) - 30.0 * f)
             total -= w * (Z_FIRST * (8.0 * (p1 - m1) - (p2 - m2)))
-            outs[q][plane] = f + PAST * previous[q, plane] + (total + added[plane])
-
-
-def near_kernel(where, velocity, near, *refs):
-    bases, outs, (slab, came) = refs[:3], refs[3:6], refs[6:]
-    parity = where[0]
+            outs[q][plane] = f + PAST * past[q, plane] + (total + added[plane])
+    for store in stores:
+        store.wait()
+
+
+def near_kernel(velocity, *refs):
+    near, refs = refs[: len(PIECES)], refs[len(PIECES) :]
+    bases, outs, (u, slab, came) = refs[:3], refs[3:6], refs[6:]
+    parity = lax.axis_index("gx") % 2
     inner, outer = 1 - parity, parity
     along = along_x(parity)
-    fetches = [pltpu.make_async_copy(near.at[q], slab.at[q], came.at[q]) for q in range(3)]
+    fetches = [
+        pltpu.make_async_copy(part.at[i], slab.at[q], came.at[q])
+        for c, part in zip(PIECES, near)
+        for i, q in enumerate(c)
+    ]
+    fetches.append(pltpu.make_async_copy(velocity.at[0], u, came.at[3]))
     for fetch in fetches:
         fetch.start()
+    fetches[3].wait()
     for q in range(3):
         fetches[q].wait()
         base, out = bases[q], outs[q]
         first, second = slab[q, parity], slab[q, 1 - parity]
-        out[outer] = base[outer] - X_SECOND * first + (along * velocity[0, outer]) * first
+        out[outer] = base[outer] - X_SECOND * first + (along * u[outer]) * first
         out[inner] = (
             base[inner]
             + X_SECOND * (16.0 * first - second)
-            - (along * velocity[0, inner]) * (8.0 * first - second)
+            - (along * u[inner]) * (8.0 * first - second)
         )
 
 
@@ -128,9 +157,9 @@
             out[plane] = base[plane] + added[plane]
 
 
-def far_kernel(where, velocity, far, *refs):
+def far_kernel(velocity, far, *refs):
     bases, (out, total, sent) = refs[:3], refs[3:]
-    parity = where[0]
+    parity = lax.axis_index("gx") % 2
     inner, outer = 1 - parity, parity
     along = along_x(parity)
     stores = []
@@ -151,7 +180,6 @@
 
 
 VMEM = pl.BlockSpec(memory_space=pltpu.VMEM)
-SMEM = pl.BlockSpec(memory_space=pltpu.SMEM)
 ANY = pl.BlockSpec(memory_space=pl.ANY)
 
 
@@ -159,16 +187,18 @@
     return pltpu.with_memory_space_constraint(array, pltpu.VMEM)
 
 
-def call(kernel, ins, in_specs, out_shape, flops, name, **kwargs):
-    leaves = jax.tree.leaves(out_shape)
+def hbm(array):
+    return pltpu.with_memory_space_constraint(array, pltpu.HBM)
+
+
+def call(kernel, ins, in_specs, out_shape, name, **kwargs):
     kwargs.setdefault("out_specs", jax.tree.map(lambda _: VMEM, out_shape))
-    size = sum(int(np.prod(x.shape)) * x.dtype.itemsize for x in (*ins, *leaves))
     return pl.pallas_call(
         kernel,
         in_specs=in_specs,
         out_shape=out_shape,
         compiler_params=pltpu.CompilerParams(vmem_limit_bytes=VMEM_LIMIT),
-        cost_estimate=pl.CostEstimate(flops=flops, bytes_accessed=size, transcendentals=0),
+        cost_estimate=pl.CostEstimate(flops=0, bytes_accessed=0, transcendentals=0),
         name=name,
         **kwargs,
     )(*ins)
@@ -180,12 +210,10 @@
     assert shape[0] == 3 and shape[1] == 2 and count % 2 == 0
     rows = shape[2]
     me = lax.axis_index("gy")
-    parity = (lax.axis_index("gx") % 2).astype(jnp.int32).reshape(1)
 
     outward = [(i, (i - 1) % count if i % 2 == 0 else (i + 1) % count) for i in range(count)]
     inward = [(i, i ^ 1) for i in range(count)]
     far = lax.ppermute(velocity, "gx", outward)
-    near = lax.ppermute(velocity, "gx", inward)
     others = [
         lax.ppermute(velocity, "gy", [(i, (i + k) % parts) for i in range(parts)])
         for k in range(1, parts)
@@ -194,45 +222,54 @@
     blocks = jnp.asarray(operator_blocks(rows * parts, parts))
     mine = lax.dynamic_index_in_dim(blocks, me, 0, keepdims=False)
     operators = [
-        lax.dynamic_index_in_dim(mine, (me - k) % parts, 0, keepdims=False) for k in range(parts)
+        lax.dynamic_index_in_dim(mine, (me - k) % parts, 0, keepdims=False)
+        for k in range(1, parts)
     ]
 
     one = jax.ShapeDtypeStruct(shape[1:], jnp.float32)
     whole = jax.ShapeDtypeStruct(shape, jnp.float32)
-    flops = 3 * 2 * 2 * 2 * rows * rows * 6 * shape[3]
-    light = 20 * 6 * rows * shape[3]
     totals = call(
         local_kernel,
-        (operators[0], velocity, previous),
-        [VMEM] * 3,
-        (one,) * 3,
-        flops,
+        (hbm(blocks), hbm(velocity), hbm(previous)),
+        [ANY] * 3,
+        (one,) * 3
+        + tuple(jax.ShapeDtypeStruct((len(c),) + shape[1:], jnp.float32) for c in PIECES),
         "local",
-    )
+        out_specs=(VMEM,) * 3 + (ANY,) * len(PIECES),
+        scratch_shapes=[
+            pltpu.VMEM(shape, jnp.float32),
+            pltpu.VMEM(shape, jnp.float32),
+            pltpu.VMEM(blocks.shape[2:], jnp.bfloat16),
+            pltpu.SemaphoreType.DMA((3,)),
+            pltpu.SemaphoreType.DMA((len(PIECES),)),
+        ],
+    )
+    near = [lax.ppermute(part, "gx", inward) for part in totals[3:]]
     totals = call(
         near_kernel,
-        (parity, velocity, pltpu.with_memory_space_constraint(near, pltpu.HBM), *totals),
-        [SMEM, VMEM, ANY] + [VMEM] * 3,
+        (hbm(velocity), *map(hbm, near), *totals[:3]),
+        [ANY] * (1 + len(PIECES)) + [VMEM] * 3,
         (one,) * 3,
-        light,
         "near",
-        scratch_shapes=[pltpu.VMEM(shape, jnp.float32), pltpu.SemaphoreType.DMA((3,))],
+        scratch_shapes=[
+            pltpu.VMEM(shape[1:], jnp.float32),
+            pltpu.VMEM(shape, jnp.float32),
+            pltpu.SemaphoreType.DMA((4,)),
+        ],
     )
     for k in range(1, parts):
         totals = call(
             remote_kernel,
-            (vmem(operators[k]), vmem(velocity), vmem(others[k - 1]), *totals),
+            (vmem(operators[k - 1]), vmem(velocity), vmem(others[k - 1]), *totals),
             [VMEM] * 6,
             (one,) * 3,
-            flops,
             "remote",
         )
     return call(
         far_kernel,
-        (parity, vmem(velocity), vmem(far), *totals),
-        [SMEM, VMEM, VMEM] + [VMEM] * 3,
+        (vmem(velocity), vmem(far), *totals),
+        [VMEM] * 5,
         whole,
-        light,
         "far",
         out_specs=ANY,
         scratch_shapes=[

time: 42.4 us -> 41.6 us (0.981)
  the two profiles are of different devices: /device:TPU:1 before, /device:TPU:0 now
where the time goes in v3:
time: 41.6 us; the launch traced here: 41.5 us
  waiting for transfers between devices  18.1 us (44%)
  Pallas kernels  11.9 us (29%)
  starting transfers between devices  7.17 us (17%)
  local copies, waits for them, and re-layouts  4.27 us (10%)
    ppermute x1, waiting for transfers between devices, shards(): lax.ppermute(velocity, 'gy', [(i, (i + k) % parts) for i in range(parts)])  16.7 us
    pallas_call x4, Pallas kernels, call(): pl.pallas_call(kernel, in_specs=in_specs, out_shape=out_shape, compiler_p...  11.9 us
    ppermute x1, starting transfers between devices, shards(): far = lax.ppermute(velocity, 'gx', outward)  3.69 us
    ppermute x1, starting transfers between devices, shards(): lax.ppermute(velocity, 'gy', [(i, (i + k) % parts) for i in range(parts)])  2.97 us
    unnamed x14, local copies, waits for them, and re-layouts  2.43 us
    squeeze x1, local copies, waits for them, and re-layouts, shards(): lax.dynamic_index_in_dim(mine, (me - k) % parts, 0, keepdims=False)  1.84 us
    ppermute x2, waiting for transfers between devices, shards(): near = [lax.ppermute(part, 'gx', inward) for part in totals[3:]]  1.39 us
  transfers between devices with their start and end apart: 4, of which 2 were waited for; matrix products, arithmetic and copies ran while one was open for 4% of the time, Pallas kernels for 26%

profile of v3, /device:TPU:0, one launch (start us, length us, event | category | flops | bytes accessed | tf_op | source)
XLA Modules:
  0.0 41.5 jit_solution(4175866401028160138)
XLA Ops:
  0.0 3.0 %collective-permute-start.1 = (f32[3,2,512,128]{3,2,1,0:T(8,128)}, f32[3,2,512,128]{3,2,1,0:T(8,128)S(1)}, u32[]{:S(2)}, u32[]{:S(2)}) collective-permute-start(f32[3,2,512,128]{3,2,1,0:T(8,128)} %velocity.7), channel_id=1, source_target_pairs={{0,1},{1,0},{2,3},{3,2},{4,5},{5,4},{6,7},{7,6},{8,9},{9,8},{10,11... | collective-permute-start | bytes 4718600 | tf_op jit(solution)/shard_map/ppermute | solution.py:218
  3.0 3.7 %collective-permute-start = (f32[3,2,512,128]{3,2,1,0:T(8,128)}, f32[3,2,512,128]{3,2,1,0:T(8,128)S(1)}, u32[]{:S(2)}, u32[]{:S(2)}) collective-permute-start(f32[3,2,512,128]{3,2,1,0:T(8,128)} %velocity.7), channel_id=1, source_target_pairs={{0,30},{2,4},{4,2},{6,8},{8,6},{10,12},{12,10},{14,16},{16,14},{18... | collective-permute-start | bytes 4718600 | tf_op jit(solution)/shard_map/ppermute | solution.py:216
  6.7 6.0 %local.1 = (f32[2,512,128]{2,1,0:T(8,128)S(1)}, f32[2,512,128]{2,1,0:T(8,128)S(1)}, f32[2,512,128]{2,1,0:T(8,128)S(1)}, f32[2,2,512,128]{3,2,1,0:T(8,128)}, f32[1,2,512,128]{3,2,1,0:T(8,128)}) custom-call(bf16[2,2,2,1024,512]{4,3,2,1,0:T(8,128)(2,1)} %constant.54.clone.blocks, f32[3,2,512,128]{3,2,1,0:T(8,128)} %velocity.7, f32[3,2,512,128]{3,2,1,0:T(8,128)} %previous.1), custom_call_target="tpu_custom_call" | custom-call | tf_op jit(solution)/shard_map/local/pallas_call | solution.py:196
  12.6 0.0 copy-start.1
  12.6 0.8 %copy-done.1 = f32[2,512,128]{2,1,0:T(8,128)} copy-done((f32[2,512,128]{2,1,0:T(8,128)}, f32[2,512,128]{2,1,0:T(8,128)S(1)}, u32[]{:S(2)}) %copy-start.1) | copy-done | bytes 524312
  13.4 0.0 copy-start.3
  13.4 0.8 %copy-done.3 = f32[2,512,128]{2,1,0:T(8,128)} copy-done((f32[2,512,128]{2,1,0:T(8,128)}, f32[2,512,128]{2,1,0:T(8,128)S(1)}, u32[]{:S(2)}) %copy-start.3) | copy-done | bytes 524312
  14.2 0.0 copy-start.5
  14.2 0.8 %copy-done.5 = f32[2,512,128]{2,1,0:T(8,128)} copy-done((f32[2,512,128]{2,1,0:T(8,128)}, f32[2,512,128]{2,1,0:T(8,128)S(1)}, u32[]{:S(2)}) %copy-start.5) | copy-done | bytes 524312
  15.0 0.0 collective-permute-start.2
  15.0 0.5 %collective-permute-start.3 = (f32[1,2,512,128]{3,2,1,0:T(8,128)}, f32[1,2,512,128]{3,2,1,0:T(8,128)}, u32[]{:S(2)}, u32[]{:S(2)}) collective-permute-start(f32[1,2,512,128]{3,2,1,0:T(8,128)} %get-tuple-element.17), channel_id=1, source_target_pairs={{0,2},{2,0},{4,6},{6,4},{8,10},{10,8},{12,14},{14,12},{16,18},{18,... | collective-permute-start | bytes 1572872 | tf_op jit(solution)/shard_map/ppermute | solution.py:247
  15.6 0.0 copy-start.2
  15.6 0.0 copy-start.4
  15.6 0.0 copy-start.6
  15.6 1.8 %dynamic-slice_bitcast_fusion.operators = bf16[2,1024,512]{2,1,0:T(8,128)(2,1)S(1)} fusion(bf16[2,2,2,1024,512]{4,3,2,1,0:T(8,128)(2,1)} %constant.54.clone.blocks, s32[]{:T(128)S(6)} %select_n.20, s32[]{:T(128)S(6)} %select_n.23), kind=kLoop, calls=%fused_computation | loop fusion | bytes 4194312 | tf_op jit(solution)/shard_map/jit(dynamic_index_in_dim)/squeeze | solution.py:225
  17.4 1.4 %collective-permute-done.3.refs_1_ = f32[1,2,512,128]{3,2,1,0:T(8,128)} collective-permute-done((f32[1,2,512,128]{3,2,1,0:T(8,128)}, f32[1,2,512,128]{3,2,1,0:T(8,128)}, u32[]{:S(2)}, u32[]{:S(2)}) %collective-permute-start.3) | collective-permute-done | bytes 524320 | tf_op jit(solution)/shard_map/ppermute | solution.py:247
  18.8 0.0 collective-permute-done.2.refs_0_
  18.8 0.0 copy-done.2
  18.8 0.0 copy-done.4
  18.8 0.0 copy-done.6
  18.8 0.0 copy-start
  18.8 2.0 %near.1 = (f32[2,512,128]{2,1,0:T(8,128)S(1)}, f32[2,512,128]{2,1,0:T(8,128)S(1)}, f32[2,512,128]{2,1,0:T(8,128)S(1)}) custom-call(f32[3,2,512,128]{3,2,1,0:T(8,128)} %velocity.7, f32[2,2,512,128]{3,2,1,0:T(8,128)} %collective-permute-done.2.refs_0_, f32[1,2,512,128]{3,2,1,0:T(8,128)} %collective-permute-done.3.refs_1_, f32[2,512,128]{2,1,0:T(8,128)S(1)} %copy-done.2, ...), custom_call_target="tpu_custom_call" | custom-call | tf_op jit(solution)/shard_map/near/pallas_call | solution.py:196
  20.9 16.7 %collective-permute-done.1.others = f32[3,2,512,128]{3,2,1,0:T(8,128)S(1)} collective-permute-done((f32[3,2,512,128]{3,2,1,0:T(8,128)}, f32[3,2,512,128]{3,2,1,0:T(8,128)S(1)}, u32[]{:S(2)}, u32[]{:S(2)}) %collective-permute-start.1) | collective-permute-done | bytes 1572896 | tf_op jit(solution)/shard_map/ppermute | solution.py:218
  37.6 0.0 copy-done
  37.6 2.6 %remote.1 = (f32[2,512,128]{2,1,0:T(8,128)S(1)}, f32[2,512,128]{2,1,0:T(8,128)S(1)}, f32[2,512,128]{2,1,0:T(8,128)S(1)}) custom-call(bf16[2,1024,512]{2,1,0:T(8,128)(2,1)S(1)} %dynamic-slice_bitcast_fusion.operators, f32[3,2,512,128]{3,2,1,0:T(8,128)S(1)} %copy-done, f32[3,2,512,128]{3,2,1,0:T(8,128)S(1)} %collective-permute-done.1.others, ...), custom_call_target="tpu_custom_call" | custom-call | tf_op jit(solution)/shard_map/remote/pallas_call | solution.py:196
  40.2 0.0 collective-permute-done.far
  40.2 1.3 %far.1 = f32[3,2,512,128]{3,2,1,0:T(8,128)} custom-call(f32[3,2,512,128]{3,2,1,0:T(8,128)S(1)} %copy-done, f32[3,2,512,128]{3,2,1,0:T(8,128)S(1)} %collective-permute-done.far, f32[2,512,128]{2,1,0:T(8,128)S(1)} %get-tuple-element.24.refs_0_, f32[2,512,128]{2,1,0:T(8,128)S(1)} %get-tuple-element.25.refs_1_, f32[2,512,128]{2,1,0:T(8,128)S(1)} %get-tuple-element.26.refs_2_), custom_call_target="tpu_custom_call" | custom-call | tf_op jit(solution)/shard_map/far/pallas_call | solution.py:196
Async XLA Ops:
  0.0 37.6 %collective-permute-start.1 = (f32[3,2,512,128]{3,2,1,0:T(8,128)}, f32[3,2,512,128]{3,2,1,0:T(8,128)S(1)}, u32[]{:S(2)}, u32[]{:S(2)}) collective-permute-start(f32[3,2,512,128]{3,2,1,0:T(8,128)} %velocity.7), channel_id=1, source_target_pairs={{0,1},{1,0},{2,3},{3,2},{4,5},{5,4},{6,7},{7,6},{8,9},{9,8},{10,11... | collective-permute-start | bytes 4718600 | tf_op jit(solution)/shard_map/ppermute | solution.py:218
  3.0 37.2 %collective-permute-start = (f32[3,2,512,128]{3,2,1,0:T(8,128)}, f32[3,2,512,128]{3,2,1,0:T(8,128)S(1)}, u32[]{:S(2)}, u32[]{:S(2)}) collective-permute-start(f32[3,2,512,128]{3,2,1,0:T(8,128)} %velocity.7), channel_id=1, source_target_pairs={{0,30},{2,4},{4,2},{6,8},{8,6},{10,12},{12,10},{14,16},{16,14},{18... | collective-permute-start | bytes 4718600 | tf_op jit(solution)/shard_map/ppermute | solution.py:216
  12.6 0.8 %copy-start.1 = (f32[2,512,128]{2,1,0:T(8,128)}, f32[2,512,128]{2,1,0:T(8,128)S(1)}, u32[]{:S(2)}) copy-start(f32[2,512,128]{2,1,0:T(8,128)S(1)} %get-tuple-element.18.refs_2_) | copy-start | bytes 1572868
  13.4 0.8 %copy-start.3 = (f32[2,512,128]{2,1,0:T(8,128)}, f32[2,512,128]{2,1,0:T(8,128)S(1)}, u32[]{:S(2)}) copy-start(f32[2,512,128]{2,1,0:T(8,128)S(1)} %get-tuple-element.19.refs_3_) | copy-start | bytes 1572868
  14.2 0.8 %copy-start.5 = (f32[2,512,128]{2,1,0:T(8,128)}, f32[2,512,128]{2,1,0:T(8,128)S(1)}, u32[]{:S(2)}) copy-start(f32[2,512,128]{2,1,0:T(8,128)S(1)} %get-tuple-element.20.refs_4_) | copy-start | bytes 1572868
  15.0 3.8 %collective-permute-start.2 = (f32[2,2,512,128]{3,2,1,0:T(8,128)}, f32[2,2,512,128]{3,2,1,0:T(8,128)}, u32[]{:S(2)}, u32[]{:S(2)}) collective-permute-start(f32[2,2,512,128]{3,2,1,0:T(8,128)} %get-tuple-element.16), channel_id=1, source_target_pairs={{0,2},{2,0},{4,6},{6,4},{8,10},{10,8},{12,14},{14,12},{16,18},{18,... | collective-permute-start | bytes 3145736 | tf_op jit(solution)/shard_map/ppermute | solution.py:247
  15.0 3.7 %collective-permute-start.3 = (f32[1,2,512,128]{3,2,1,0:T(8,128)}, f32[1,2,512,128]{3,2,1,0:T(8,128)}, u32[]{:S(2)}, u32[]{:S(2)}) collective-permute-start(f32[1,2,512,128]{3,2,1,0:T(8,128)} %get-tuple-element.17), channel_id=1, source_target_pairs={{0,2},{2,0},{4,6},{6,4},{8,10},{10,8},{12,14},{14,12},{16,18},{18,... | collective-permute-start | bytes 1572872 | tf_op jit(solution)/shard_map/ppermute | solution.py:247
  15.6 3.2 %copy-start.2 = (f32[2,512,128]{2,1,0:T(8,128)S(1)}, f32[2,512,128]{2,1,0:T(8,128)}, u32[]{:S(2)}) copy-start(f32[2,512,128]{2,1,0:T(8,128)} %copy-done.1) | copy-start | bytes 1572868
  15.6 3.2 %copy-start.4 = (f32[2,512,128]{2,1,0:T(8,128)S(1)}, f32[2,512,128]{2,1,0:T(8,128)}, u32[]{:S(2)}) copy-start(f32[2,512,128]{2,1,0:T(8,128)} %copy-done.3) | copy-start | bytes 1572868
  15.6 3.3 %copy-start.6 = (f32[2,512,128]{2,1,0:T(8,128)S(1)}, f32[2,512,128]{2,1,0:T(8,128)}, u32[]{:S(2)}) copy-start(f32[2,512,128]{2,1,0:T(8,128)} %copy-done.5) | copy-start | bytes 1572868
  18.8 18.8 %copy-start = (f32[3,2,512,128]{3,2,1,0:T(8,128)S(1)}, f32[3,2,512,128]{3,2,1,0:T(8,128)}, u32[]{:S(2)}) copy-start(f32[3,2,512,128]{3,2,1,0:T(8,128)} %velocity.7) | copy-start | bytes 4718596

commit v4 on v3

--- a/solution.py
+++ b/solution.py
@@ -27,6 +27,9 @@
 
 VMEM_LIMIT = 24 * 1024 * 1024
 PIECES = ((0, 1), (2,))
+COARSE_LARGEST = 224.0
+COARSE_LIFT = 32.0
+LOW_LIFT = 512.0
 
 
 def chebyshev_matrices(total):
@@ -63,10 +66,21 @@
         [first.astype(np.float64) * SCALE, second.astype(np.float64) * (SCALE * VISCOSITY)]
     ).astype(np.float32)
     blocks = stacked.reshape(2, parts, rows, parts, rows).transpose(1, 3, 0, 2, 4)
-    blocks = blocks.reshape(parts, parts, 2 * rows, rows)
-    high = blocks.astype(jnp.bfloat16)
-    low = (blocks - high.astype(np.float32)).astype(jnp.bfloat16)
-    return np.stack([high, low], axis=2)
+    mine = np.arange(parts)
+    own = blocks[mine, mine]
+    there = np.stack([blocks[mine, (mine - k) % parts] for k in range(1, parts)], axis=1)
+    largest = np.max(np.abs(there), axis=(0, 1, 3, 4))
+    scale = np.exp2(np.floor(np.log2(COARSE_LARGEST / largest))).astype(np.float32)
+    own = own.reshape(parts, 2 * rows, rows)
+    high = own.astype(jnp.bfloat16)
+    own = np.stack([high, (own - high.astype(np.float32)).astype(jnp.bfloat16)], axis=1)
+    high = there.astype(jnp.bfloat16)
+    low = there - high.astype(np.float32)
+    coarse = np.concatenate([LOW_LIFT * low, there], axis=-1) * scale[:, None, None]
+    coarse = coarse.astype(jnp.float8_e4m3fn)
+    shape = (parts, parts - 1, 2 * rows)
+    undo = [float(1.0 / (x * LOW_LIFT * COARSE_LIFT)) for x in scale]
+    return own, high.reshape(shape + (rows,)), coarse.reshape(shape + (2 * rows,)), undo
 
 
 def wall(operators, fields, v):
@@ -81,6 +95,27 @@
     return added[:, : v.shape[2]], added[:, v.shape[2] :]
 
 
+def wall_there(undo, high_operators, coarse_operators, fields, v):
+    rows = v.shape[1]
+    side = jnp.concatenate([fields[0], fields[1]], axis=1)
+    high = side.astype(jnp.bfloat16)
+    low = side - high.astype(jnp.float32)
+    coarse = jnp.concatenate(
+        [
+            (COARSE_LIFT * side).astype(jnp.float8_e4m3fn),
+            (LOW_LIFT * COARSE_LIFT * low).astype(jnp.float8_e4m3fn),
+        ],
+        axis=0,
+    )
+    dot = functools.partial(jnp.dot, preferred_element_type=jnp.float32)
+    product = dot(high_operators[...], high)
+    rest = dot(coarse_operators[...], coarse)
+    first = product[:rows] + undo[0] * rest[:rows]
+    second = product[rows:] + undo[1] * rest[rows:]
+    added = second - jnp.concatenate([v[0], v[1]], axis=1) * first
+    return added[:, : v.shape[2]], added[:, v.shape[2] :]
+
+
 def along_x(parity):
     return jnp.where(parity == 0, X_FIRST, -X_FIRST).astype(jnp.float32)
 
@@ -91,7 +126,7 @@
     me = lax.axis_index("gy")
     fetches = [
         pltpu.make_async_copy(velocity, own, came.at[0]),
-        pltpu.make_async_copy(blocks.at[me, me], operators, came.at[1]),
+        pltpu.make_async_copy(blocks.at[me], operators, came.at[1]),
         pltpu.make_async_copy(previous, past, came.at[2]),
     ]
     for fetch in fetches:
@@ -149,10 +184,10 @@
         )
 
 
-def remote_kernel(operators, velocity, others, *refs):
+def remote_kernel(undo, high_operators, coarse_operators, velocity, others, *refs):
     for q in range(3):
         base, out = refs[q], refs[3 + q]
-        added = wall(operators, others[q], velocity[1])
+        added = wall_there(undo, high_operators, coarse_operators, others[q], velocity[1])
         for plane in range(2):
             out[plane] = base[plane] + added[plane]
 
@@ -219,18 +254,16 @@
         for k in range(1, parts)
     ]
 
-    blocks = jnp.asarray(operator_blocks(rows * parts, parts))
-    mine = lax.dynamic_index_in_dim(blocks, me, 0, keepdims=False)
-    operators = [
-        lax.dynamic_index_in_dim(mine, (me - k) % parts, 0, keepdims=False)
-        for k in range(1, parts)
-    ]
+    own, high, coarse, undo = operator_blocks(rows * parts, parts)
+    own = jnp.asarray(own)
+    high = lax.dynamic_index_in_dim(jnp.asarray(high), me, 0, keepdims=False)
+    coarse = lax.dynamic_index_in_dim(jnp.asarray(coarse), me, 0, keepdims=False)
 
     one = jax.ShapeDtypeStruct(shape[1:], jnp.float32)
     whole = jax.ShapeDtypeStruct(shape, jnp.float32)
     totals = call(
         local_kernel,
-        (hbm(blocks), hbm(velocity), hbm(previous)),
+        (hbm(own), hbm(velocity), hbm(previous)),
         [ANY] * 3,
         (one,) * 3
         + tuple(jax.ShapeDtypeStruct((len(c),) + shape[1:], jnp.float32) for c in PIECES),
@@ -239,7 +272,7 @@
         scratch_shapes=[
             pltpu.VMEM(shape, jnp.float32),
             pltpu.VMEM(shape, jnp.float32),
-            pltpu.VMEM(blocks.shape[2:], jnp.bfloat16),
+            pltpu.VMEM(own.shape[1:], jnp.bfloat16),
             pltpu.SemaphoreType.DMA((3,)),
             pltpu.SemaphoreType.DMA((len(PIECES),)),
         ],
@@ -259,9 +292,12 @@
     )
     for k in range(1, parts):
         totals = call(
-            remote_kernel,
-            (vmem(operators[k - 1]), vmem(velocity), vmem(others[k - 1]), *totals),
-            [VMEM] * 6,
+            functools.partial(remote_kernel, undo),
+            (
+                *map(vmem, (high[k - 1], coarse[k - 1], velocity, others[k - 1])),
+                *totals,
+            ),
+            [VMEM] * 7,
             (one,) * 3,
             "remote",
         )

time: 41.6 us -> 40.9 us (0.983)
  the two profiles are of different devices: /device:TPU:0 before, /device:TPU:1 now
where the time goes in v4:
time: 40.9 us; the launch traced here: 40.6 us
  waiting for transfers between devices  17.5 us (43%)
  Pallas kernels  11.1 us (27%)
  starting transfers between devices  6.71 us (16%)
  local copies, waits for them, and re-layouts  5.18 us (13%)
    ppermute x1, waiting for transfers between devices, shards(): lax.ppermute(velocity, 'gy', [(i, (i + k) % parts) for i in range(parts)])  15.8 us
    pallas_call x4, Pallas kernels, call(): pl.pallas_call(kernel, in_specs=in_specs, out_shape=out_shape, compiler_p...  11.1 us
    ppermute x2, starting transfers between devices, shards(): near = [lax.ppermute(part, 'gx', inward) for part in totals[3:]]  2.59 us
    unnamed x14, local copies, waits for them, and re-layouts  2.43 us
    ppermute x1, starting transfers between devices, shards(): lax.ppermute(velocity, 'gy', [(i, (i + k) % parts) for i in range(parts)])  2.07 us
    ppermute x1, starting transfers between devices, shards(): far = lax.ppermute(velocity, 'gx', outward)  2.05 us
    squeeze x1, local copies, waits for them, and re-layouts, shards(): high[k - 1]  1.42 us
    squeeze x1, local copies, waits for them, and re-layouts, shards(): coarse[k - 1]  1.33 us
  transfers between devices with their start and end apart: 4, of which 3 were waited for; matrix products, arithmetic and copies ran while one was open for 7% of the time, Pallas kernels for 24%

profile of v4, /device:TPU:1, one launch (start us, length us, event | category | flops | bytes accessed | tf_op | source)
XLA Modules:
  0.0 40.6 jit_solution(718676827046544909)
XLA Ops:
  0.0 2.1 %collective-permute-start.1 = (f32[3,2,512,128]{3,2,1,0:T(8,128)}, f32[3,2,512,128]{3,2,1,0:T(8,128)S(1)}, u32[]{:S(2)}, u32[]{:S(2)}) collective-permute-start(f32[3,2,512,128]{3,2,1,0:T(8,128)} %velocity.7), channel_id=1, source_target_pairs={{0,1},{1,0},{2,3},{3,2},{4,5},{5,4},{6,7},{7,6},{8,9},{9,8},{10,11... | collective-permute-start | bytes 4718600 | tf_op jit(solution)/shard_map/ppermute | solution.py:253
  2.1 2.1 %collective-permute-start = (f32[3,2,512,128]{3,2,1,0:T(8,128)}, f32[3,2,512,128]{3,2,1,0:T(8,128)S(1)}, u32[]{:S(2)}, u32[]{:S(2)}) collective-permute-start(f32[3,2,512,128]{3,2,1,0:T(8,128)} %velocity.7), channel_id=1, source_target_pairs={{0,30},{2,4},{4,2},{6,8},{8,6},{10,12},{12,10},{14,16},{16,14},{18... | collective-permute-start | bytes 4718600 | tf_op jit(solution)/shard_map/ppermute | solution.py:251
  4.1 6.0 %local.1 = (f32[2,512,128]{2,1,0:T(8,128)S(1)}, f32[2,512,128]{2,1,0:T(8,128)S(1)}, f32[2,512,128]{2,1,0:T(8,128)S(1)}, f32[2,2,512,128]{3,2,1,0:T(8,128)}, f32[1,2,512,128]{3,2,1,0:T(8,128)}) custom-call(bf16[2,2,1024,512]{3,2,1,0:T(8,128)(2,1)} %constant.20.clone.blocks, f32[3,2,512,128]{3,2,1,0:T(8,128)} %velocity.7, f32[3,2,512,128]{3,2,1,0:T(8,128)} %previous.1), custom_call_target="tpu_custom_call" | custom-call | tf_op jit(solution)/shard_map/local/pallas_call | solution.py:231
  10.1 0.0 copy-start.1
  10.1 0.8 %copy-done.1 = f32[2,512,128]{2,1,0:T(8,128)} copy-done((f32[2,512,128]{2,1,0:T(8,128)}, f32[2,512,128]{2,1,0:T(8,128)S(1)}, u32[]{:S(2)}) %copy-start.1) | copy-done | bytes 524312
  10.9 0.0 copy-start.3
  10.9 0.8 %copy-done.3 = f32[2,512,128]{2,1,0:T(8,128)} copy-done((f32[2,512,128]{2,1,0:T(8,128)}, f32[2,512,128]{2,1,0:T(8,128)S(1)}, u32[]{:S(2)}) %copy-start.3) | copy-done | bytes 524312
  11.7 0.0 copy-start.5
  11.7 0.8 %copy-done.5 = f32[2,512,128]{2,1,0:T(8,128)} copy-done((f32[2,512,128]{2,1,0:T(8,128)}, f32[2,512,128]{2,1,0:T(8,128)S(1)}, u32[]{:S(2)}) %copy-start.5) | copy-done | bytes 524312
  12.5 2.6 %collective-permute-start.2 = (f32[2,2,512,128]{3,2,1,0:T(8,128)}, f32[2,2,512,128]{3,2,1,0:T(8,128)}, u32[]{:S(2)}, u32[]{:S(2)}) collective-permute-start(f32[2,2,512,128]{3,2,1,0:T(8,128)} %get-tuple-element.16), channel_id=1, source_target_pairs={{0,2},{2,0},{4,6},{6,4},{8,10},{10,8},{12,14},{14,12},{16,18},{18,... | collective-permute-start | bytes 3145736 | tf_op jit(solution)/shard_map/ppermute | solution.py:280
  15.1 0.0 collective-permute-start.3
  15.1 0.0 copy-start.2
  15.1 0.0 copy-start.4
  15.1 0.0 copy-start.6
  15.1 1.4 %dynamic-slice_bitcast_fusion.1.high_operators = bf16[1024,512]{1,0:T(8,128)(2,1)S(1)} fusion(bf16[2,1,1024,512]{3,2,1,0:T(8,128)(2,1)} %constant.21.clone, s32[]{:T(128)S(6)} %select_n.6), kind=kLoop, calls=%fused_computation.1 | loop fusion | bytes 2097156 | tf_op jit(solution)/shard_map/squeeze | solution.py:297
  16.5 1.3 %dynamic-slice_bitcast_fusion.coarse_operators = f8e4m3fn[1024,1024]{1,0:T(32,128)(4,1)S(1)} fusion(f8e4m3fn[2,1,1024,1024]{3,2,1,0:T(32,128)(4,1)} %constant.22.clone, s32[]{:T(128)S(6)} %select_n.6), kind=kLoop, calls=%fused_computation | loop fusion | bytes 2097156 | tf_op jit(solution)/shard_map/squeeze | solution.py:297
  17.9 0.6 %collective-permute-done.3.refs_1_ = f32[1,2,512,128]{3,2,1,0:T(8,128)} collective-permute-done((f32[1,2,512,128]{3,2,1,0:T(8,128)}, f32[1,2,512,128]{3,2,1,0:T(8,128)}, u32[]{:S(2)}, u32[]{:S(2)}) %collective-permute-start.3) | collective-permute-done | bytes 524320 | tf_op jit(solution)/shard_map/ppermute | solution.py:280
  18.5 0.0 collective-permute-done.2.refs_0_
  18.5 0.0 copy-done.2
  18.5 0.0 copy-done.4
  18.5 0.0 copy-done.6
  18.5 0.0 copy-start
  18.5 2.0 %near.1 = (f32[2,512,128]{2,1,0:T(8,128)S(1)}, f32[2,512,128]{2,1,0:T(8,128)S(1)}, f32[2,512,128]{2,1,0:T(8,128)S(1)}) custom-call(f32[3,2,512,128]{3,2,1,0:T(8,128)} %velocity.7, f32[2,2,512,128]{3,2,1,0:T(8,128)} %collective-permute-done.2.refs_0_, f32[1,2,512,128]{3,2,1,0:T(8,128)} %collective-permute-done.3.refs_1_, f32[2,512,128]{2,1,0:T(8,128)S(1)} %copy-done.2, ...), custom_call_target="tpu_custom_call" | custom-call | tf_op jit(solution)/shard_map/near/pallas_call | solution.py:231
  20.6 15.8 %collective-permute-done.1.others = f32[3,2,512,128]{3,2,1,0:T(8,128)S(1)} collective-permute-done((f32[3,2,512,128]{3,2,1,0:T(8,128)}, f32[3,2,512,128]{3,2,1,0:T(8,128)S(1)}, u32[]{:S(2)}, u32[]{:S(2)}) %collective-permute-start.1) | collective-permute-done | bytes 1572896 | tf_op jit(solution)/shard_map/ppermute | solution.py:253
  36.4 0.0 copy-done
  36.4 1.9 %remote.1 = (f32[2,512,128]{2,1,0:T(8,128)S(1)}, f32[2,512,128]{2,1,0:T(8,128)S(1)}, f32[2,512,128]{2,1,0:T(8,128)S(1)}) custom-call(bf16[1024,512]{1,0:T(8,128)(2,1)S(1)} %dynamic-slice_bitcast_fusion.1.high_operators, f8e4m3fn[1024,1024]{1,0:T(32,128)(4,1)S(1)} %dynamic-slice_bitcast_fusion.coarse_operators, f32[3,2,512,128]{3,2,1,0:T(8,128)S(1)} %copy-done, ...), custom_call_target="tpu_custom_call" | custom-call | tf_op jit(solution)/shard_map/remote/pallas_call | solution.py:231
  38.3 1.0 %collective-permute-done.far = f32[3,2,512,128]{3,2,1,0:T(8,128)S(1)} collective-permute-done((f32[3,2,512,128]{3,2,1,0:T(8,128)}, f32[3,2,512,128]{3,2,1,0:T(8,128)S(1)}, u32[]{:S(2)}, u32[]{:S(2)}) %collective-permute-start) | collective-permute-done | bytes 1572896 | tf_op jit(solution)/shard_map/ppermute | solution.py:251
  39.3 1.3 %far.1 = f32[3,2,512,128]{3,2,1,0:T(8,128)} custom-call(f32[3,2,512,128]{3,2,1,0:T(8,128)S(1)} %copy-done, f32[3,2,512,128]{3,2,1,0:T(8,128)S(1)} %collective-permute-done.far, f32[2,512,128]{2,1,0:T(8,128)S(1)} %get-tuple-element.24.refs_0_, f32[2,512,128]{2,1,0:T(8,128)S(1)} %get-tuple-element.25.refs_1_, f32[2,512,128]{2,1,0:T(8,128)S(1)} %get-tuple-element.26.refs_2_), custom_call_target="tpu_custom_call" | custom-call | tf_op jit(solution)/shard_map/far/pallas_call | solution.py:231
Async XLA Ops:
  0.0 36.4 %collective-permute-start.1 = (f32[3,2,512,128]{3,2,1,0:T(8,128)}, f32[3,2,512,128]{3,2,1,0:T(8,128)S(1)}, u32[]{:S(2)}, u32[]{:S(2)}) collective-permute-start(f32[3,2,512,128]{3,2,1,0:T(8,128)} %velocity.7), channel_id=1, source_target_pairs={{0,1},{1,0},{2,3},{3,2},{4,5},{5,4},{6,7},{7,6},{8,9},{9,8},{10,11... | collective-permute-start | bytes 4718600 | tf_op jit(solution)/shard_map/ppermute | solution.py:253
  2.1 37.2 %collective-permute-start = (f32[3,2,512,128]{3,2,1,0:T(8,128)}, f32[3,2,512,128]{3,2,1,0:T(8,128)S(1)}, u32[]{:S(2)}, u32[]{:S(2)}) collective-permute-start(f32[3,2,512,128]{3,2,1,0:T(8,128)} %velocity.7), channel_id=1, source_target_pairs={{0,30},{2,4},{4,2},{6,8},{8,6},{10,12},{12,10},{14,16},{16,14},{18... | collective-permute-start | bytes 4718600 | tf_op jit(solution)/shard_map/ppermute | solution.py:251
  10.1 0.8 %copy-start.1 = (f32[2,512,128]{2,1,0:T(8,128)}, f32[2,512,128]{2,1,0:T(8,128)S(1)}, u32[]{:S(2)}) copy-start(f32[2,512,128]{2,1,0:T(8,128)S(1)} %get-tuple-element.18.refs_2_) | copy-start | bytes 1572868
  10.9 0.8 %copy-start.3 = (f32[2,512,128]{2,1,0:T(8,128)}, f32[2,512,128]{2,1,0:T(8,128)S(1)}, u32[]{:S(2)}) copy-start(f32[2,512,128]{2,1,0:T(8,128)S(1)} %get-tuple-element.19.refs_3_) | copy-start | bytes 1572868
  11.7 0.8 %copy-start.5 = (f32[2,512,128]{2,1,0:T(8,128)}, f32[2,512,128]{2,1,0:T(8,128)S(1)}, u32[]{:S(2)}) copy-start(f32[2,512,128]{2,1,0:T(8,128)S(1)} %get-tuple-element.20.refs_4_) | copy-start | bytes 1572868
  12.5 6.0 %collective-permute-start.2 = (f32[2,2,512,128]{3,2,1,0:T(8,128)}, f32[2,2,512,128]{3,2,1,0:T(8,128)}, u32[]{:S(2)}, u32[]{:S(2)}) collective-permute-start(f32[2,2,512,128]{3,2,1,0:T(8,128)} %get-tuple-element.16), channel_id=1, source_target_pairs={{0,2},{2,0},{4,6},{6,4},{8,10},{10,8},{12,14},{14,12},{16,18},{18,... | collective-permute-start | bytes 3145736 | tf_op jit(solution)/shard_map/ppermute | solution.py:280
  15.1 3.4 %collective-permute-start.3 = (f32[1,2,512,128]{3,2,1,0:T(8,128)}, f32[1,2,512,128]{3,2,1,0:T(8,128)}, u32[]{:S(2)}, u32[]{:S(2)}) collective-permute-start(f32[1,2,512,128]{3,2,1,0:T(8,128)} %get-tuple-element.17), channel_id=1, source_target_pairs={{0,2},{2,0},{4,6},{6,4},{8,10},{10,8},{12,14},{14,12},{16,18},{18,... | collective-permute-start | bytes 1572872 | tf_op jit(solution)/shard_map/ppermute | solution.py:280
  15.1 3.4 %copy-start.2 = (f32[2,512,128]{2,1,0:T(8,128)S(1)}, f32[2,512,128]{2,1,0:T(8,128)}, u32[]{:S(2)}) copy-start(f32[2,512,128]{2,1,0:T(8,128)} %copy-done.1) | copy-start | bytes 1572868
  15.1 3.4 %copy-start.4 = (f32[2,512,128]{2,1,0:T(8,128)S(1)}, f32[2,512,128]{2,1,0:T(8,128)}, u32[]{:S(2)}) copy-start(f32[2,512,128]{2,1,0:T(8,128)} %copy-done.3) | copy-start | bytes 1572868
  15.1 3.4 %copy-start.6 = (f32[2,512,128]{2,1,0:T(8,128)S(1)}, f32[2,512,128]{2,1,0:T(8,128)}, u32[]{:S(2)}) copy-start(f32[2,512,128]{2,1,0:T(8,128)} %copy-done.5) | copy-start | bytes 1572868
  18.5 17.9 %copy-start = (f32[3,2,512,128]{3,2,1,0:T(8,128)S(1)}, f32[3,2,512,128]{3,2,1,0:T(8,128)}, u32[]{:S(2)}) copy-start(f32[3,2,512,128]{3,2,1,0:T(8,128)} %velocity.7) | copy-start | bytes 4718596

commit v5 on v4

--- a/solution.py
+++ b/solution.py
@@ -184,32 +184,82 @@
         )
 
 
-def remote_kernel(undo, high_operators, coarse_operators, velocity, others, *refs):
-    for q in range(3):
-        base, out = refs[q], refs[3 + q]
-        added = wall_there(undo, high_operators, coarse_operators, others[q], velocity[1])
-        for plane in range(2):
-            out[plane] = base[plane] + added[plane]
-
-
-def far_kernel(velocity, far, *refs):
-    bases, (out, total, sent) = refs[:3], refs[3:]
+def far_terms(u):
     parity = lax.axis_index("gx") % 2
     inner, outer = 1 - parity, parity
     along = along_x(parity)
-    stores = []
+    inner_first = along * u[inner] + X_SECOND
+    outer_second = along * u[outer] + X_SECOND
+    outer_first = 8.0 * (outer_second + X_SECOND)
+
+    def terms(far):
+        first, second = far[1 - parity], far[parity]
+        return (inner, -(inner_first * first)), (outer, outer_first * first - outer_second * second)
+
+    return terms
+
+
+def add(base, out, *terms):
+    for plane, term in terms:
+        out[plane] = base[plane] + term
+
+
+def far_first(place):
+    return (place + 1) // 2 % 2 == 1
+
+
+def remote_kernel(undo, high_operators, coarse_operators, velocity, others, *refs):
     for q in range(3):
-        first, second = far[q, 1 - parity], far[q, parity]
-        total[q, inner] = (
-            bases[q][inner] - X_SECOND * first - (along * velocity[0, inner]) * first
-        )
-        total[q, outer] = (
-            bases[q][outer]
-            + X_SECOND * (16.0 * first - second)
-            + (along * velocity[0, outer]) * (8.0 * first - second)
-        )
-        stores.append(pltpu.make_async_copy(total.at[q], out.at[q], sent.at[q]))
-        stores[-1].start()
+        terms = wall_there(undo, high_operators, coarse_operators, others[q], velocity[1])
+        add(refs[q], refs[3 + q], *enumerate(terms))
+
+
+def middle_kernel(undo, high_operators, coarse_operators, velocity, piece, *refs):
+    bases, outs = refs[: len(refs) // 2], refs[len(refs) // 2 :]
+    swapped = far_first(lax.axis_index("gx"))
+
+    @pl.when(swapped)
+    def _():
+        for i, (base, out) in enumerate(zip(bases, outs)):
+            terms = wall_there(undo, high_operators, coarse_operators, piece[i], velocity[1])
+            add(base, out, *enumerate(terms))
+
+    @pl.when(jnp.logical_not(swapped))
+    def _():
+        terms = far_terms(velocity.at[0])
+        for i, (base, out) in enumerate(zip(bases, outs)):
+            add(base, out, *terms(piece.at[i]))
+
+
+def last_kernel(undo, high_operators, coarse_operators, velocity, whole, piece, *refs):
+    bases, (out, total, sent) = refs[:3], refs[3:]
+    swapped = far_first(lax.axis_index("gx"))
+    rest = PIECES[-1]
+    stores = [pltpu.make_async_copy(total.at[q], out.at[q], sent.at[q]) for q in range(3)]
+
+    @pl.when(swapped)
+    def _():
+        terms = far_terms(velocity.at[0])
+        for q in range(3):
+            out = total.at[q]
+            add(bases[q], out, *terms(whole.at[q]))
+            if q in rest:
+                field = piece[rest.index(q)]
+                more = wall_there(undo, high_operators, coarse_operators, field, velocity[1])
+                add(out, out, *enumerate(more))
+            stores[q].start()
+
+    @pl.when(jnp.logical_not(swapped))
+    def _():
+        terms = far_terms(velocity.at[0])
+        for q in range(3):
+            out = total.at[q]
+            more = wall_there(undo, high_operators, coarse_operators, whole[q], velocity[1])
+            add(bases[q], out, *enumerate(more))
+            if q in rest:
+                add(out, out, *terms(piece.at[rest.index(q)]))
+            stores[q].start()
+
     for store in stores:
         store.wait()
 
@@ -242,16 +292,24 @@
 def shards(parts, velocity, previous):
     count = lax.axis_size("gx")
     shape = velocity.shape
-    assert shape[0] == 3 and shape[1] == 2 and count % 2 == 0
+    assert shape[0] == 3 and shape[1] == 2 and count % 4 == 0
     rows = shape[2]
     me = lax.axis_index("gy")
 
-    outward = [(i, (i - 1) % count if i % 2 == 0 else (i + 1) % count) for i in range(count)]
     inward = [(i, i ^ 1) for i in range(count)]
-    far = lax.ppermute(velocity, "gx", outward)
+    firsts, seconds = [], []
+    for g in range(count):
+        beyond = (g - 1) % count if g % 2 == 0 else (g + 1) % count
+        for i in range(parts):
+            here = g * parts + i
+            pair = [(here, beyond * parts + i), (here, g * parts + (i + 1) % parts)]
+            firsts.append(pair[0] if far_first(g) else pair[1])
+            seconds.append(pair[1] if far_first(g) else pair[0])
+    both = ("gx", "gy")
+    first = lax.ppermute(velocity, both, firsts)
     others = [
         lax.ppermute(velocity, "gy", [(i, (i + k) % parts) for i in range(parts)])
-        for k in range(1, parts)
+        for k in range(2, parts)
     ]
 
     own, high, coarse, undo = operator_blocks(rows * parts, parts)
@@ -278,6 +336,7 @@
         ],
     )
     near = [lax.ppermute(part, "gx", inward) for part in totals[3:]]
+    second = [lax.ppermute(part, both, seconds) for part in totals[3:]]
     totals = call(
         near_kernel,
         (hbm(velocity), *map(hbm, near), *totals[:3]),
@@ -290,28 +349,34 @@
             pltpu.SemaphoreType.DMA((4,)),
         ],
     )
-    for k in range(1, parts):
+    for k in range(2, parts):
         totals = call(
             functools.partial(remote_kernel, undo),
-            (
-                *map(vmem, (high[k - 1], coarse[k - 1], velocity, others[k - 1])),
-                *totals,
-            ),
+            (high[k - 1], coarse[k - 1], velocity, others[k - 2], *totals),
             [VMEM] * 7,
             (one,) * 3,
             "remote",
         )
+    totals = list(totals)
+    fixed = (vmem(high[0]), vmem(coarse[0]), vmem(velocity))
+    for c, piece in zip(PIECES[:-1], second):
+        added = call(
+            functools.partial(middle_kernel, undo),
+            (*fixed, piece, *(totals[q] for q in c)),
+            [VMEM] * (4 + len(c)),
+            (one,) * len(c),
+            "middle",
+        )
+        for q, total in zip(c, added):
+            totals[q] = total
     return call(
-        far_kernel,
-        (vmem(velocity), vmem(far), *totals),
-        [VMEM] * 5,
+        functools.partial(last_kernel, undo),
+        (*fixed, vmem(first), vmem(second[-1]), *totals),
+        [VMEM] * 8,
         whole,
-        "far",
+        "last",
         out_specs=ANY,
-        scratch_shapes=[
-            pltpu.VMEM(shape, jnp.float32),
-            pltpu.SemaphoreType.DMA((3,)),
-        ],
+        scratch_shapes=[pltpu.VMEM(shape, jnp.float32), pltpu.SemaphoreType.DMA((3,))],
     )
 
 

time: 40.9 us -> 40.1 us (0.980)
  waiting for transfers between devices: 17.5 us -> 15.9 us
  starting transfers between devices: 6.71 us -> 7.39 us
    ppermute x2 -> x3, waiting for transfers between devices: 16.9 us -> 15.9 us  [the longest x2 15.8 us: shards(): second = [lax.ppermute(part, both, seconds) for part in totals[3:]]]
    ppermute x2, starting transfers between devices: 2.59 us -> 3.3 us  [shards(): near = [lax.ppermute(part, 'gx', inward) for part in totals[3:]]]
    ppermute x2, waiting for transfers between devices: 0.61 us -> 0.01 us  [shards(): near = [lax.ppermute(part, 'gx', inward) for part in totals[3:]]]
    ppermute x2 -> x3, starting transfers between devices: 4.12 us -> 4.09 us  [the longest x1 2.6 us: shards(): first = lax.ppermute(velocity, both, firsts)]
  transfers between devices with their start and end apart: 4 -> 5, of which waited for: 3 -> 2; matrix products, arithmetic and copies ran while one was open for 7% -> 7% of each run, Pallas kernels for 24% -> 23%
where the time goes in v5:
time: 40.1 us; the launch traced here: 39.9 us
  waiting for transfers between devices  15.9 us (40%)
  Pallas kernels  11.4 us (28%)
  starting transfers between devices  7.39 us (18%)
  local copies, waits for them, and re-layouts  5.16 us (13%)
    ppermute x2, waiting for transfers between devices, shards(): second = [lax.ppermute(part, both, seconds) for part in totals[3:]]  15.8 us
    pallas_call x4, Pallas kernels, call(): pl.pallas_call(kernel, in_specs=in_specs, out_shape=out_shape, compiler_p...  11.4 us
    ppermute x2, starting transfers between devices, shards(): near = [lax.ppermute(part, 'gx', inward) for part in totals[3:]]  3.3 us
    squeeze x2, local copies, waits for them, and re-layouts, shards(): fixed = (vmem(high[0]), vmem(coarse[0]), vmem(velocity))  2.74 us
    ppermute x1, starting transfers between devices, shards(): first = lax.ppermute(velocity, both, firsts)  2.6 us
    unnamed x14, local copies, waits for them, and re-layouts  2.41 us
    ppermute x2, starting transfers between devices, shards(): second = [lax.ppermute(part, both, seconds) for part in totals[3:]]  1.49 us
  transfers between devices with their start and end apart: 5, of which 2 were waited for; matrix products, arithmetic and copies ran while one was open for 7% of the time, Pallas kernels for 23%

profile of v5, /device:TPU:1, one launch (start us, length us, event | category | flops | bytes accessed | tf_op | source)
XLA Modules:
  0.0 39.9 jit_solution(757679446439008280)
XLA Ops:
  0.0 2.6 %collective-permute-start = (f32[3,2,512,128]{3,2,1,0:T(8,128)}, f32[3,2,512,128]{3,2,1,0:T(8,128)S(1)}, u32[]{:S(2)}, u32[]{:S(2)}) collective-permute-start(f32[3,2,512,128]{3,2,1,0:T(8,128)} %velocity.7), channel_id=1, source_target_pairs={{0,1},{1,0},{2,4},{3,5},{4,2},{5,3},{6,7},{7,6},{8,9},{9,8},{10,12... | collective-permute-start | bytes 4718600 | tf_op jit(solution)/shard_map/ppermute | solution.py:309
  2.6 6.0 %local.1 = (f32[2,512,128]{2,1,0:T(8,128)S(1)}, f32[2,512,128]{2,1,0:T(8,128)S(1)}, f32[2,512,128]{2,1,0:T(8,128)S(1)}, f32[2,2,512,128]{3,2,1,0:T(8,128)}, f32[1,2,512,128]{3,2,1,0:T(8,128)}) custom-call(bf16[2,2,1024,512]{3,2,1,0:T(8,128)(2,1)} %constant.20.clone.blocks, f32[3,2,512,128]{3,2,1,0:T(8,128)} %velocity.7, f32[3,2,512,128]{3,2,1,0:T(8,128)} %previous.1), custom_call_target="tpu_custom_call" | custom-call | tf_op jit(solution)/shard_map/local/pallas_call | solution.py:281
  8.6 0.0 copy-start.1
  8.6 0.8 %copy-done.1 = f32[2,512,128]{2,1,0:T(8,128)} copy-done((f32[2,512,128]{2,1,0:T(8,128)}, f32[2,512,128]{2,1,0:T(8,128)S(1)}, u32[]{:S(2)}) %copy-start.1) | copy-done | bytes 524312
  9.4 0.0 copy-start.3
  9.4 0.8 %copy-done.3 = f32[2,512,128]{2,1,0:T(8,128)} copy-done((f32[2,512,128]{2,1,0:T(8,128)}, f32[2,512,128]{2,1,0:T(8,128)S(1)}, u32[]{:S(2)}) %copy-start.3) | copy-done | bytes 524312
  10.2 0.0 copy-start.5
  10.2 0.8 %copy-done.5 = f32[2,512,128]{2,1,0:T(8,128)} copy-done((f32[2,512,128]{2,1,0:T(8,128)}, f32[2,512,128]{2,1,0:T(8,128)S(1)}, u32[]{:S(2)}) %copy-start.5) | copy-done | bytes 524312
  11.0 0.4 %collective-permute-start.3 = (f32[2,2,512,128]{3,2,1,0:T(8,128)}, f32[2,2,512,128]{3,2,1,0:T(8,128)}, u32[]{:S(2)}, u32[]{:S(2)}) collective-permute-start(f32[2,2,512,128]{3,2,1,0:T(8,128)} %get-tuple-element.16), channel_id=1, source_target_pairs={{0,2},{2,0},{4,6},{6,4},{8,10},{10,8},{12,14},{14,12},{16,18},{18,... | collective-permute-start | bytes 3145736 | tf_op jit(solution)/shard_map/ppermute | solution.py:338
  11.4 0.8 %collective-permute-start.2 = (f32[2,2,512,128]{3,2,1,0:T(8,128)}, f32[2,2,512,128]{3,2,1,0:T(8,128)S(1)}, u32[]{:S(2)}, u32[]{:S(2)}) collective-permute-start(f32[2,2,512,128]{3,2,1,0:T(8,128)} %get-tuple-element.16), channel_id=1, source_target_pairs={{0,30},{1,31},{2,3},{3,2},{4,5},{5,4},{6,8},{7,9},{8,6},{9,7},{10,... | collective-permute-start | bytes 3145736 | tf_op jit(solution)/shard_map/ppermute | solution.py:339
  12.2 2.9 %collective-permute-start.4 = (f32[1,2,512,128]{3,2,1,0:T(8,128)}, f32[1,2,512,128]{3,2,1,0:T(8,128)}, u32[]{:S(2)}, u32[]{:S(2)}) collective-permute-start(f32[1,2,512,128]{3,2,1,0:T(8,128)} %get-tuple-element.15), channel_id=1, source_target_pairs={{0,2},{2,0},{4,6},{6,4},{8,10},{10,8},{12,14},{14,12},{16,18},{18,... | collective-permute-start | bytes 1572872 | tf_op jit(solution)/shard_map/ppermute | solution.py:338
  15.1 0.7 %collective-permute-start.1 = (f32[1,2,512,128]{3,2,1,0:T(8,128)}, f32[1,2,512,128]{3,2,1,0:T(8,128)S(1)}, u32[]{:S(2)}, u32[]{:S(2)}) collective-permute-start(f32[1,2,512,128]{3,2,1,0:T(8,128)} %get-tuple-element.15), channel_id=1, source_target_pairs={{0,30},{1,31},{2,3},{3,2},{4,5},{5,4},{6,8},{7,9},{8,6},{9,7},{10,... | collective-permute-start | bytes 1572872 | tf_op jit(solution)/shard_map/ppermute | solution.py:339
  15.8 0.0 copy-start.2
  15.8 0.0 copy-start.4
  15.8 0.0 copy-start.6
  15.8 1.4 %dynamic-slice_bitcast_fusion.1.high_operators = bf16[1024,512]{1,0:T(8,128)(2,1)S(1)} fusion(bf16[2,1,1024,512]{3,2,1,0:T(8,128)(2,1)} %constant.21.clone, s32[]{:T(128)S(6)} %select_n.6), kind=kLoop, calls=%fused_computation.1 | loop fusion | bytes 2097156 | tf_op jit(solution)/shard_map/squeeze | solution.py:361
  17.2 1.3 %dynamic-slice_bitcast_fusion.coarse_operators = f8e4m3fn[1024,1024]{1,0:T(32,128)(4,1)S(1)} fusion(f8e4m3fn[2,1,1024,1024]{3,2,1,0:T(32,128)(4,1)} %constant.22.clone, s32[]{:T(128)S(6)} %select_n.6), kind=kLoop, calls=%fused_computation | loop fusion | bytes 2097156 | tf_op jit(solution)/shard_map/squeeze | solution.py:361
  18.5 0.0 collective-permute-done.4.refs_1_
  18.5 0.0 collective-permute-done.3.refs_0_
  18.5 0.0 copy-done.2
  18.6 0.0 copy-done.4
  18.6 0.0 copy-done.6
  18.6 0.0 copy-start
  18.6 2.0 %near.1 = (f32[2,512,128]{2,1,0:T(8,128)S(1)}, f32[2,512,128]{2,1,0:T(8,128)S(1)}, f32[2,512,128]{2,1,0:T(8,128)S(1)}) custom-call(f32[3,2,512,128]{3,2,1,0:T(8,128)} %velocity.7, f32[2,2,512,128]{3,2,1,0:T(8,128)} %collective-permute-done.3.refs_0_, f32[1,2,512,128]{3,2,1,0:T(8,128)} %collective-permute-done.4.refs_1_, f32[2,512,128]{2,1,0:T(8,128)S(1)} %copy-done.2, ...), custom_call_target="tpu_custom_call" | custom-call | tf_op jit(solution)/shard_map/near/pallas_call | solution.py:281
  20.6 11.8 %collective-permute-done.2.piece = f32[2,2,512,128]{3,2,1,0:T(8,128)S(1)} collective-permute-done((f32[2,2,512,128]{3,2,1,0:T(8,128)}, f32[2,2,512,128]{3,2,1,0:T(8,128)S(1)}, u32[]{:S(2)}, u32[]{:S(2)}) %collective-permute-start.2) | collective-permute-done | bytes 1048608 | tf_op jit(solution)/shard_map/ppermute | solution.py:339
  32.5 0.0 copy-done
  32.5 1.3 %middle.1 = (f32[2,512,128]{2,1,0:T(8,128)S(1)}, f32[2,512,128]{2,1,0:T(8,128)S(1)}) custom-call(bf16[1024,512]{1,0:T(8,128)(2,1)S(1)} %dynamic-slice_bitcast_fusion.1.high_operators, f8e4m3fn[1024,1024]{1,0:T(32,128)(4,1)S(1)} %dynamic-slice_bitcast_fusion.coarse_operators, f32[3,2,512,128]{3,2,1,0:T(8,128)S(1)} %copy-done, ...), custom_call_target="tpu_custom_call" | custom-call | tf_op jit(solution)/shard_map/middle/pallas_call | solution.py:281
  33.8 4.0 %collective-permute-done.1.piece = f32[1,2,512,128]{3,2,1,0:T(8,128)S(1)} collective-permute-done((f32[1,2,512,128]{3,2,1,0:T(8,128)}, f32[1,2,512,128]{3,2,1,0:T(8,128)S(1)}, u32[]{:S(2)}, u32[]{:S(2)}) %collective-permute-start.1) | collective-permute-done | bytes 524320 | tf_op jit(solution)/shard_map/ppermute | solution.py:339
  37.8 0.0 collective-permute-done.whole
  37.8 2.1 %last.1 = f32[3,2,512,128]{3,2,1,0:T(8,128)} custom-call(bf16[1024,512]{1,0:T(8,128)(2,1)S(1)} %dynamic-slice_bitcast_fusion.1.high_operators, f8e4m3fn[1024,1024]{1,0:T(32,128)(4,1)S(1)} %dynamic-slice_bitcast_fusion.coarse_operators, f32[3,2,512,128]{3,2,1,0:T(8,128)S(1)} %copy-done, f32[3,2,512,128]{3,2,1,0:T(8,128)S(1)} %collective-permute-done.whole, ...), custom_call_target="tpu_custom_call" | custom-call | tf_op jit(solution)/shard_map/last/pallas_call | solution.py:281
Async XLA Ops:
  0.0 37.8 %collective-permute-start = (f32[3,2,512,128]{3,2,1,0:T(8,128)}, f32[3,2,512,128]{3,2,1,0:T(8,128)S(1)}, u32[]{:S(2)}, u32[]{:S(2)}) collective-permute-start(f32[3,2,512,128]{3,2,1,0:T(8,128)} %velocity.7), channel_id=1, source_target_pairs={{0,1},{1,0},{2,4},{3,5},{4,2},{5,3},{6,7},{7,6},{8,9},{9,8},{10,12... | collective-permute-start | bytes 4718600 | tf_op jit(solution)/shard_map/ppermute | solution.py:309
  8.6 0.8 %copy-start.1 = (f32[2,512,128]{2,1,0:T(8,128)}, f32[2,512,128]{2,1,0:T(8,128)S(1)}, u32[]{:S(2)}) copy-start(f32[2,512,128]{2,1,0:T(8,128)S(1)} %get-tuple-element.17.refs_2_) | copy-start | bytes 1572868
  9.4 0.8 %copy-start.3 = (f32[2,512,128]{2,1,0:T(8,128)}, f32[2,512,128]{2,1,0:T(8,128)S(1)}, u32[]{:S(2)}) copy-start(f32[2,512,128]{2,1,0:T(8,128)S(1)} %get-tuple-element.18.refs_3_) | copy-start | bytes 1572868
  10.2 0.8 %copy-start.5 = (f32[2,512,128]{2,1,0:T(8,128)}, f32[2,512,128]{2,1,0:T(8,128)S(1)}, u32[]{:S(2)}) copy-start(f32[2,512,128]{2,1,0:T(8,128)S(1)} %get-tuple-element.19.refs_4_) | copy-start | bytes 1572868
  11.0 7.6 %collective-permute-start.3 = (f32[2,2,512,128]{3,2,1,0:T(8,128)}, f32[2,2,512,128]{3,2,1,0:T(8,128)}, u32[]{:S(2)}, u32[]{:S(2)}) collective-permute-start(f32[2,2,512,128]{3,2,1,0:T(8,128)} %get-tuple-element.16), channel_id=1, source_target_pairs={{0,2},{2,0},{4,6},{6,4},{8,10},{10,8},{12,14},{14,12},{16,18},{18,... | collective-permute-start | bytes 3145736 | tf_op jit(solution)/shard_map/ppermute | solution.py:338
  11.4 21.1 %collective-permute-start.2 = (f32[2,2,512,128]{3,2,1,0:T(8,128)}, f32[2,2,512,128]{3,2,1,0:T(8,128)S(1)}, u32[]{:S(2)}, u32[]{:S(2)}) collective-permute-start(f32[2,2,512,128]{3,2,1,0:T(8,128)} %get-tuple-element.16), channel_id=1, source_target_pairs={{0,30},{1,31},{2,3},{3,2},{4,5},{5,4},{6,8},{7,9},{8,6},{9,7},{10,... | collective-permute-start | bytes 3145736 | tf_op jit(solution)/shard_map/ppermute | solution.py:339
  12.2 6.3 %collective-permute-start.4 = (f32[1,2,512,128]{3,2,1,0:T(8,128)}, f32[1,2,512,128]{3,2,1,0:T(8,128)}, u32[]{:S(2)}, u32[]{:S(2)}) collective-permute-start(f32[1,2,512,128]{3,2,1,0:T(8,128)} %get-tuple-element.15), channel_id=1, source_target_pairs={{0,2},{2,0},{4,6},{6,4},{8,10},{10,8},{12,14},{14,12},{16,18},{18,... | collective-permute-start | bytes 1572872 | tf_op jit(solution)/shard_map/ppermute | solution.py:338
  15.1 22.7 %collective-permute-start.1 = (f32[1,2,512,128]{3,2,1,0:T(8,128)}, f32[1,2,512,128]{3,2,1,0:T(8,128)S(1)}, u32[]{:S(2)}, u32[]{:S(2)}) collective-permute-start(f32[1,2,512,128]{3,2,1,0:T(8,128)} %get-tuple-element.15), channel_id=1, source_target_pairs={{0,30},{1,31},{2,3},{3,2},{4,5},{5,4},{6,8},{7,9},{8,6},{9,7},{10,... | collective-permute-start | bytes 1572872 | tf_op jit(solution)/shard_map/ppermute | solution.py:339
  15.8 2.8 %copy-start.2 = (f32[2,512,128]{2,1,0:T(8,128)S(1)}, f32[2,512,128]{2,1,0:T(8,128)}, u32[]{:S(2)}) copy-start(f32[2,512,128]{2,1,0:T(8,128)} %copy-done.1) | copy-start | bytes 1572868
  15.8 2.8 %copy-start.4 = (f32[2,512,128]{2,1,0:T(8,128)S(1)}, f32[2,512,128]{2,1,0:T(8,128)}, u32[]{:S(2)}) copy-start(f32[2,512,128]{2,1,0:T(8,128)} %copy-done.3) | copy-start | bytes 1572868
  15.8 2.8 %copy-start.6 = (f32[2,512,128]{2,1,0:T(8,128)S(1)}, f32[2,512,128]{2,1,0:T(8,128)}, u32[]{:S(2)}) copy-start(f32[2,512,128]{2,1,0:T(8,128)} %copy-done.5) | copy-start | bytes 1572868
  18.6 13.9 %copy-start = (f32[3,2,512,128]{3,2,1,0:T(8,128)S(1)}, f32[3,2,512,128]{3,2,1,0:T(8,128)}, u32[]{:S(2)}) copy-start(f32[3,2,512,128]{3,2,1,0:T(8,128)} %velocity.7) | copy-start | bytes 4718596

commit v6 on v5

--- a/solution.py
+++ b/solution.py
@@ -95,8 +95,7 @@
     return added[:, : v.shape[2]], added[:, v.shape[2] :]
 
 
-def wall_there(undo, high_operators, coarse_operators, fields, v):
-    rows = v.shape[1]
+def parted_field(fields):
     side = jnp.concatenate([fields[0], fields[1]], axis=1)
     high = side.astype(jnp.bfloat16)
     low = side - high.astype(jnp.float32)
@@ -107,13 +106,25 @@
         ],
         axis=0,
     )
+    return high, coarse
+
+
+def wall_rows(undo, operators, field, v, start, count):
+    rows = v.shape[1]
     dot = functools.partial(jnp.dot, preferred_element_type=jnp.float32)
-    product = dot(high_operators[...], high)
-    rest = dot(coarse_operators[...], coarse)
-    first = product[:rows] + undo[0] * rest[:rows]
-    second = product[rows:] + undo[1] * rest[rows:]
-    added = second - jnp.concatenate([v[0], v[1]], axis=1) * first
+    sums = []
+    for matrix in range(2):
+        at = pl.ds(matrix * rows + start, count)
+        products = [dot(operator[at], part) for operator, part in zip(operators, field)]
+        sums.append(products[0] + undo[matrix] * products[1])
+    at = pl.ds(start, count)
+    added = sums[1] - jnp.concatenate([v[0, at], v[1, at]], axis=1) * sums[0]
     return added[:, : v.shape[2]], added[:, v.shape[2] :]
+
+
+def wall_there(undo, high_operators, coarse_operators, fields, v):
+    operators = (high_operators, coarse_operators)
+    return wall_rows(undo, operators, parted_field(fields), v, 0, v.shape[1])
 
 
 def along_x(parity):
@@ -210,7 +221,7 @@
 
 def remote_kernel(undo, high_operators, coarse_operators, velocity, others, *refs):
     for q in range(3):
-        terms = wall_there(undo, high_operators, coarse_operators, others[q], velocity[1])
+        terms = wall_there(undo, high_operators, coarse_operators, others[q], velocity.at[1])
         add(refs[q], refs[3 + q], *enumerate(terms))
 
 
@@ -221,7 +232,7 @@
     @pl.when(swapped)
     def _():
         for i, (base, out) in enumerate(zip(bases, outs)):
-            terms = wall_there(undo, high_operators, coarse_operators, piece[i], velocity[1])
+            terms = wall_there(undo, high_operators, coarse_operators, piece[i], velocity.at[1])
             add(base, out, *enumerate(terms))
 
     @pl.when(jnp.logical_not(swapped))
@@ -231,34 +242,52 @@
             add(base, out, *terms(piece.at[i]))
 
 
-def last_kernel(undo, high_operators, coarse_operators, velocity, whole, piece, *refs):
+def first_kernel(undo, high_operators, coarse_operators, velocity, whole, *refs):
+    bases, outs = refs[:3], refs[3:]
+    swapped = far_first(lax.axis_index("gx"))
+
+    @pl.when(swapped)
+    def _():
+        terms = far_terms(velocity.at[0])
+        for q in range(3):
+            add(bases[q], outs[q], *terms(whole.at[q]))
+
+    @pl.when(jnp.logical_not(swapped))
+    def _():
+        for q in range(3):
+            terms = wall_there(undo, high_operators, coarse_operators, whole[q], velocity.at[1])
+            add(bases[q], outs[q], *enumerate(terms))
+
+
+def last_kernel(undo, high_operators, coarse_operators, velocity, piece, *refs):
     bases, (out, total, sent) = refs[:3], refs[3:]
     swapped = far_first(lax.axis_index("gx"))
-    rest = PIECES[-1]
-    stores = [pltpu.make_async_copy(total.at[q], out.at[q], sent.at[q]) for q in range(3)]
+    (last,) = PIECES[-1]
+    operators = (high_operators, coarse_operators)
+    half = velocity.shape[2] // 2
+    ready = [q for q in range(3) if q != last]
+    stores = [pltpu.make_async_copy(bases[q], out.at[q], sent.at[q]) for q in ready]
+    for store in stores:
+        store.start()
+    for i in range(2):
+        at = pl.ds(i * half, half)
+        stores.append(pltpu.make_async_copy(total.at[:, at], out.at[last, :, at], sent.at[3 + i]))
 
     @pl.when(swapped)
     def _():
-        terms = far_terms(velocity.at[0])
-        for q in range(3):
-            out = total.at[q]
-            add(bases[q], out, *terms(whole.at[q]))
-            if q in rest:
-                field = piece[rest.index(q)]
-                more = wall_there(undo, high_operators, coarse_operators, field, velocity[1])
-                add(out, out, *enumerate(more))
-            stores[q].start()
+        field = parted_field(piece[0])
+        for i in range(2):
+            at = pl.ds(i * half, half)
+            more = wall_rows(undo, operators, field, velocity.at[1], i * half, half)
+            for plane in range(2):
+                total[plane, at] = bases[last][plane, at] + more[plane]
+            stores[2 + i].start()
 
     @pl.when(jnp.logical_not(swapped))
     def _():
-        terms = far_terms(velocity.at[0])
-        for q in range(3):
-            out = total.at[q]
-            more = wall_there(undo, high_operators, coarse_operators, whole[q], velocity[1])
-            add(bases[q], out, *enumerate(more))
-            if q in rest:
-                add(out, out, *terms(piece.at[rest.index(q)]))
-            stores[q].start()
+        add(bases[last], total, *far_terms(velocity.at[0])(piece.at[0]))
+        for i in range(2):
+            stores[2 + i].start()
 
     for store in stores:
         store.wait()
@@ -369,14 +398,21 @@
         )
         for q, total in zip(c, added):
             totals[q] = total
+    totals = call(
+        functools.partial(first_kernel, undo),
+        (*fixed, vmem(first), *totals),
+        [VMEM] * 7,
+        (one,) * 3,
+        "first",
+    )
     return call(
         functools.partial(last_kernel, undo),
-        (*fixed, vmem(first), vmem(second[-1]), *totals),
-        [VMEM] * 8,
+        (*fixed, vmem(second[-1]), *totals),
+        [VMEM] * 7,
         whole,
         "last",
         out_specs=ANY,
-        scratch_shapes=[pltpu.VMEM(shape, jnp.float32), pltpu.SemaphoreType.DMA((3,))],
+        scratch_shapes=[pltpu.VMEM(shape[1:], jnp.float32), pltpu.SemaphoreType.DMA((5,))],
     )
 
 

time: 40.1 us -> 39.8 us (level)
    ppermute x2, waiting for transfers between devices: 15.8 us -> 11.8 us  [shards(): second = [lax.ppermute(part, both, seconds) for part in totals[3:]]]
    ppermute x1, waiting for transfers between devices: 0.01 us -> 3.99 us  [shards(): first = lax.ppermute(velocity, both, firsts)]
    pallas_call x4 -> x5, Pallas kernels: 11.4 us -> 11.1 us  [call(): pl.pallas_call(kernel, in_specs=in_specs, out_shape=out_shape, compiler_p...]
  transfers between devices with their start and end apart: 5 -> 5, of which waited for: 2 -> 2; matrix products, arithmetic and copies ran while one was open for 7% -> 7% of each run, Pallas kernels for 23% -> 24%
where the time goes in v6:
time: 39.8 us; the launch traced here: 39.6 us
  waiting for transfers between devices  15.8 us (40%)
  Pallas kernels  11.1 us (28%)
  starting transfers between devices  7.39 us (19%)
  local copies, waits for them, and re-layouts  5.17 us (13%)
    ppermute x2, waiting for transfers between devices, shards(): second = [lax.ppermute(part, both, seconds) for part in totals[3:]]  11.8 us
    pallas_call x5, Pallas kernels, call(): pl.pallas_call(kernel, in_specs=in_specs, out_shape=out_shape, compiler_p...  11.1 us
    ppermute x1, waiting for transfers between devices, shards(): first = lax.ppermute(velocity, both, firsts)  3.99 us
    ppermute x2, starting transfers between devices, shards(): near = [lax.ppermute(part, 'gx', inward) for part in totals[3:]]  3.3 us
    squeeze x2, local copies, waits for them, and re-layouts, shards(): fixed = (vmem(high[0]), vmem(coarse[0]), vmem(velocity))  2.74 us
    ppermute x1, starting transfers between devices, shards(): first = lax.ppermute(velocity, both, firsts)  2.6 us
    unnamed x14, local copies, waits for them, and re-layouts  2.43 us
    ppermute x2, starting transfers between devices, shards(): second = [lax.ppermute(part, both, seconds) for part in totals[3:]]  1.49 us
  transfers between devices with their start and end apart: 5, of which 2 were waited for; matrix products, arithmetic and copies ran while one was open for 7% of the time, Pallas kernels for 24%

profile of v6, /device:TPU:1, one launch (start us, length us, event | category | flops | bytes accessed | tf_op | source)
XLA Modules:
  0.0 39.6 jit_solution(1155171106140871295)
XLA Ops:
  0.0 2.6 %collective-permute-start.1 = (f32[3,2,512,128]{3,2,1,0:T(8,128)}, f32[3,2,512,128]{3,2,1,0:T(8,128)S(1)}, u32[]{:S(2)}, u32[]{:S(2)}) collective-permute-start(f32[3,2,512,128]{3,2,1,0:T(8,128)} %velocity.9), channel_id=1, source_target_pairs={{0,1},{1,0},{2,4},{3,5},{4,2},{5,3},{6,7},{7,6},{8,9},{9,8},{10,12... | collective-permute-start | bytes 4718600 | tf_op jit(solution)/shard_map/ppermute | solution.py:338
  2.6 6.0 %local.1 = (f32[2,512,128]{2,1,0:T(8,128)S(1)}, f32[2,512,128]{2,1,0:T(8,128)S(1)}, f32[2,512,128]{2,1,0:T(8,128)S(1)}, f32[2,2,512,128]{3,2,1,0:T(8,128)}, f32[1,2,512,128]{3,2,1,0:T(8,128)}) custom-call(bf16[2,2,1024,512]{3,2,1,0:T(8,128)(2,1)} %constant.20.clone.blocks, f32[3,2,512,128]{3,2,1,0:T(8,128)} %velocity.9, f32[3,2,512,128]{3,2,1,0:T(8,128)} %previous.1), custom_call_target="tpu_custom_call" | custom-call | tf_op jit(solution)/shard_map/local/pallas_call | solution.py:310
  8.6 0.0 copy-start.1
  8.6 0.8 %copy-done.1 = f32[2,512,128]{2,1,0:T(8,128)} copy-done((f32[2,512,128]{2,1,0:T(8,128)}, f32[2,512,128]{2,1,0:T(8,128)S(1)}, u32[]{:S(2)}) %copy-start.1) | copy-done | bytes 524312
  9.4 0.0 copy-start.3
  9.4 0.8 %copy-done.3 = f32[2,512,128]{2,1,0:T(8,128)} copy-done((f32[2,512,128]{2,1,0:T(8,128)}, f32[2,512,128]{2,1,0:T(8,128)S(1)}, u32[]{:S(2)}) %copy-start.3) | copy-done | bytes 524312
  10.2 0.0 copy-start.5
  10.2 0.8 %copy-done.5 = f32[2,512,128]{2,1,0:T(8,128)} copy-done((f32[2,512,128]{2,1,0:T(8,128)}, f32[2,512,128]{2,1,0:T(8,128)S(1)}, u32[]{:S(2)}) %copy-start.5) | copy-done | bytes 524312
  11.0 0.4 %collective-permute-start.3 = (f32[2,2,512,128]{3,2,1,0:T(8,128)}, f32[2,2,512,128]{3,2,1,0:T(8,128)}, u32[]{:S(2)}, u32[]{:S(2)}) collective-permute-start(f32[2,2,512,128]{3,2,1,0:T(8,128)} %get-tuple-element.19), channel_id=1, source_target_pairs={{0,2},{2,0},{4,6},{6,4},{8,10},{10,8},{12,14},{14,12},{16,18},{18,... | collective-permute-start | bytes 3145736 | tf_op jit(solution)/shard_map/ppermute | solution.py:367
  11.4 0.8 %collective-permute-start.2 = (f32[2,2,512,128]{3,2,1,0:T(8,128)}, f32[2,2,512,128]{3,2,1,0:T(8,128)S(1)}, u32[]{:S(2)}, u32[]{:S(2)}) collective-permute-start(f32[2,2,512,128]{3,2,1,0:T(8,128)} %get-tuple-element.19), channel_id=1, source_target_pairs={{0,30},{1,31},{2,3},{3,2},{4,5},{5,4},{6,8},{7,9},{8,6},{9,7},{10,... | collective-permute-start | bytes 3145736 | tf_op jit(solution)/shard_map/ppermute | solution.py:368
  12.2 2.9 %collective-permute-start.4 = (f32[1,2,512,128]{3,2,1,0:T(8,128)}, f32[1,2,512,128]{3,2,1,0:T(8,128)}, u32[]{:S(2)}, u32[]{:S(2)}) collective-permute-start(f32[1,2,512,128]{3,2,1,0:T(8,128)} %get-tuple-element.18), channel_id=1, source_target_pairs={{0,2},{2,0},{4,6},{6,4},{8,10},{10,8},{12,14},{14,12},{16,18},{18,... | collective-permute-start | bytes 1572872 | tf_op jit(solution)/shard_map/ppermute | solution.py:367
  15.1 0.7 %collective-permute-start = (f32[1,2,512,128]{3,2,1,0:T(8,128)}, f32[1,2,512,128]{3,2,1,0:T(8,128)S(1)}, u32[]{:S(2)}, u32[]{:S(2)}) collective-permute-start(f32[1,2,512,128]{3,2,1,0:T(8,128)} %get-tuple-element.18), channel_id=1, source_target_pairs={{0,30},{1,31},{2,3},{3,2},{4,5},{5,4},{6,8},{7,9},{8,6},{9,7},{10,... | collective-permute-start | bytes 1572872 | tf_op jit(solution)/shard_map/ppermute | solution.py:368
  15.8 0.0 copy-start.2
  15.8 0.0 copy-start.4
  15.8 0.0 copy-start.6
  15.8 1.4 %dynamic-slice_bitcast_fusion.1.high_operators = bf16[1024,512]{1,0:T(8,128)(2,1)S(1)} fusion(bf16[2,1,1024,512]{3,2,1,0:T(8,128)(2,1)} %constant.21.clone, s32[]{:T(128)S(6)} %select_n.6), kind=kLoop, calls=%fused_computation.1 | loop fusion | bytes 2097156 | tf_op jit(solution)/shard_map/squeeze | solution.py:390
  17.2 1.3 %dynamic-slice_bitcast_fusion.coarse_operators = f8e4m3fn[1024,1024]{1,0:T(32,128)(4,1)S(1)} fusion(f8e4m3fn[2,1,1024,1024]{3,2,1,0:T(32,128)(4,1)} %constant.22.clone, s32[]{:T(128)S(6)} %select_n.6), kind=kLoop, calls=%fused_computation | loop fusion | bytes 2097156 | tf_op jit(solution)/shard_map/squeeze | solution.py:390
  18.5 0.0 collective-permute-done.4.refs_1_
  18.6 0.0 collective-permute-done.3.refs_0_
  18.6 0.0 copy-done.2
  18.6 0.0 copy-done.4
  18.6 0.0 copy-done.6
  18.6 0.0 copy-start
  18.6 2.0 %near.1 = (f32[2,512,128]{2,1,0:T(8,128)S(1)}, f32[2,512,128]{2,1,0:T(8,128)S(1)}, f32[2,512,128]{2,1,0:T(8,128)S(1)}) custom-call(f32[3,2,512,128]{3,2,1,0:T(8,128)} %velocity.9, f32[2,2,512,128]{3,2,1,0:T(8,128)} %collective-permute-done.3.refs_0_, f32[1,2,512,128]{3,2,1,0:T(8,128)} %collective-permute-done.4.refs_1_, f32[2,512,128]{2,1,0:T(8,128)S(1)} %copy-done.2, ...), custom_call_target="tpu_custom_call" | custom-call | tf_op jit(solution)/shard_map/near/pallas_call | solution.py:310
  20.7 11.8 %collective-permute-done.2.piece = f32[2,2,512,128]{3,2,1,0:T(8,128)S(1)} collective-permute-done((f32[2,2,512,128]{3,2,1,0:T(8,128)}, f32[2,2,512,128]{3,2,1,0:T(8,128)S(1)}, u32[]{:S(2)}, u32[]{:S(2)}) %collective-permute-start.2) | collective-permute-done | bytes 1048608 | tf_op jit(solution)/shard_map/ppermute | solution.py:368
  32.5 0.0 copy-done
  32.5 1.3 %middle.1 = (f32[2,512,128]{2,1,0:T(8,128)S(1)}, f32[2,512,128]{2,1,0:T(8,128)S(1)}) custom-call(bf16[1024,512]{1,0:T(8,128)(2,1)S(1)} %dynamic-slice_bitcast_fusion.1.high_operators, f8e4m3fn[1024,1024]{1,0:T(32,128)(4,1)S(1)} %dynamic-slice_bitcast_fusion.coarse_operators, f32[3,2,512,128]{3,2,1,0:T(8,128)S(1)} %copy-done, ...), custom_call_target="tpu_custom_call" | custom-call | tf_op jit(solution)/shard_map/middle/pallas_call | solution.py:310
  33.8 4.0 %collective-permute-done.1.whole = f32[3,2,512,128]{3,2,1,0:T(8,128)S(1)} collective-permute-done((f32[3,2,512,128]{3,2,1,0:T(8,128)}, f32[3,2,512,128]{3,2,1,0:T(8,128)S(1)}, u32[]{:S(2)}, u32[]{:S(2)}) %collective-permute-start.1) | collective-permute-done | bytes 1572896 | tf_op jit(solution)/shard_map/ppermute | solution.py:338
  37.8 0.3 first.1
  38.1 0.0 collective-permute-done.piece
  38.1 1.5 %last.1 = f32[3,2,512,128]{3,2,1,0:T(8,128)} custom-call(bf16[1024,512]{1,0:T(8,128)(2,1)S(1)} %dynamic-slice_bitcast_fusion.1.high_operators, f8e4m3fn[1024,1024]{1,0:T(32,128)(4,1)S(1)} %dynamic-slice_bitcast_fusion.coarse_operators, f32[3,2,512,128]{3,2,1,0:T(8,128)S(1)} %copy-done, f32[1,2,512,128]{3,2,1,0:T(8,128)S(1)} %collective-permute-done.piece, ...), custom_call_target="tpu_custom_call" | custom-call | tf_op jit(solution)/shard_map/last/pallas_call | solution.py:310
Async XLA Ops:
  0.0 37.8 %collective-permute-start.1 = (f32[3,2,512,128]{3,2,1,0:T(8,128)}, f32[3,2,512,128]{3,2,1,0:T(8,128)S(1)}, u32[]{:S(2)}, u32[]{:S(2)}) collective-permute-start(f32[3,2,512,128]{3,2,1,0:T(8,128)} %velocity.9), channel_id=1, source_target_pairs={{0,1},{1,0},{2,4},{3,5},{4,2},{5,3},{6,7},{7,6},{8,9},{9,8},{10,12... | collective-permute-start | bytes 4718600 | tf_op jit(solution)/shard_map/ppermute | solution.py:338
  8.6 0.8 %copy-start.1 = (f32[2,512,128]{2,1,0:T(8,128)}, f32[2,512,128]{2,1,0:T(8,128)S(1)}, u32[]{:S(2)}) copy-start(f32[2,512,128]{2,1,0:T(8,128)S(1)} %get-tuple-element.20.refs_2_) | copy-start | bytes 1572868
  9.4 0.8 %copy-start.3 = (f32[2,512,128]{2,1,0:T(8,128)}, f32[2,512,128]{2,1,0:T(8,128)S(1)}, u32[]{:S(2)}) copy-start(f32[2,512,128]{2,1,0:T(8,128)S(1)} %get-tuple-element.21.refs_3_) | copy-start | bytes 1572868
  10.2 0.8 %copy-start.5 = (f32[2,512,128]{2,1,0:T(8,128)}, f32[2,512,128]{2,1,0:T(8,128)S(1)}, u32[]{:S(2)}) copy-start(f32[2,512,128]{2,1,0:T(8,128)S(1)} %get-tuple-element.22.refs_4_) | copy-start | bytes 1572868
  11.0 7.6 %collective-permute-start.3 = (f32[2,2,512,128]{3,2,1,0:T(8,128)}, f32[2,2,512,128]{3,2,1,0:T(8,128)}, u32[]{:S(2)}, u32[]{:S(2)}) collective-permute-start(f32[2,2,512,128]{3,2,1,0:T(8,128)} %get-tuple-element.19), channel_id=1, source_target_pairs={{0,2},{2,0},{4,6},{6,4},{8,10},{10,8},{12,14},{14,12},{16,18},{18,... | collective-permute-start | bytes 3145736 | tf_op jit(solution)/shard_map/ppermute | solution.py:367
  11.4 21.1 %collective-permute-start.2 = (f32[2,2,512,128]{3,2,1,0:T(8,128)}, f32[2,2,512,128]{3,2,1,0:T(8,128)S(1)}, u32[]{:S(2)}, u32[]{:S(2)}) collective-permute-start(f32[2,2,512,128]{3,2,1,0:T(8,128)} %get-tuple-element.19), channel_id=1, source_target_pairs={{0,30},{1,31},{2,3},{3,2},{4,5},{5,4},{6,8},{7,9},{8,6},{9,7},{10,... | collective-permute-start | bytes 3145736 | tf_op jit(solution)/shard_map/ppermute | solution.py:368
  12.2 6.3 %collective-permute-start.4 = (f32[1,2,512,128]{3,2,1,0:T(8,128)}, f32[1,2,512,128]{3,2,1,0:T(8,128)}, u32[]{:S(2)}, u32[]{:S(2)}) collective-permute-start(f32[1,2,512,128]{3,2,1,0:T(8,128)} %get-tuple-element.18), channel_id=1, source_target_pairs={{0,2},{2,0},{4,6},{6,4},{8,10},{10,8},{12,14},{14,12},{16,18},{18,... | collective-permute-start | bytes 1572872 | tf_op jit(solution)/shard_map/ppermute | solution.py:367
  15.1 23.0 %collective-permute-start = (f32[1,2,512,128]{3,2,1,0:T(8,128)}, f32[1,2,512,128]{3,2,1,0:T(8,128)S(1)}, u32[]{:S(2)}, u32[]{:S(2)}) collective-permute-start(f32[1,2,512,128]{3,2,1,0:T(8,128)} %get-tuple-element.18), channel_id=1, source_target_pairs={{0,30},{1,31},{2,3},{3,2},{4,5},{5,4},{6,8},{7,9},{8,6},{9,7},{10,... | collective-permute-start | bytes 1572872 | tf_op jit(solution)/shard_map/ppermute | solution.py:368
  15.8 2.8 %copy-start.2 = (f32[2,512,128]{2,1,0:T(8,128)S(1)}, f32[2,512,128]{2,1,0:T(8,128)}, u32[]{:S(2)}) copy-start(f32[2,512,128]{2,1,0:T(8,128)} %copy-done.1) | copy-start | bytes 1572868
  15.8 2.8 %copy-start.4 = (f32[2,512,128]{2,1,0:T(8,128)S(1)}, f32[2,512,128]{2,1,0:T(8,128)}, u32[]{:S(2)}) copy-start(f32[2,512,128]{2,1,0:T(8,128)} %copy-done.3) | copy-start | bytes 1572868
  15.8 2.8 %copy-start.6 = (f32[2,512,128]{2,1,0:T(8,128)S(1)}, f32[2,512,128]{2,1,0:T(8,128)}, u32[]{:S(2)}) copy-start(f32[2,512,128]{2,1,0:T(8,128)} %copy-done.5) | copy-start | bytes 1572868
  18.6 13.9 %copy-start = (f32[3,2,512,128]{3,2,1,0:T(8,128)S(1)}, f32[3,2,512,128]{3,2,1,0:T(8,128)}, u32[]{:S(2)}) copy-start(f32[3,2,512,128]{3,2,1,0:T(8,128)} %velocity.9) | copy-start | bytes 4718596

commit v7 on v6

--- a/solution.py
+++ b/solution.py
@@ -27,6 +27,7 @@
 
 VMEM_LIMIT = 24 * 1024 * 1024
 PIECES = ((0, 1), (2,))
+LAST = 2
 COARSE_LARGEST = 224.0
 COARSE_LIFT = 32.0
 LOW_LIFT = 512.0
@@ -95,45 +96,51 @@
     return added[:, : v.shape[2]], added[:, v.shape[2] :]
 
 
+def second_pieces(rows):
+    early = rows * 3 // 4 if rows % 512 == 0 else rows
+    pieces = [((0, 1), 0, rows), ((LAST,), 0, early), ((LAST,), early, rows - early)]
+    return [piece for piece in pieces if piece[2]]
+
+
 def parted_field(fields):
     side = jnp.concatenate([fields[0], fields[1]], axis=1)
     high = side.astype(jnp.bfloat16)
     low = side - high.astype(jnp.float32)
-    coarse = jnp.concatenate(
-        [
-            (COARSE_LIFT * side).astype(jnp.float8_e4m3fn),
-            (LOW_LIFT * COARSE_LIFT * low).astype(jnp.float8_e4m3fn),
-        ],
-        axis=0,
-    )
-    return high, coarse
-
-
-def wall_rows(undo, operators, field, v, start, count):
+    values = (COARSE_LIFT * side).astype(jnp.float8_e4m3fn)
+    return high, values, (LOW_LIFT * COARSE_LIFT * low).astype(jnp.float8_e4m3fn)
+
+
+def wall_rows(undo, operators, field, v, start, count, begin=0):
     rows = v.shape[1]
+    (high_operators, coarse_operators), (high, values, lows) = operators, field
+    depth = high.shape[0]
     dot = functools.partial(jnp.dot, preferred_element_type=jnp.float32)
     sums = []
     for matrix in range(2):
         at = pl.ds(matrix * rows + start, count)
-        products = [dot(operator[at], part) for operator, part in zip(operators, field)]
-        sums.append(products[0] + undo[matrix] * products[1])
+        product = dot(high_operators[at, begin : begin + depth], high)
+        if depth == rows:
+            rest = dot(coarse_operators[at], jnp.concatenate([values, lows], axis=0))
+        else:
+            rest = dot(coarse_operators[at, begin : begin + depth], values)
+            rest += dot(coarse_operators[at, rows + begin : rows + begin + depth], lows)
+        sums.append(product + undo[matrix] * rest)
     at = pl.ds(start, count)
     added = sums[1] - jnp.concatenate([v[0, at], v[1, at]], axis=1) * sums[0]
     return added[:, : v.shape[2]], added[:, v.shape[2] :]
 
 
-def wall_there(undo, high_operators, coarse_operators, fields, v):
+def wall_there(undo, high_operators, coarse_operators, fields, v, begin=0):
     operators = (high_operators, coarse_operators)
-    return wall_rows(undo, operators, parted_field(fields), v, 0, v.shape[1])
+    return wall_rows(undo, operators, parted_field(fields), v, 0, v.shape[1], begin)
 
 
 def along_x(parity):
     return jnp.where(parity == 0, X_FIRST, -X_FIRST).astype(jnp.float32)
 
 
-def local_kernel(blocks, velocity, previous, *refs):
-    outs, parted = refs[:3], refs[3 : 3 + len(PIECES)]
-    own, past, operators, came, sent = refs[3 + len(PIECES) :]
+def local_kernel(cuts, blocks, velocity, previous, *refs):
+    outs, parted, (own, past, operators, came, sent) = refs[:3], refs[3:-5], refs[-5:]
     me = lax.axis_index("gy")
     fetches = [
         pltpu.make_async_copy(velocity, own, came.at[0]),
@@ -144,8 +151,8 @@
         fetch.start()
     fetches[0].wait()
     stores = [
-        pltpu.make_async_copy(own.at[c[0] : c[-1] + 1], part, sent.at[i])
-        for i, (c, part) in enumerate(zip(PIECES, parted))
+        pltpu.make_async_copy(own.at[c[0] : c[-1] + 1, :, pl.ds(begin, count)], part, sent.at[i])
+        for i, ((c, begin, count), part) in enumerate(zip(cuts, parted))
     ]
     for store in stores:
         store.start()
@@ -225,21 +232,26 @@
         add(refs[q], refs[3 + q], *enumerate(terms))
 
 
-def middle_kernel(undo, high_operators, coarse_operators, velocity, piece, *refs):
-    bases, outs = refs[: len(refs) // 2], refs[len(refs) // 2 :]
+def middle_kernel(undo, begin, count, high_operators, coarse_operators, velocity, piece, *refs):
+    bases, outs = refs[:count], refs[-count:]
     swapped = far_first(lax.axis_index("gx"))
+    at = pl.ds(begin, piece.shape[2])
 
     @pl.when(swapped)
     def _():
         for i, (base, out) in enumerate(zip(bases, outs)):
-            terms = wall_there(undo, high_operators, coarse_operators, piece[i], velocity.at[1])
+            terms = wall_there(
+                undo, high_operators, coarse_operators, piece[i], velocity.at[1], begin
+            )
             add(base, out, *enumerate(terms))
 
     @pl.when(jnp.logical_not(swapped))
     def _():
-        terms = far_terms(velocity.at[0])
+        terms = far_terms(velocity.at[0, :, at])
         for i, (base, out) in enumerate(zip(bases, outs)):
-            add(base, out, *terms(piece.at[i]))
+            if piece.shape[2] < out.shape[1]:
+                out[...] = base[...]
+            add(base.at[:, at], out.at[:, at], *terms(piece.at[i]))
 
 
 def first_kernel(undo, high_operators, coarse_operators, velocity, whole, *refs):
@@ -259,33 +271,35 @@
             add(bases[q], outs[q], *enumerate(terms))
 
 
-def last_kernel(undo, high_operators, coarse_operators, velocity, piece, *refs):
+def last_kernel(undo, begin, high_operators, coarse_operators, velocity, piece, *refs):
     bases, (out, total, sent) = refs[:3], refs[3:]
     swapped = far_first(lax.axis_index("gx"))
-    (last,) = PIECES[-1]
     operators = (high_operators, coarse_operators)
     half = velocity.shape[2] // 2
-    ready = [q for q in range(3) if q != last]
+    ready = [q for q in range(3) if q != LAST]
     stores = [pltpu.make_async_copy(bases[q], out.at[q], sent.at[q]) for q in ready]
     for store in stores:
         store.start()
     for i in range(2):
         at = pl.ds(i * half, half)
-        stores.append(pltpu.make_async_copy(total.at[:, at], out.at[last, :, at], sent.at[3 + i]))
+        stores.append(pltpu.make_async_copy(total.at[:, at], out.at[LAST, :, at], sent.at[3 + i]))
 
     @pl.when(swapped)
     def _():
         field = parted_field(piece[0])
         for i in range(2):
             at = pl.ds(i * half, half)
-            more = wall_rows(undo, operators, field, velocity.at[1], i * half, half)
+            more = wall_rows(undo, operators, field, velocity.at[1], i * half, half, begin)
             for plane in range(2):
-                total[plane, at] = bases[last][plane, at] + more[plane]
+                total[plane, at] = bases[LAST][plane, at] + more[plane]
             stores[2 + i].start()
 
     @pl.when(jnp.logical_not(swapped))
     def _():
-        add(bases[last], total, *far_terms(velocity.at[0])(piece.at[0]))
+        at = pl.ds(begin, piece.shape[2])
+        total[...] = bases[LAST][...]
+        terms = far_terms(velocity.at[0, :, at])
+        add(bases[LAST].at[:, at], total.at[:, at], *terms(piece.at[0]))
         for i in range(2):
             stores[2 + i].start()
 
@@ -348,27 +362,33 @@
 
     one = jax.ShapeDtypeStruct(shape[1:], jnp.float32)
     whole = jax.ShapeDtypeStruct(shape, jnp.float32)
-    totals = call(
-        local_kernel,
+    pieces = second_pieces(rows)
+    cuts = [(c, 0, rows) for c in PIECES]
+    cuts += [piece for piece in pieces if piece not in cuts]
+    made = call(
+        functools.partial(local_kernel, cuts),
         (hbm(own), hbm(velocity), hbm(previous)),
         [ANY] * 3,
         (one,) * 3
-        + tuple(jax.ShapeDtypeStruct((len(c),) + shape[1:], jnp.float32) for c in PIECES),
+        + tuple(
+            jax.ShapeDtypeStruct((len(c), shape[1], n, shape[3]), jnp.float32) for c, _, n in cuts
+        ),
         "local",
-        out_specs=(VMEM,) * 3 + (ANY,) * len(PIECES),
+        out_specs=(VMEM,) * 3 + (ANY,) * len(cuts),
         scratch_shapes=[
             pltpu.VMEM(shape, jnp.float32),
             pltpu.VMEM(shape, jnp.float32),
             pltpu.VMEM(own.shape[1:], jnp.bfloat16),
             pltpu.SemaphoreType.DMA((3,)),
-            pltpu.SemaphoreType.DMA((len(PIECES),)),
+            pltpu.SemaphoreType.DMA((len(cuts),)),
         ],
     )
-    near = [lax.ppermute(part, "gx", inward) for part in totals[3:]]
-    second = [lax.ppermute(part, both, seconds) for part in totals[3:]]
+    totals, parted = made[:3], made[3:]
+    near = [lax.ppermute(part, "gx", inward) for part in parted[: len(PIECES)]]
+    second = [lax.ppermute(parted[cuts.index(piece)], both, seconds) for piece in pieces]
     totals = call(
         near_kernel,
-        (hbm(velocity), *map(hbm, near), *totals[:3]),
+        (hbm(velocity), *map(hbm, near), *totals),
         [ANY] * (1 + len(PIECES)) + [VMEM] * 3,
         (one,) * 3,
         "near",
@@ -388,16 +408,18 @@
         )
     totals = list(totals)
     fixed = (vmem(high[0]), vmem(coarse[0]), vmem(velocity))
-    for c, piece in zip(PIECES[:-1], second):
+    behind = ()
+    for (c, begin, _), piece in zip(pieces[:-1], second):
         added = call(
-            functools.partial(middle_kernel, undo),
-            (*fixed, piece, *(totals[q] for q in c)),
-            [VMEM] * (4 + len(c)),
+            functools.partial(middle_kernel, undo, begin, len(c)),
+            (*fixed, piece, *(totals[q] for q in c), *behind),
+            [VMEM] * (4 + len(c)) + [ANY] * len(behind),
             (one,) * len(c),
             "middle",
         )
         for q, total in zip(c, added):
             totals[q] = total
+        behind = added[:1]
     totals = call(
         functools.partial(first_kernel, undo),
         (*fixed, vmem(first), *totals),
@@ -406,7 +428,7 @@
         "first",
     )
     return call(
-        functools.partial(last_kernel, undo),
+        functools.partial(last_kernel, undo, pieces[-1][1]),
         (*fixed, vmem(second[-1]), *totals),
         [VMEM] * 7,
         whole,

time: 39.8 us -> 39.5 us (level)
  waiting for transfers between devices: 15.8 us -> 14.4 us
  starting transfers between devices: 7.39 us -> 8.25 us
  Pallas kernels: 11.1 us -> 11.6 us
    ppermute x1, waiting for transfers between devices: 3.99 us -> 0.63 us  [shards(): first = lax.ppermute(velocity, both, firsts)]
    ppermute x4 -> x5, waiting for transfers between devices: 11.8 us -> 13.7 us  [the longest x3 13.7 us: shards(): lax.ppermute(parted[cuts.index(piece)], both, seconds)]
    ppermute x4 -> x5, starting transfers between devices: 4.79 us -> 5.65 us  [the longest x2 3.3 us: shards(): near = [lax.ppermute(part, 'gx', inward) for part in parted[:len(PIECES)]]]
    pallas_call x5 -> x6, Pallas kernels: 11.1 us -> 11.6 us  [call(): pl.pallas_call(kernel, in_specs=in_specs, out_shape=out_shape, compiler_p...]
  transfers between devices with their start and end apart: 5 -> 6, of which waited for: 2 -> 3; matrix products, arithmetic and copies ran while one was open for 7% -> 7% of each run, Pallas kernels for 24% -> 26%
where the time goes in v7:
time: 39.5 us; the launch traced here: 39.3 us
  waiting for transfers between devices  14.4 us (36%)
  Pallas kernels  11.6 us (29%)
  starting transfers between devices  8.25 us (21%)
  local copies, waits for them, and re-layouts  5.01 us (13%)
    ppermute x3, waiting for transfers between devices, shards(): lax.ppermute(parted[cuts.index(piece)], both, seconds)  13.7 us
    pallas_call x6, Pallas kernels, call(): pl.pallas_call(kernel, in_specs=in_specs, out_shape=out_shape, compiler_p...  11.6 us
    ppermute x2, starting transfers between devices, shards(): near = [lax.ppermute(part, 'gx', inward) for part in parted[:len(PIECES)]]  3.3 us
    squeeze x2, local copies, waits for them, and re-layouts, shards(): fixed = (vmem(high[0]), vmem(coarse[0]), vmem(velocity))  2.71 us
    ppermute x1, starting transfers between devices, shards(): first = lax.ppermute(velocity, both, firsts)  2.6 us
    ppermute x3, starting transfers between devices, shards(): lax.ppermute(parted[cuts.index(piece)], both, seconds)  2.35 us
    unnamed x14, local copies, waits for them, and re-layouts  2.29 us
  transfers between devices with their start and end apart: 6, of which 3 were waited for; matrix products, arithmetic and copies ran while one was open for 7% of the time, Pallas kernels for 26%

profile of v7, /device:TPU:1, one launch (start us, length us, event | category | flops | bytes accessed | tf_op | source)
XLA Modules:
  0.0 39.3 jit_solution(1161193232289233288)
XLA Ops:
  0.0 2.6 %collective-permute-start.1 = (f32[3,2,512,128]{3,2,1,0:T(8,128)}, f32[3,2,512,128]{3,2,1,0:T(8,128)S(1)}, u32[]{:S(2)}, u32[]{:S(2)}) collective-permute-start(f32[3,2,512,128]{3,2,1,0:T(8,128)} %velocity.11), channel_id=1, source_target_pairs={{0,1},{1,0},{2,4},{3,5},{4,2},{5,3},{6,7},{7,6},{8,9},{9,8},{10,12... | collective-permute-start | bytes 4718600 | tf_op jit(solution)/shard_map/ppermute | solution.py:352
  2.6 6.0 %local.1 = (f32[2,512,128]{2,1,0:T(8,128)S(1)}, f32[2,512,128]{2,1,0:T(8,128)S(1)}, f32[2,512,128]{2,1,0:T(8,128)S(1)}, f32[2,2,512,128]{3,2,1,0:T(8,128)}, f32[...) custom-call(bf16[2,2,1024,512]{3,2,1,0:T(8,128)(2,1)} %constant.20.clone.blocks, ...), custom_call_target="tpu_custom_call" | custom-call | tf_op jit(solution)/shard_map/local/pallas_call | solution.py:324
  8.6 0.0 copy-start.1
  8.6 0.8 %copy-done.1 = f32[2,512,128]{2,1,0:T(8,128)} copy-done((f32[2,512,128]{2,1,0:T(8,128)}, f32[2,512,128]{2,1,0:T(8,128)S(1)}, u32[]{:S(2)}) %copy-start.1) | copy-done | bytes 524312
  9.4 0.0 copy-start.3
  9.4 0.8 %copy-done.3 = f32[2,512,128]{2,1,0:T(8,128)} copy-done((f32[2,512,128]{2,1,0:T(8,128)}, f32[2,512,128]{2,1,0:T(8,128)S(1)}, u32[]{:S(2)}) %copy-start.3) | copy-done | bytes 524312
  10.2 0.0 copy-start.5
  10.2 0.6 %copy-done.5 = f32[1,2,128,128]{3,2,1,0:T(8,128)} copy-done((f32[1,2,128,128]{3,2,1,0:T(8,128)}, f32[1,2,128,128]{3,2,1,0:T(8,128)S(1)}, u32[]{:S(2)}) %copy-start.5) | copy-done | bytes 131096
  10.9 0.4 %collective-permute-start.3 = (f32[2,2,512,128]{3,2,1,0:T(8,128)}, f32[2,2,512,128]{3,2,1,0:T(8,128)}, u32[]{:S(2)}, u32[]{:S(2)}) collective-permute-start(f32[2,2,512,128]{3,2,1,0:T(8,128)} %get-tuple-element.21), channel_id=1, source_target_pairs={{0,2},{2,0},{4,6},{6,4},{8,10},{10,8},{12,14},{14,12},{16,18},{18,... | collective-permute-start | bytes 3145736 | tf_op jit(solution)/shard_map/ppermute | solution.py:387
  11.3 0.8 %collective-permute-start.2 = (f32[2,2,512,128]{3,2,1,0:T(8,128)}, f32[2,2,512,128]{3,2,1,0:T(8,128)S(1)}, u32[]{:S(2)}, u32[]{:S(2)}) collective-permute-start(f32[2,2,512,128]{3,2,1,0:T(8,128)} %get-tuple-element.21), channel_id=1, source_target_pairs={{0,30},{1,31},{2,3},{3,2},{4,5},{5,4},{6,8},{7,9},{8,6},{9,7},{10,... | collective-permute-start | bytes 3145736 | tf_op jit(solution)/shard_map/ppermute | solution.py:388
  12.1 2.9 %collective-permute-start.4 = (f32[1,2,512,128]{3,2,1,0:T(8,128)}, f32[1,2,512,128]{3,2,1,0:T(8,128)}, u32[]{:S(2)}, u32[]{:S(2)}) collective-permute-start(f32[1,2,512,128]{3,2,1,0:T(8,128)} %get-tuple-element.22), channel_id=1, source_target_pairs={{0,2},{2,0},{4,6},{6,4},{8,10},{10,8},{12,14},{14,12},{16,18},{18,... | collective-permute-start | bytes 1572872 | tf_op jit(solution)/shard_map/ppermute | solution.py:387
  15.0 0.7 %collective-permute-start.5 = (f32[1,2,384,128]{3,2,1,0:T(8,128)}, f32[1,2,384,128]{3,2,1,0:T(8,128)S(1)}, u32[]{:S(2)}, u32[]{:S(2)}) collective-permute-start(f32[1,2,384,128]{3,2,1,0:T(8,128)} %get-tuple-element.30), channel_id=1, source_target_pairs={{0,30},{1,31},{2,3},{3,2},{4,5},{5,4},{6,8},{7,9},{8,6},{9,7},{10,... | collective-permute-start | bytes 1179656 | tf_op jit(solution)/shard_map/ppermute | solution.py:388
  15.7 0.0 copy-start.6
  15.7 0.0 copy-start.2
  15.7 0.0 copy-start.4
  15.7 1.4 %dynamic-slice_bitcast_fusion.coarse_operators = f8e4m3fn[1024,1024]{1,0:T(32,128)(4,1)S(1)} fusion(f8e4m3fn[2,1,1024,1024]{3,2,1,0:T(32,128)(4,1)} %constant.22.clone, s32[]{:T(128)S(6)} %select_n.6), kind=kLoop, calls=%fused_computation | loop fusion | bytes 2097156 | tf_op jit(solution)/shard_map/squeeze | solution.py:410
  17.1 0.0 collective-permute-done.4.refs_1_
  17.1 0.0 copy-done.6
  17.1 0.9 %collective-permute-start = (f32[1,2,128,128]{3,2,1,0:T(8,128)S(1)}, f32[1,2,128,128]{3,2,1,0:T(8,128)S(1)}, u32[]{:S(2)}, u32[]{:S(2)}) collective-permute-start(f32[1,2,128,128]{3,2,1,0:T(8,128)S(1)} %copy-done.6), channel_id=1, source_target_pairs={{0,30},{1,31},{2,3},{3,2},{4,5},{5,4},{6,8},{7,9},{8,6},{9,7},{10,... | collective-permute-start | bytes 393224 | tf_op jit(solution)/shard_map/ppermute | solution.py:388
  18.0 1.3 %dynamic-slice_bitcast_fusion.1.high_operators = bf16[1024,512]{1,0:T(8,128)(2,1)S(1)} fusion(bf16[2,1,1024,512]{3,2,1,0:T(8,128)(2,1)} %constant.21.clone, s32[]{:T(128)S(6)} %select_n.6), kind=kLoop, calls=%fused_computation.1 | loop fusion | bytes 2097156 | tf_op jit(solution)/shard_map/squeeze | solution.py:410
  19.3 0.0 collective-permute-done.3.refs_0_
  19.3 0.0 copy-done.2
  19.3 0.0 copy-done.4
  19.3 0.0 copy-start
  19.3 2.0 %near.1 = (f32[2,512,128]{2,1,0:T(8,128)S(1)}, f32[2,512,128]{2,1,0:T(8,128)S(1)}, f32[2,512,128]{2,1,0:T(8,128)S(1)}) custom-call(f32[3,2,512,128]{3,2,1,0:T(8,128)} %velocity.11, f32[2,2,512,128]{3,2,1,0:T(8,128)} %collective-permute-done.3.refs_0_, f32[1,2,512,128]{3,2,1,0:T(8,128)} %collective-permute-done.4.refs_1_, ...), custom_call_target="tpu_custom_call" | custom-call | tf_op jit(solution)/shard_map/near/pallas_call | solution.py:324
  21.4 11.1 %collective-permute-done.2.piece = f32[2,2,512,128]{3,2,1,0:T(8,128)S(1)} collective-permute-done((f32[2,2,512,128]{3,2,1,0:T(8,128)}, f32[2,2,512,128]{3,2,1,0:T(8,128)S(1)}, u32[]{:S(2)}, u32[]{:S(2)}) %collective-permute-start.2) | collective-permute-done | bytes 1048608 | tf_op jit(solution)/shard_map/ppermute | solution.py:388
  32.5 0.0 copy-done
  32.5 1.3 %middle.2 = (f32[2,512,128]{2,1,0:T(8,128)S(1)}, f32[2,512,128]{2,1,0:T(8,128)S(1)}) custom-call(bf16[1024,512]{1,0:T(8,128)(2,1)S(1)} %dynamic-slice_bitcast_fusion.1.high_operators, f8e4m3fn[1024,1024]{1,0:T(32,128)(4,1)S(1)} %dynamic-slice_bitcast_fusion.coarse_operators, f32[3,2,512,128]{3,2,1,0:T(8,128)S(1)} %copy-done, ...), custom_call_target="tpu_custom_call" | custom-call | tf_op jit(solution)/shard_map/middle/pallas_call | solution.py:324
  33.8 2.6 %collective-permute-done.5.piece = f32[1,2,384,128]{3,2,1,0:T(8,128)S(1)} collective-permute-done((f32[1,2,384,128]{3,2,1,0:T(8,128)}, f32[1,2,384,128]{3,2,1,0:T(8,128)S(1)}, u32[]{:S(2)}, u32[]{:S(2)}) %collective-permute-start.5) | collective-permute-done | bytes 393248 | tf_op jit(solution)/shard_map/ppermute | solution.py:388
  36.4 0.7 %middle.3.refs_2_ = f32[2,512,128]{2,1,0:T(8,128)S(1)} custom-call(bf16[1024,512]{1,0:T(8,128)(2,1)S(1)} %dynamic-slice_bitcast_fusion.1.high_operators, f8e4m3fn[1024,1024]{1,0:T(32,128)(4,1)S(1)} %dynamic-slice_bitcast_fusion.coarse_operators, f32[3,2,512,128]{3,2,1,0:T(8,128)S(1)} %copy-done, f32[1,2,384,128]{3,2,1,0:T(8,128)S(1)} %collective-permute-done.5.piece, ...), custom_call_target="tpu_custom_call" | custom-call | tf_op jit(solution)/shard_map/middle/pallas_call | solution.py:324
  37.1 0.6 %collective-permute-done.1.whole = f32[3,2,512,128]{3,2,1,0:T(8,128)S(1)} collective-permute-done((f32[3,2,512,128]{3,2,1,0:T(8,128)}, f32[3,2,512,128]{3,2,1,0:T(8,128)S(1)}, u32[]{:S(2)}, u32[]{:S(2)}) %collective-permute-start.1) | collective-permute-done | bytes 1572896 | tf_op jit(solution)/shard_map/ppermute | solution.py:352
  37.8 0.3 first.1
  38.1 0.0 collective-permute-done.piece
  38.1 1.2 %last.1 = f32[3,2,512,128]{3,2,1,0:T(8,128)} custom-call(bf16[1024,512]{1,0:T(8,128)(2,1)S(1)} %dynamic-slice_bitcast_fusion.1.high_operators, f8e4m3fn[1024,1024]{1,0:T(32,128)(4,1)S(1)} %dynamic-slice_bitcast_fusion.coarse_operators, f32[3,2,512,128]{3,2,1,0:T(8,128)S(1)} %copy-done, f32[1,2,128,128]{3,2,1,0:T(8,128)S(1)} %collective-permute-done.piece, ...), custom_call_target="tpu_custom_call" | custom-call | tf_op jit(solution)/shard_map/last/pallas_call | solution.py:324
Async XLA Ops:
  0.0 37.8 %collective-permute-start.1 = (f32[3,2,512,128]{3,2,1,0:T(8,128)}, f32[3,2,512,128]{3,2,1,0:T(8,128)S(1)}, u32[]{:S(2)}, u32[]{:S(2)}) collective-permute-start(f32[3,2,512,128]{3,2,1,0:T(8,128)} %velocity.11), channel_id=1, source_target_pairs={{0,1},{1,0},{2,4},{3,5},{4,2},{5,3},{6,7},{7,6},{8,9},{9,8},{10,12... | collective-permute-start | bytes 4718600 | tf_op jit(solution)/shard_map/ppermute | solution.py:352
  8.6 0.8 %copy-start.1 = (f32[2,512,128]{2,1,0:T(8,128)}, f32[2,512,128]{2,1,0:T(8,128)S(1)}, u32[]{:S(2)}) copy-start(f32[2,512,128]{2,1,0:T(8,128)S(1)} %get-tuple-element.24.refs_3_) | copy-start | bytes 1572868
  9.4 0.8 %copy-start.3 = (f32[2,512,128]{2,1,0:T(8,128)}, f32[2,512,128]{2,1,0:T(8,128)S(1)}, u32[]{:S(2)}) copy-start(f32[2,512,128]{2,1,0:T(8,128)S(1)} %get-tuple-element.25.refs_4_) | copy-start | bytes 1572868
  10.2 0.6 %copy-start.5 = (f32[1,2,128,128]{3,2,1,0:T(8,128)}, f32[1,2,128,128]{3,2,1,0:T(8,128)S(1)}, u32[]{:S(2)}) copy-start(f32[1,2,128,128]{3,2,1,0:T(8,128)S(1)} %get-tuple-element.20) | copy-start | bytes 393220
  10.9 8.4 %collective-permute-start.3 = (f32[2,2,512,128]{3,2,1,0:T(8,128)}, f32[2,2,512,128]{3,2,1,0:T(8,128)}, u32[]{:S(2)}, u32[]{:S(2)}) collective-permute-start(f32[2,2,512,128]{3,2,1,0:T(8,128)} %get-tuple-element.21), channel_id=1, source_target_pairs={{0,2},{2,0},{4,6},{6,4},{8,10},{10,8},{12,14},{14,12},{16,18},{18,... | collective-permute-start | bytes 3145736 | tf_op jit(solution)/shard_map/ppermute | solution.py:387
  11.3 21.2 %collective-permute-start.2 = (f32[2,2,512,128]{3,2,1,0:T(8,128)}, f32[2,2,512,128]{3,2,1,0:T(8,128)S(1)}, u32[]{:S(2)}, u32[]{:S(2)}) collective-permute-start(f32[2,2,512,128]{3,2,1,0:T(8,128)} %get-tuple-element.21), channel_id=1, source_target_pairs={{0,30},{1,31},{2,3},{3,2},{4,5},{5,4},{6,8},{7,9},{8,6},{9,7},{10,... | collective-permute-start | bytes 3145736 | tf_op jit(solution)/shard_map/ppermute | solution.py:388
  12.1 5.0 %collective-permute-start.4 = (f32[1,2,512,128]{3,2,1,0:T(8,128)}, f32[1,2,512,128]{3,2,1,0:T(8,128)}, u32[]{:S(2)}, u32[]{:S(2)}) collective-permute-start(f32[1,2,512,128]{3,2,1,0:T(8,128)} %get-tuple-element.22), channel_id=1, source_target_pairs={{0,2},{2,0},{4,6},{6,4},{8,10},{10,8},{12,14},{14,12},{16,18},{18,... | collective-permute-start | bytes 1572872 | tf_op jit(solution)/shard_map/ppermute | solution.py:387
  15.0 21.4 %collective-permute-start.5 = (f32[1,2,384,128]{3,2,1,0:T(8,128)}, f32[1,2,384,128]{3,2,1,0:T(8,128)S(1)}, u32[]{:S(2)}, u32[]{:S(2)}) collective-permute-start(f32[1,2,384,128]{3,2,1,0:T(8,128)} %get-tuple-element.30), channel_id=1, source_target_pairs={{0,30},{1,31},{2,3},{3,2},{4,5},{5,4},{6,8},{7,9},{8,6},{9,7},{10,... | collective-permute-start | bytes 1179656 | tf_op jit(solution)/shard_map/ppermute | solution.py:388
  15.7 1.4 %copy-start.6 = (f32[1,2,128,128]{3,2,1,0:T(8,128)S(1)}, f32[1,2,128,128]{3,2,1,0:T(8,128)}, u32[]{:S(2)}) copy-start(f32[1,2,128,128]{3,2,1,0:T(8,128)} %copy-done.5) | copy-start | bytes 393220
  15.7 3.6 %copy-start.2 = (f32[2,512,128]{2,1,0:T(8,128)S(1)}, f32[2,512,128]{2,1,0:T(8,128)}, u32[]{:S(2)}) copy-start(f32[2,512,128]{2,1,0:T(8,128)} %copy-done.1) | copy-start | bytes 1572868
  15.7 3.6 %copy-start.4 = (f32[2,512,128]{2,1,0:T(8,128)S(1)}, f32[2,512,128]{2,1,0:T(8,128)}, u32[]{:S(2)}) copy-start(f32[2,512,128]{2,1,0:T(8,128)} %copy-done.3) | copy-start | bytes 1572868
  17.1 21.0 %collective-permute-start = (f32[1,2,128,128]{3,2,1,0:T(8,128)S(1)}, f32[1,2,128,128]{3,2,1,0:T(8,128)S(1)}, u32[]{:S(2)}, u32[]{:S(2)}) collective-permute-start(f32[1,2,128,128]{3,2,1,0:T(8,128)S(1)} %copy-done.6), channel_id=1, source_target_pairs={{0,30},{1,31},{2,3},{3,2},{4,5},{5,4},{6,8},{7,9},{8,6},{9,7},{10,... | collective-permute-start | bytes 393224 | tf_op jit(solution)/shard_map/ppermute | solution.py:388
  19.3 13.2 %copy-start = (f32[3,2,512,128]{3,2,1,0:T(8,128)S(1)}, f32[3,2,512,128]{3,2,1,0:T(8,128)}, u32[]{:S(2)}) copy-start(f32[3,2,512,128]{3,2,1,0:T(8,128)} %velocity.11) | copy-start | bytes 4718596

commit v8 on v7

--- a/solution.py
+++ b/solution.py
@@ -28,6 +28,7 @@
 VMEM_LIMIT = 24 * 1024 * 1024
 PIECES = ((0, 1), (2,))
 LAST = 2
+TILE = 32
 COARSE_LARGEST = 224.0
 COARSE_LIFT = 32.0
 LOW_LIFT = 512.0
@@ -260,9 +261,13 @@
 
     @pl.when(swapped)
     def _():
-        terms = far_terms(velocity.at[0])
-        for q in range(3):
-            add(bases[q], outs[q], *terms(whole.at[q]))
+        outs[LAST][...] = bases[LAST][...]
+        for start in range(0, velocity.shape[2], TILE):
+            at = pl.ds(start, TILE)
+            terms = far_terms(velocity.at[0, :, at])
+            for q in range(3):
+                if q != LAST:
+                    add(bases[q].at[:, at], outs[q].at[:, at], *terms(whole.at[q, :, at]))
 
     @pl.when(jnp.logical_not(swapped))
     def _():
@@ -271,7 +276,7 @@
             add(bases[q], outs[q], *enumerate(terms))
 
 
-def last_kernel(undo, begin, high_operators, coarse_operators, velocity, piece, *refs):
+def last_kernel(undo, begin, high_operators, coarse_operators, velocity, whole, piece, *refs):
     bases, (out, total, sent) = refs[:3], refs[3:]
     swapped = far_first(lax.axis_index("gx"))
     operators = (high_operators, coarse_operators)
@@ -289,9 +294,11 @@
         field = parted_field(piece[0])
         for i in range(2):
             at = pl.ds(i * half, half)
+            terms = far_terms(velocity.at[0, :, at])
+            add(bases[LAST].at[:, at], total.at[:, at], *terms(whole.at[LAST, :, at]))
             more = wall_rows(undo, operators, field, velocity.at[1], i * half, half, begin)
             for plane in range(2):
-                total[plane, at] = bases[LAST][plane, at] + more[plane]
+                total[plane, at] += more[plane]
             stores[2 + i].start()
 
     @pl.when(jnp.logical_not(swapped))
@@ -429,8 +436,8 @@
     )
     return call(
         functools.partial(last_kernel, undo, pieces[-1][1]),
-        (*fixed, vmem(second[-1]), *totals),
-        [VMEM] * 7,
+        (*fixed, vmem(first), vmem(second[-1]), *totals),
+        [VMEM] * 8,
         whole,
         "last",
         out_specs=ANY,

time: 39.5 us -> 39.4 us (level)
  no operation moved by 1% of the time
where the time goes in v8:
time: 39.4 us; the launch traced here: 39.3 us
  waiting for transfers between devices  14.4 us (37%)
  Pallas kernels  11.5 us (29%)
  starting transfers between devices  8.25 us (21%)
  local copies, waits for them, and re-layouts  5.01 us (13%)
    ppermute x3, waiting for transfers between devices, shards(): lax.ppermute(parted[cuts.index(piece)], both, seconds)  13.7 us
    pallas_call x6, Pallas kernels, call(): pl.pallas_call(kernel, in_specs=in_specs, out_shape=out_shape, compiler_p...  11.5 us
    ppermute x2, starting transfers between devices, shards(): near = [lax.ppermute(part, 'gx', inward) for part in parted[:len(PIECES)]]  3.3 us
    squeeze x2, local copies, waits for them, and re-layouts, shards(): fixed = (vmem(high[0]), vmem(coarse[0]), vmem(velocity))  2.71 us
    ppermute x1, starting transfers between devices, shards(): first = lax.ppermute(velocity, both, firsts)  2.6 us
    ppermute x3, starting transfers between devices, shards(): lax.ppermute(parted[cuts.index(piece)], both, seconds)  2.35 us
    unnamed x14, local copies, waits for them, and re-layouts  2.29 us
  transfers between devices with their start and end apart: 6, of which 3 were waited for; matrix products, arithmetic and copies ran while one was open for 7% of the time, Pallas kernels for 26%

profile of v8, /device:TPU:1, one launch (start us, length us, event | category | flops | bytes accessed | tf_op | source)
XLA Modules:
  0.0 39.3 jit_solution(12920556317462023230)
XLA Ops:
  0.0 2.6 %collective-permute-start = (f32[3,2,512,128]{3,2,1,0:T(8,128)}, f32[3,2,512,128]{3,2,1,0:T(8,128)S(1)}, u32[]{:S(2)}, u32[]{:S(2)}) collective-permute-start(f32[3,2,512,128]{3,2,1,0:T(8,128)} %velocity.11), channel_id=1, source_target_pairs={{0,1},{1,0},{2,4},{3,5},{4,2},{5,3},{6,7},{7,6},{8,9},{9,8},{10,12... | collective-permute-start | bytes 4718600 | tf_op jit(solution)/shard_map/ppermute | solution.py:359
  2.6 6.0 %local.1 = (f32[2,512,128]{2,1,0:T(8,128)S(1)}, f32[2,512,128]{2,1,0:T(8,128)S(1)}, f32[2,512,128]{2,1,0:T(8,128)S(1)}, f32[2,2,512,128]{3,2,1,0:T(8,128)}, f32[...) custom-call(bf16[2,2,1024,512]{3,2,1,0:T(8,128)(2,1)} %constant.20.clone.blocks, ...), custom_call_target="tpu_custom_call" | custom-call | tf_op jit(solution)/shard_map/local/pallas_call | solution.py:331
  8.6 0.0 copy-start.1
  8.6 0.8 %copy-done.1 = f32[2,512,128]{2,1,0:T(8,128)} copy-done((f32[2,512,128]{2,1,0:T(8,128)}, f32[2,512,128]{2,1,0:T(8,128)S(1)}, u32[]{:S(2)}) %copy-start.1) | copy-done | bytes 524312
  9.4 0.0 copy-start.3
  9.4 0.8 %copy-done.3 = f32[2,512,128]{2,1,0:T(8,128)} copy-done((f32[2,512,128]{2,1,0:T(8,128)}, f32[2,512,128]{2,1,0:T(8,128)S(1)}, u32[]{:S(2)}) %copy-start.3) | copy-done | bytes 524312
  10.2 0.0 copy-start.5
  10.2 0.6 %copy-done.5 = f32[1,2,128,128]{3,2,1,0:T(8,128)} copy-done((f32[1,2,128,128]{3,2,1,0:T(8,128)}, f32[1,2,128,128]{3,2,1,0:T(8,128)S(1)}, u32[]{:S(2)}) %copy-start.5) | copy-done | bytes 131096
  10.9 0.4 %collective-permute-start.3 = (f32[2,2,512,128]{3,2,1,0:T(8,128)}, f32[2,2,512,128]{3,2,1,0:T(8,128)}, u32[]{:S(2)}, u32[]{:S(2)}) collective-permute-start(f32[2,2,512,128]{3,2,1,0:T(8,128)} %get-tuple-element.21), channel_id=1, source_target_pairs={{0,2},{2,0},{4,6},{6,4},{8,10},{10,8},{12,14},{14,12},{16,18},{18,... | collective-permute-start | bytes 3145736 | tf_op jit(solution)/shard_map/ppermute | solution.py:394
  11.3 0.8 %collective-permute-start.2 = (f32[2,2,512,128]{3,2,1,0:T(8,128)}, f32[2,2,512,128]{3,2,1,0:T(8,128)S(1)}, u32[]{:S(2)}, u32[]{:S(2)}) collective-permute-start(f32[2,2,512,128]{3,2,1,0:T(8,128)} %get-tuple-element.21), channel_id=1, source_target_pairs={{0,30},{1,31},{2,3},{3,2},{4,5},{5,4},{6,8},{7,9},{8,6},{9,7},{10,... | collective-permute-start | bytes 3145736 | tf_op jit(solution)/shard_map/ppermute | solution.py:395
  12.1 2.9 %collective-permute-start.4 = (f32[1,2,512,128]{3,2,1,0:T(8,128)}, f32[1,2,512,128]{3,2,1,0:T(8,128)}, u32[]{:S(2)}, u32[]{:S(2)}) collective-permute-start(f32[1,2,512,128]{3,2,1,0:T(8,128)} %get-tuple-element.22), channel_id=1, source_target_pairs={{0,2},{2,0},{4,6},{6,4},{8,10},{10,8},{12,14},{14,12},{16,18},{18,... | collective-permute-start | bytes 1572872 | tf_op jit(solution)/shard_map/ppermute | solution.py:394
  15.0 0.7 %collective-permute-start.5 = (f32[1,2,384,128]{3,2,1,0:T(8,128)}, f32[1,2,384,128]{3,2,1,0:T(8,128)S(1)}, u32[]{:S(2)}, u32[]{:S(2)}) collective-permute-start(f32[1,2,384,128]{3,2,1,0:T(8,128)} %get-tuple-element.30), channel_id=1, source_target_pairs={{0,30},{1,31},{2,3},{3,2},{4,5},{5,4},{6,8},{7,9},{8,6},{9,7},{10,... | collective-permute-start | bytes 1179656 | tf_op jit(solution)/shard_map/ppermute | solution.py:395
  15.7 0.0 copy-start.6
  15.7 0.0 copy-start.2
  15.7 0.0 copy-start.4
  15.7 1.4 %dynamic-slice_bitcast_fusion.coarse_operators = f8e4m3fn[1024,1024]{1,0:T(32,128)(4,1)S(1)} fusion(f8e4m3fn[2,1,1024,1024]{3,2,1,0:T(32,128)(4,1)} %constant.22.clone, s32[]{:T(128)S(6)} %select_n.6), kind=kLoop, calls=%fused_computation | loop fusion | bytes 2097156 | tf_op jit(solution)/shard_map/squeeze | solution.py:417
  17.1 0.0 collective-permute-done.4.refs_1_
  17.1 0.0 copy-done.6
  17.1 0.9 %collective-permute-start.1 = (f32[1,2,128,128]{3,2,1,0:T(8,128)S(1)}, f32[1,2,128,128]{3,2,1,0:T(8,128)S(1)}, u32[]{:S(2)}, u32[]{:S(2)}) collective-permute-start(f32[1,2,128,128]{3,2,1,0:T(8,128)S(1)} %copy-done.6), channel_id=1, source_target_pairs={{0,30},{1,31},{2,3},{3,2},{4,5},{5,4},{6,8},{7,9},{8,6},{9,7},{10,... | collective-permute-start | bytes 393224 | tf_op jit(solution)/shard_map/ppermute | solution.py:395
  18.0 1.3 %dynamic-slice_bitcast_fusion.1.high_operators = bf16[1024,512]{1,0:T(8,128)(2,1)S(1)} fusion(bf16[2,1,1024,512]{3,2,1,0:T(8,128)(2,1)} %constant.21.clone, s32[]{:T(128)S(6)} %select_n.6), kind=kLoop, calls=%fused_computation.1 | loop fusion | bytes 2097156 | tf_op jit(solution)/shard_map/squeeze | solution.py:417
  19.3 0.0 collective-permute-done.3.refs_0_
  19.3 0.0 copy-done.2
  19.3 0.0 copy-done.4
  19.3 0.0 copy-start
  19.3 2.0 %near.1 = (f32[2,512,128]{2,1,0:T(8,128)S(1)}, f32[2,512,128]{2,1,0:T(8,128)S(1)}, f32[2,512,128]{2,1,0:T(8,128)S(1)}) custom-call(f32[3,2,512,128]{3,2,1,0:T(8,128)} %velocity.11, f32[2,2,512,128]{3,2,1,0:T(8,128)} %collective-permute-done.3.refs_0_, f32[1,2,512,128]{3,2,1,0:T(8,128)} %collective-permute-done.4.refs_1_, ...), custom_call_target="tpu_custom_call" | custom-call | tf_op jit(solution)/shard_map/near/pallas_call | solution.py:331
  21.4 11.1 %collective-permute-done.2.piece = f32[2,2,512,128]{3,2,1,0:T(8,128)S(1)} collective-permute-done((f32[2,2,512,128]{3,2,1,0:T(8,128)}, f32[2,2,512,128]{3,2,1,0:T(8,128)S(1)}, u32[]{:S(2)}, u32[]{:S(2)}) %collective-permute-start.2) | collective-permute-done | bytes 1048608 | tf_op jit(solution)/shard_map/ppermute | solution.py:395
  32.5 0.0 copy-done
  32.5 1.3 %middle.2 = (f32[2,512,128]{2,1,0:T(8,128)S(1)}, f32[2,512,128]{2,1,0:T(8,128)S(1)}) custom-call(bf16[1024,512]{1,0:T(8,128)(2,1)S(1)} %dynamic-slice_bitcast_fusion.1.high_operators, f8e4m3fn[1024,1024]{1,0:T(32,128)(4,1)S(1)} %dynamic-slice_bitcast_fusion.coarse_operators, f32[3,2,512,128]{3,2,1,0:T(8,128)S(1)} %copy-done, ...), custom_call_target="tpu_custom_call" | custom-call | tf_op jit(solution)/shard_map/middle/pallas_call | solution.py:331
  33.8 2.6 %collective-permute-done.5.piece = f32[1,2,384,128]{3,2,1,0:T(8,128)S(1)} collective-permute-done((f32[1,2,384,128]{3,2,1,0:T(8,128)}, f32[1,2,384,128]{3,2,1,0:T(8,128)S(1)}, u32[]{:S(2)}, u32[]{:S(2)}) %collective-permute-start.5) | collective-permute-done | bytes 393248 | tf_op jit(solution)/shard_map/ppermute | solution.py:395
  36.4 0.7 %middle.3.refs_2_ = f32[2,512,128]{2,1,0:T(8,128)S(1)} custom-call(bf16[1024,512]{1,0:T(8,128)(2,1)S(1)} %dynamic-slice_bitcast_fusion.1.high_operators, f8e4m3fn[1024,1024]{1,0:T(32,128)(4,1)S(1)} %dynamic-slice_bitcast_fusion.coarse_operators, f32[3,2,512,128]{3,2,1,0:T(8,128)S(1)} %copy-done, f32[1,2,384,128]{3,2,1,0:T(8,128)S(1)} %collective-permute-done.5.piece, ...), custom_call_target="tpu_custom_call" | custom-call | tf_op jit(solution)/shard_map/middle/pallas_call | solution.py:331
  37.1 0.6 %collective-permute-done.whole = f32[3,2,512,128]{3,2,1,0:T(8,128)S(1)} collective-permute-done((f32[3,2,512,128]{3,2,1,0:T(8,128)}, f32[3,2,512,128]{3,2,1,0:T(8,128)S(1)}, u32[]{:S(2)}, u32[]{:S(2)}) %collective-permute-start) | collective-permute-done | bytes 1572896 | tf_op jit(solution)/shard_map/ppermute | solution.py:359
  37.8 0.2 first.1
  38.0 0.0 collective-permute-done.1.piece
  38.0 1.2 %last.1 = f32[3,2,512,128]{3,2,1,0:T(8,128)} custom-call(bf16[1024,512]{1,0:T(8,128)(2,1)S(1)} %dynamic-slice_bitcast_fusion.1.high_operators, f8e4m3fn[1024,1024]{1,0:T(32,128)(4,1)S(1)} %dynamic-slice_bitcast_fusion.coarse_operators, f32[3,2,512,128]{3,2,1,0:T(8,128)S(1)} %copy-done, f32[3,2,512,128]{3,2,1,0:T(8,128)S(1)} %collective-permute-done.whole, ...), custom_call_target="tpu_custom_call" | custom-call | tf_op jit(solution)/shard_map/last/pallas_call | solution.py:331
Async XLA Ops:
  0.0 37.8 %collective-permute-start = (f32[3,2,512,128]{3,2,1,0:T(8,128)}, f32[3,2,512,128]{3,2,1,0:T(8,128)S(1)}, u32[]{:S(2)}, u32[]{:S(2)}) collective-permute-start(f32[3,2,512,128]{3,2,1,0:T(8,128)} %velocity.11), channel_id=1, source_target_pairs={{0,1},{1,0},{2,4},{3,5},{4,2},{5,3},{6,7},{7,6},{8,9},{9,8},{10,12... | collective-permute-start | bytes 4718600 | tf_op jit(solution)/shard_map/ppermute | solution.py:359
  8.6 0.8 %copy-start.1 = (f32[2,512,128]{2,1,0:T(8,128)}, f32[2,512,128]{2,1,0:T(8,128)S(1)}, u32[]{:S(2)}) copy-start(f32[2,512,128]{2,1,0:T(8,128)S(1)} %get-tuple-element.24.refs_3_) | copy-start | bytes 1572868
  9.4 0.8 %copy-start.3 = (f32[2,512,128]{2,1,0:T(8,128)}, f32[2,512,128]{2,1,0:T(8,128)S(1)}, u32[]{:S(2)}) copy-start(f32[2,512,128]{2,1,0:T(8,128)S(1)} %get-tuple-element.25.refs_4_) | copy-start | bytes 1572868
  10.2 0.6 %copy-start.5 = (f32[1,2,128,128]{3,2,1,0:T(8,128)}, f32[1,2,128,128]{3,2,1,0:T(8,128)S(1)}, u32[]{:S(2)}) copy-start(f32[1,2,128,128]{3,2,1,0:T(8,128)S(1)} %get-tuple-element.20) | copy-start | bytes 393220
  10.9 8.4 %collective-permute-start.3 = (f32[2,2,512,128]{3,2,1,0:T(8,128)}, f32[2,2,512,128]{3,2,1,0:T(8,128)}, u32[]{:S(2)}, u32[]{:S(2)}) collective-permute-start(f32[2,2,512,128]{3,2,1,0:T(8,128)} %get-tuple-element.21), channel_id=1, source_target_pairs={{0,2},{2,0},{4,6},{6,4},{8,10},{10,8},{12,14},{14,12},{16,18},{18,... | collective-permute-start | bytes 3145736 | tf_op jit(solution)/shard_map/ppermute | solution.py:394
  11.3 21.2 %collective-permute-start.2 = (f32[2,2,512,128]{3,2,1,0:T(8,128)}, f32[2,2,512,128]{3,2,1,0:T(8,128)S(1)}, u32[]{:S(2)}, u32[]{:S(2)}) collective-permute-start(f32[2,2,512,128]{3,2,1,0:T(8,128)} %get-tuple-element.21), channel_id=1, source_target_pairs={{0,30},{1,31},{2,3},{3,2},{4,5},{5,4},{6,8},{7,9},{8,6},{9,7},{10,... | collective-permute-start | bytes 3145736 | tf_op jit(solution)/shard_map/ppermute | solution.py:395
  12.1 5.0 %collective-permute-start.4 = (f32[1,2,512,128]{3,2,1,0:T(8,128)}, f32[1,2,512,128]{3,2,1,0:T(8,128)}, u32[]{:S(2)}, u32[]{:S(2)}) collective-permute-start(f32[1,2,512,128]{3,2,1,0:T(8,128)} %get-tuple-element.22), channel_id=1, source_target_pairs={{0,2},{2,0},{4,6},{6,4},{8,10},{10,8},{12,14},{14,12},{16,18},{18,... | collective-permute-start | bytes 1572872 | tf_op jit(solution)/shard_map/ppermute | solution.py:394
  15.0 21.4 %collective-permute-start.5 = (f32[1,2,384,128]{3,2,1,0:T(8,128)}, f32[1,2,384,128]{3,2,1,0:T(8,128)S(1)}, u32[]{:S(2)}, u32[]{:S(2)}) collective-permute-start(f32[1,2,384,128]{3,2,1,0:T(8,128)} %get-tuple-element.30), channel_id=1, source_target_pairs={{0,30},{1,31},{2,3},{3,2},{4,5},{5,4},{6,8},{7,9},{8,6},{9,7},{10,... | collective-permute-start | bytes 1179656 | tf_op jit(solution)/shard_map/ppermute | solution.py:395
  15.7 1.4 %copy-start.6 = (f32[1,2,128,128]{3,2,1,0:T(8,128)S(1)}, f32[1,2,128,128]{3,2,1,0:T(8,128)}, u32[]{:S(2)}) copy-start(f32[1,2,128,128]{3,2,1,0:T(8,128)} %copy-done.5) | copy-start | bytes 393220
  15.7 3.6 %copy-start.2 = (f32[2,512,128]{2,1,0:T(8,128)S(1)}, f32[2,512,128]{2,1,0:T(8,128)}, u32[]{:S(2)}) copy-start(f32[2,512,128]{2,1,0:T(8,128)} %copy-done.1) | copy-start | bytes 1572868
  15.7 3.6 %copy-start.4 = (f32[2,512,128]{2,1,0:T(8,128)S(1)}, f32[2,512,128]{2,1,0:T(8,128)}, u32[]{:S(2)}) copy-start(f32[2,512,128]{2,1,0:T(8,128)} %copy-done.3) | copy-start | bytes 1572868
  17.1 20.9 %collective-permute-start.1 = (f32[1,2,128,128]{3,2,1,0:T(8,128)S(1)}, f32[1,2,128,128]{3,2,1,0:T(8,128)S(1)}, u32[]{:S(2)}, u32[]{:S(2)}) collective-permute-start(f32[1,2,128,128]{3,2,1,0:T(8,128)S(1)} %copy-done.6), channel_id=1, source_target_pairs={{0,30},{1,31},{2,3},{3,2},{4,5},{5,4},{6,8},{7,9},{8,6},{9,7},{10,... | collective-permute-start | bytes 393224 | tf_op jit(solution)/shard_map/ppermute | solution.py:395
  19.3 13.2 %copy-start = (f32[3,2,512,128]{3,2,1,0:T(8,128)S(1)}, f32[3,2,512,128]{3,2,1,0:T(8,128)}, u32[]{:S(2)}) copy-start(f32[3,2,512,128]{3,2,1,0:T(8,128)} %velocity.11) | copy-start | bytes 4718596

commit v9 on v8

--- a/solution.py
+++ b/solution.py
@@ -299,7 +299,7 @@
             more = wall_rows(undo, operators, field, velocity.at[1], i * half, half, begin)
             for plane in range(2):
                 total[plane, at] += more[plane]
-            stores[2 + i].start()
+            stores[2 + i].start(priority=1)
 
     @pl.when(jnp.logical_not(swapped))
     def _():
@@ -308,7 +308,7 @@
         terms = far_terms(velocity.at[0, :, at])
         add(bases[LAST].at[:, at], total.at[:, at], *terms(piece.at[0]))
         for i in range(2):
-            stores[2 + i].start()
+            stores[2 + i].start(priority=1)
 
     for store in stores:
         store.wait()

time: 39.4 us -> 39.4 us (level)
  no operation moved by 1% of the time
where the time goes in v9:
time: 39.4 us; the launch traced here: 39.3 us
  waiting for transfers between devices  14.4 us (37%)
  Pallas kernels  11.5 us (29%)
  starting transfers between devices  8.25 us (21%)
  local copies, waits for them, and re-layouts  5.01 us (13%)
    ppermute x3, waiting for transfers between devices, shards(): lax.ppermute(parted[cuts.index(piece)], both, seconds)  13.7 us
    pallas_call x6, Pallas kernels, call(): pl.pallas_call(kernel, in_specs=in_specs, out_shape=out_shape, compiler_p...  11.5 us
    ppermute x2, starting transfers between devices, shards(): near = [lax.ppermute(part, 'gx', inward) for part in parted[:len(PIECES)]]  3.3 us
    squeeze x2, local copies, waits for them, and re-layouts, shards(): fixed = (vmem(high[0]), vmem(coarse[0]), vmem(velocity))  2.71 us
    ppermute x1, starting transfers between devices, shards(): first = lax.ppermute(velocity, both, firsts)  2.6 us
    ppermute x3, starting transfers between devices, shards(): lax.ppermute(parted[cuts.index(piece)], both, seconds)  2.35 us
    unnamed x14, local copies, waits for them, and re-layouts  2.29 us
  transfers between devices with their start and end apart: 6, of which 3 were waited for; matrix products, arithmetic and copies ran while one was open for 7% of the time, Pallas kernels for 26%

profile of v9, /device:TPU:1, one launch (start us, length us, event | category | flops | bytes accessed | tf_op | source)
XLA Modules:
  0.0 39.3 jit_solution(10069534370091707159)
XLA Ops:
  0.0 2.6 %collective-permute-start = (f32[3,2,512,128]{3,2,1,0:T(8,128)}, f32[3,2,512,128]{3,2,1,0:T(8,128)S(1)}, u32[]{:S(2)}, u32[]{:S(2)}) collective-permute-start(f32[3,2,512,128]{3,2,1,0:T(8,128)} %velocity.11), channel_id=1, source_target_pairs={{0,1},{1,0},{2,4},{3,5},{4,2},{5,3},{6,7},{7,6},{8,9},{9,8},{10,12... | collective-permute-start | bytes 4718600 | tf_op jit(solution)/shard_map/ppermute | solution.py:359
  2.6 6.0 %local.1 = (f32[2,512,128]{2,1,0:T(8,128)S(1)}, f32[2,512,128]{2,1,0:T(8,128)S(1)}, f32[2,512,128]{2,1,0:T(8,128)S(1)}, f32[2,2,512,128]{3,2,1,0:T(8,128)}, f32[...) custom-call(bf16[2,2,1024,512]{3,2,1,0:T(8,128)(2,1)} %constant.20.clone.blocks, ...), custom_call_target="tpu_custom_call" | custom-call | tf_op jit(solution)/shard_map/local/pallas_call | solution.py:331
  8.6 0.0 copy-start.1
  8.6 0.8 %copy-done.1 = f32[2,512,128]{2,1,0:T(8,128)} copy-done((f32[2,512,128]{2,1,0:T(8,128)}, f32[2,512,128]{2,1,0:T(8,128)S(1)}, u32[]{:S(2)}) %copy-start.1) | copy-done | bytes 524312
  9.4 0.0 copy-start.3
  9.4 0.8 %copy-done.3 = f32[2,512,128]{2,1,0:T(8,128)} copy-done((f32[2,512,128]{2,1,0:T(8,128)}, f32[2,512,128]{2,1,0:T(8,128)S(1)}, u32[]{:S(2)}) %copy-start.3) | copy-done | bytes 524312
  10.2 0.0 copy-start.5
  10.2 0.6 %copy-done.5 = f32[1,2,128,128]{3,2,1,0:T(8,128)} copy-done((f32[1,2,128,128]{3,2,1,0:T(8,128)}, f32[1,2,128,128]{3,2,1,0:T(8,128)S(1)}, u32[]{:S(2)}) %copy-start.5) | copy-done | bytes 131096
  10.9 0.4 %collective-permute-start.3 = (f32[2,2,512,128]{3,2,1,0:T(8,128)}, f32[2,2,512,128]{3,2,1,0:T(8,128)}, u32[]{:S(2)}, u32[]{:S(2)}) collective-permute-start(f32[2,2,512,128]{3,2,1,0:T(8,128)} %get-tuple-element.21), channel_id=1, source_target_pairs={{0,2},{2,0},{4,6},{6,4},{8,10},{10,8},{12,14},{14,12},{16,18},{18,... | collective-permute-start | bytes 3145736 | tf_op jit(solution)/shard_map/ppermute | solution.py:394
  11.3 0.8 %collective-permute-start.2 = (f32[2,2,512,128]{3,2,1,0:T(8,128)}, f32[2,2,512,128]{3,2,1,0:T(8,128)S(1)}, u32[]{:S(2)}, u32[]{:S(2)}) collective-permute-start(f32[2,2,512,128]{3,2,1,0:T(8,128)} %get-tuple-element.21), channel_id=1, source_target_pairs={{0,30},{1,31},{2,3},{3,2},{4,5},{5,4},{6,8},{7,9},{8,6},{9,7},{10,... | collective-permute-start | bytes 3145736 | tf_op jit(solution)/shard_map/ppermute | solution.py:395
  12.1 2.9 %collective-permute-start.4 = (f32[1,2,512,128]{3,2,1,0:T(8,128)}, f32[1,2,512,128]{3,2,1,0:T(8,128)}, u32[]{:S(2)}, u32[]{:S(2)}) collective-permute-start(f32[1,2,512,128]{3,2,1,0:T(8,128)} %get-tuple-element.22), channel_id=1, source_target_pairs={{0,2},{2,0},{4,6},{6,4},{8,10},{10,8},{12,14},{14,12},{16,18},{18,... | collective-permute-start | bytes 1572872 | tf_op jit(solution)/shard_map/ppermute | solution.py:394
  15.0 0.7 %collective-permute-start.5 = (f32[1,2,384,128]{3,2,1,0:T(8,128)}, f32[1,2,384,128]{3,2,1,0:T(8,128)S(1)}, u32[]{:S(2)}, u32[]{:S(2)}) collective-permute-start(f32[1,2,384,128]{3,2,1,0:T(8,128)} %get-tuple-element.30), channel_id=1, source_target_pairs={{0,30},{1,31},{2,3},{3,2},{4,5},{5,4},{6,8},{7,9},{8,6},{9,7},{10,... | collective-permute-start | bytes 1179656 | tf_op jit(solution)/shard_map/ppermute | solution.py:395
  15.7 0.0 copy-start.6
  15.7 0.0 copy-start.2
  15.7 0.0 copy-start.4
  15.7 1.4 %dynamic-slice_bitcast_fusion.coarse_operators = f8e4m3fn[1024,1024]{1,0:T(32,128)(4,1)S(1)} fusion(f8e4m3fn[2,1,1024,1024]{3,2,1,0:T(32,128)(4,1)} %constant.22.clone, s32[]{:T(128)S(6)} %select_n.6), kind=kLoop, calls=%fused_computation | loop fusion | bytes 2097156 | tf_op jit(solution)/shard_map/squeeze | solution.py:417
  17.1 0.0 collective-permute-done.4.refs_1_
  17.1 0.0 copy-done.6
  17.1 0.9 %collective-permute-start.1 = (f32[1,2,128,128]{3,2,1,0:T(8,128)S(1)}, f32[1,2,128,128]{3,2,1,0:T(8,128)S(1)}, u32[]{:S(2)}, u32[]{:S(2)}) collective-permute-start(f32[1,2,128,128]{3,2,1,0:T(8,128)S(1)} %copy-done.6), channel_id=1, source_target_pairs={{0,30},{1,31},{2,3},{3,2},{4,5},{5,4},{6,8},{7,9},{8,6},{9,7},{10,... | collective-permute-start | bytes 393224 | tf_op jit(solution)/shard_map/ppermute | solution.py:395
  18.0 1.3 %dynamic-slice_bitcast_fusion.1.high_operators = bf16[1024,512]{1,0:T(8,128)(2,1)S(1)} fusion(bf16[2,1,1024,512]{3,2,1,0:T(8,128)(2,1)} %constant.21.clone, s32[]{:T(128)S(6)} %select_n.6), kind=kLoop, calls=%fused_computation.1 | loop fusion | bytes 2097156 | tf_op jit(solution)/shard_map/squeeze | solution.py:417
  19.3 0.0 collective-permute-done.3.refs_0_
  19.3 0.0 copy-done.2
  19.3 0.0 copy-done.4
  19.3 0.0 copy-start
  19.3 2.0 %near.1 = (f32[2,512,128]{2,1,0:T(8,128)S(1)}, f32[2,512,128]{2,1,0:T(8,128)S(1)}, f32[2,512,128]{2,1,0:T(8,128)S(1)}) custom-call(f32[3,2,512,128]{3,2,1,0:T(8,128)} %velocity.11, f32[2,2,512,128]{3,2,1,0:T(8,128)} %collective-permute-done.3.refs_0_, f32[1,2,512,128]{3,2,1,0:T(8,128)} %collective-permute-done.4.refs_1_, ...), custom_call_target="tpu_custom_call" | custom-call | tf_op jit(solution)/shard_map/near/pallas_call | solution.py:331
  21.4 11.1 %collective-permute-done.2.piece = f32[2,2,512,128]{3,2,1,0:T(8,128)S(1)} collective-permute-done((f32[2,2,512,128]{3,2,1,0:T(8,128)}, f32[2,2,512,128]{3,2,1,0:T(8,128)S(1)}, u32[]{:S(2)}, u32[]{:S(2)}) %collective-permute-start.2) | collective-permute-done | bytes 1048608 | tf_op jit(solution)/shard_map/ppermute | solution.py:395
  32.5 0.0 copy-done
  32.5 1.3 %middle.2 = (f32[2,512,128]{2,1,0:T(8,128)S(1)}, f32[2,512,128]{2,1,0:T(8,128)S(1)}) custom-call(bf16[1024,512]{1,0:T(8,128)(2,1)S(1)} %dynamic-slice_bitcast_fusion.1.high_operators, f8e4m3fn[1024,1024]{1,0:T(32,128)(4,1)S(1)} %dynamic-slice_bitcast_fusion.coarse_operators, f32[3,2,512,128]{3,2,1,0:T(8,128)S(1)} %copy-done, ...), custom_call_target="tpu_custom_call" | custom-call | tf_op jit(solution)/shard_map/middle/pallas_call | solution.py:331
  33.8 2.6 %collective-permute-done.5.piece = f32[1,2,384,128]{3,2,1,0:T(8,128)S(1)} collective-permute-done((f32[1,2,384,128]{3,2,1,0:T(8,128)}, f32[1,2,384,128]{3,2,1,0:T(8,128)S(1)}, u32[]{:S(2)}, u32[]{:S(2)}) %collective-permute-start.5) | collective-permute-done | bytes 393248 | tf_op jit(solution)/shard_map/ppermute | solution.py:395
  36.4 0.7 %middle.3.refs_2_ = f32[2,512,128]{2,1,0:T(8,128)S(1)} custom-call(bf16[1024,512]{1,0:T(8,128)(2,1)S(1)} %dynamic-slice_bitcast_fusion.1.high_operators, f8e4m3fn[1024,1024]{1,0:T(32,128)(4,1)S(1)} %dynamic-slice_bitcast_fusion.coarse_operators, f32[3,2,512,128]{3,2,1,0:T(8,128)S(1)} %copy-done, f32[1,2,384,128]{3,2,1,0:T(8,128)S(1)} %collective-permute-done.5.piece, ...), custom_call_target="tpu_custom_call" | custom-call | tf_op jit(solution)/shard_map/middle/pallas_call | solution.py:331
  37.1 0.6 %collective-permute-done.whole = f32[3,2,512,128]{3,2,1,0:T(8,128)S(1)} collective-permute-done((f32[3,2,512,128]{3,2,1,0:T(8,128)}, f32[3,2,512,128]{3,2,1,0:T(8,128)S(1)}, u32[]{:S(2)}, u32[]{:S(2)}) %collective-permute-start) | collective-permute-done | bytes 1572896 | tf_op jit(solution)/shard_map/ppermute | solution.py:359
  37.8 0.2 first.1
  38.0 0.0 collective-permute-done.1.piece
  38.0 1.2 %last.1 = f32[3,2,512,128]{3,2,1,0:T(8,128)} custom-call(bf16[1024,512]{1,0:T(8,128)(2,1)S(1)} %dynamic-slice_bitcast_fusion.1.high_operators, f8e4m3fn[1024,1024]{1,0:T(32,128)(4,1)S(1)} %dynamic-slice_bitcast_fusion.coarse_operators, f32[3,2,512,128]{3,2,1,0:T(8,128)S(1)} %copy-done, f32[3,2,512,128]{3,2,1,0:T(8,128)S(1)} %collective-permute-done.whole, ...), custom_call_target="tpu_custom_call" | custom-call | tf_op jit(solution)/shard_map/last/pallas_call | solution.py:331
Async XLA Ops:
  0.0 37.8 %collective-permute-start = (f32[3,2,512,128]{3,2,1,0:T(8,128)}, f32[3,2,512,128]{3,2,1,0:T(8,128)S(1)}, u32[]{:S(2)}, u32[]{:S(2)}) collective-permute-start(f32[3,2,512,128]{3,2,1,0:T(8,128)} %velocity.11), channel_id=1, source_target_pairs={{0,1},{1,0},{2,4},{3,5},{4,2},{5,3},{6,7},{7,6},{8,9},{9,8},{10,12... | collective-permute-start | bytes 4718600 | tf_op jit(solution)/shard_map/ppermute | solution.py:359
  8.6 0.8 %copy-start.1 = (f32[2,512,128]{2,1,0:T(8,128)}, f32[2,512,128]{2,1,0:T(8,128)S(1)}, u32[]{:S(2)}) copy-start(f32[2,512,128]{2,1,0:T(8,128)S(1)} %get-tuple-element.24.refs_3_) | copy-start | bytes 1572868
  9.4 0.8 %copy-start.3 = (f32[2,512,128]{2,1,0:T(8,128)}, f32[2,512,128]{2,1,0:T(8,128)S(1)}, u32[]{:S(2)}) copy-start(f32[2,512,128]{2,1,0:T(8,128)S(1)} %get-tuple-element.25.refs_4_) | copy-start | bytes 1572868
  10.2 0.6 %copy-start.5 = (f32[1,2,128,128]{3,2,1,0:T(8,128)}, f32[1,2,128,128]{3,2,1,0:T(8,128)S(1)}, u32[]{:S(2)}) copy-start(f32[1,2,128,128]{3,2,1,0:T(8,128)S(1)} %get-tuple-element.20) | copy-start | bytes 393220
  10.9 8.4 %collective-permute-start.3 = (f32[2,2,512,128]{3,2,1,0:T(8,128)}, f32[2,2,512,128]{3,2,1,0:T(8,128)}, u32[]{:S(2)}, u32[]{:S(2)}) collective-permute-start(f32[2,2,512,128]{3,2,1,0:T(8,128)} %get-tuple-element.21), channel_id=1, source_target_pairs={{0,2},{2,0},{4,6},{6,4},{8,10},{10,8},{12,14},{14,12},{16,18},{18,... | collective-permute-start | bytes 3145736 | tf_op jit(solution)/shard_map/ppermute | solution.py:394
  11.3 21.2 %collective-permute-start.2 = (f32[2,2,512,128]{3,2,1,0:T(8,128)}, f32[2,2,512,128]{3,2,1,0:T(8,128)S(1)}, u32[]{:S(2)}, u32[]{:S(2)}) collective-permute-start(f32[2,2,512,128]{3,2,1,0:T(8,128)} %get-tuple-element.21), channel_id=1, source_target_pairs={{0,30},{1,31},{2,3},{3,2},{4,5},{5,4},{6,8},{7,9},{8,6},{9,7},{10,... | collective-permute-start | bytes 3145736 | tf_op jit(solution)/shard_map/ppermute | solution.py:395
  12.1 5.0 %collective-permute-start.4 = (f32[1,2,512,128]{3,2,1,0:T(8,128)}, f32[1,2,512,128]{3,2,1,0:T(8,128)}, u32[]{:S(2)}, u32[]{:S(2)}) collective-permute-start(f32[1,2,512,128]{3,2,1,0:T(8,128)} %get-tuple-element.22), channel_id=1, source_target_pairs={{0,2},{2,0},{4,6},{6,4},{8,10},{10,8},{12,14},{14,12},{16,18},{18,... | collective-permute-start | bytes 1572872 | tf_op jit(solution)/shard_map/ppermute | solution.py:394
  15.0 21.4 %collective-permute-start.5 = (f32[1,2,384,128]{3,2,1,0:T(8,128)}, f32[1,2,384,128]{3,2,1,0:T(8,128)S(1)}, u32[]{:S(2)}, u32[]{:S(2)}) collective-permute-start(f32[1,2,384,128]{3,2,1,0:T(8,128)} %get-tuple-element.30), channel_id=1, source_target_pairs={{0,30},{1,31},{2,3},{3,2},{4,5},{5,4},{6,8},{7,9},{8,6},{9,7},{10,... | collective-permute-start | bytes 1179656 | tf_op jit(solution)/shard_map/ppermute | solution.py:395
  15.7 1.4 %copy-start.6 = (f32[1,2,128,128]{3,2,1,0:T(8,128)S(1)}, f32[1,2,128,128]{3,2,1,0:T(8,128)}, u32[]{:S(2)}) copy-start(f32[1,2,128,128]{3,2,1,0:T(8,128)} %copy-done.5) | copy-start | bytes 393220
  15.7 3.6 %copy-start.2 = (f32[2,512,128]{2,1,0:T(8,128)S(1)}, f32[2,512,128]{2,1,0:T(8,128)}, u32[]{:S(2)}) copy-start(f32[2,512,128]{2,1,0:T(8,128)} %copy-done.1) | copy-start | bytes 1572868
  15.7 3.6 %copy-start.4 = (f32[2,512,128]{2,1,0:T(8,128)S(1)}, f32[2,512,128]{2,1,0:T(8,128)}, u32[]{:S(2)}) copy-start(f32[2,512,128]{2,1,0:T(8,128)} %copy-done.3) | copy-start | bytes 1572868
  17.1 20.9 %collective-permute-start.1 = (f32[1,2,128,128]{3,2,1,0:T(8,128)S(1)}, f32[1,2,128,128]{3,2,1,0:T(8,128)S(1)}, u32[]{:S(2)}, u32[]{:S(2)}) collective-permute-start(f32[1,2,128,128]{3,2,1,0:T(8,128)S(1)} %copy-done.6), channel_id=1, source_target_pairs={{0,30},{1,31},{2,3},{3,2},{4,5},{5,4},{6,8},{7,9},{8,6},{9,7},{10,... | collective-permute-start | bytes 393224 | tf_op jit(solution)/shard_map/ppermute | solution.py:395
  19.3 13.2 %copy-start = (f32[3,2,512,128]{3,2,1,0:T(8,128)S(1)}, f32[3,2,512,128]{3,2,1,0:T(8,128)}, u32[]{:S(2)}) copy-start(f32[3,2,512,128]{3,2,1,0:T(8,128)} %velocity.11) | copy-start | bytes 4718596

commit v10 on v8

--- a/solution.py
+++ b/solution.py
@@ -261,7 +261,6 @@
 
     @pl.when(swapped)
     def _():
-        outs[LAST][...] = bases[LAST][...]
         for start in range(0, velocity.shape[2], TILE):
             at = pl.ds(start, TILE)
             terms = far_terms(velocity.at[0, :, at])
@@ -276,7 +275,7 @@
             add(bases[q], outs[q], *enumerate(terms))
 
 
-def last_kernel(undo, begin, high_operators, coarse_operators, velocity, whole, piece, *refs):
+def last_kernel(undo, begin, high_operators, coarse_operators, velocity, whole, piece, ahead, *refs):
     bases, (out, total, sent) = refs[:3], refs[3:]
     swapped = far_first(lax.axis_index("gx"))
     operators = (high_operators, coarse_operators)
@@ -295,7 +294,7 @@
         for i in range(2):
             at = pl.ds(i * half, half)
             terms = far_terms(velocity.at[0, :, at])
-            add(bases[LAST].at[:, at], total.at[:, at], *terms(whole.at[LAST, :, at]))
+            add(ahead.at[:, at], total.at[:, at], *terms(whole.at[LAST, :, at]))
             more = wall_rows(undo, operators, field, velocity.at[1], i * half, half, begin)
             for plane in range(2):
                 total[plane, at] += more[plane]
@@ -427,6 +426,7 @@
         for q, total in zip(c, added):
             totals[q] = total
         behind = added[:1]
+    ahead = totals[LAST]
     totals = call(
         functools.partial(first_kernel, undo),
         (*fixed, vmem(first), *totals),
@@ -436,8 +436,8 @@
     )
     return call(
         functools.partial(last_kernel, undo, pieces[-1][1]),
-        (*fixed, vmem(first), vmem(second[-1]), *totals),
-        [VMEM] * 8,
+        (*fixed, vmem(first), vmem(second[-1]), ahead, *totals),
+        [VMEM] * 9,
         whole,
         "last",
         out_specs=ANY,

time: 39.4 us -> 39.4 us (level)
  no operation moved by 1% of the time
where the time goes in v10:
time: 39.4 us; the launch traced here: 39.2 us
  waiting for transfers between devices  14.4 us (37%)
  Pallas kernels  11.5 us (29%)
  starting transfers between devices  8.25 us (21%)
  local copies, waits for them, and re-layouts  5.01 us (13%)
    ppermute x3, waiting for transfers between devices, shards(): lax.ppermute(parted[cuts.index(piece)], both, seconds)  13.7 us
    pallas_call x6, Pallas kernels, call(): pl.pallas_call(kernel, in_specs=in_specs, out_shape=out_shape, compiler_p...  11.5 us
    ppermute x2, starting transfers between devices, shards(): near = [lax.ppermute(part, 'gx', inward) for part in parted[:len(PIECES)]]  3.3 us
    squeeze x2, local copies, waits for them, and re-layouts, shards(): fixed = (vmem(high[0]), vmem(coarse[0]), vmem(velocity))  2.71 us
    ppermute x1, starting transfers between devices, shards(): first = lax.ppermute(velocity, both, firsts)  2.6 us
    ppermute x3, starting transfers between devices, shards(): lax.ppermute(parted[cuts.index(piece)], both, seconds)  2.35 us
    unnamed x14, local copies, waits for them, and re-layouts  2.29 us
  transfers between devices with their start and end apart: 6, of which 3 were waited for; matrix products, arithmetic and copies ran while one was open for 7% of the time, Pallas kernels for 26%

profile of v10, /device:TPU:1, one launch (start us, length us, event | category | flops | bytes accessed | tf_op | source)
XLA Modules:
  0.0 39.2 jit_solution(4262740286978921094)
XLA Ops:
  0.0 2.6 %collective-permute-start = (f32[3,2,512,128]{3,2,1,0:T(8,128)}, f32[3,2,512,128]{3,2,1,0:T(8,128)S(1)}, u32[]{:S(2)}, u32[]{:S(2)}) collective-permute-start(f32[3,2,512,128]{3,2,1,0:T(8,128)} %velocity.11), channel_id=1, source_target_pairs={{0,1},{1,0},{2,4},{3,5},{4,2},{5,3},{6,7},{7,6},{8,9},{9,8},{10,12... | collective-permute-start | bytes 4718600 | tf_op jit(solution)/shard_map/ppermute | solution.py:358
  2.6 6.0 %local.1 = (f32[2,512,128]{2,1,0:T(8,128)S(1)}, f32[2,512,128]{2,1,0:T(8,128)S(1)}, f32[2,512,128]{2,1,0:T(8,128)S(1)}, f32[2,2,512,128]{3,2,1,0:T(8,128)}, f32[...) custom-call(bf16[2,2,1024,512]{3,2,1,0:T(8,128)(2,1)} %constant.20.clone.blocks, ...), custom_call_target="tpu_custom_call" | custom-call | tf_op jit(solution)/shard_map/local/pallas_call | solution.py:330
  8.6 0.0 copy-start.1
  8.6 0.8 %copy-done.1 = f32[2,512,128]{2,1,0:T(8,128)} copy-done((f32[2,512,128]{2,1,0:T(8,128)}, f32[2,512,128]{2,1,0:T(8,128)S(1)}, u32[]{:S(2)}) %copy-start.1) | copy-done | bytes 524312
  9.4 0.0 copy-start.3
  9.4 0.8 %copy-done.3 = f32[2,512,128]{2,1,0:T(8,128)} copy-done((f32[2,512,128]{2,1,0:T(8,128)}, f32[2,512,128]{2,1,0:T(8,128)S(1)}, u32[]{:S(2)}) %copy-start.3) | copy-done | bytes 524312
  10.2 0.0 copy-start.5
  10.2 0.6 %copy-done.5 = f32[1,2,128,128]{3,2,1,0:T(8,128)} copy-done((f32[1,2,128,128]{3,2,1,0:T(8,128)}, f32[1,2,128,128]{3,2,1,0:T(8,128)S(1)}, u32[]{:S(2)}) %copy-start.5) | copy-done | bytes 131096
  10.9 0.4 %collective-permute-start.3 = (f32[2,2,512,128]{3,2,1,0:T(8,128)}, f32[2,2,512,128]{3,2,1,0:T(8,128)}, u32[]{:S(2)}, u32[]{:S(2)}) collective-permute-start(f32[2,2,512,128]{3,2,1,0:T(8,128)} %get-tuple-element.22), channel_id=1, source_target_pairs={{0,2},{2,0},{4,6},{6,4},{8,10},{10,8},{12,14},{14,12},{16,18},{18,... | collective-permute-start | bytes 3145736 | tf_op jit(solution)/shard_map/ppermute | solution.py:393
  11.3 0.8 %collective-permute-start.5 = (f32[2,2,512,128]{3,2,1,0:T(8,128)}, f32[2,2,512,128]{3,2,1,0:T(8,128)S(1)}, u32[]{:S(2)}, u32[]{:S(2)}) collective-permute-start(f32[2,2,512,128]{3,2,1,0:T(8,128)} %get-tuple-element.22), channel_id=1, source_target_pairs={{0,30},{1,31},{2,3},{3,2},{4,5},{5,4},{6,8},{7,9},{8,6},{9,7},{10,... | collective-permute-start | bytes 3145736 | tf_op jit(solution)/shard_map/ppermute | solution.py:394
  12.1 2.9 %collective-permute-start.4 = (f32[1,2,512,128]{3,2,1,0:T(8,128)}, f32[1,2,512,128]{3,2,1,0:T(8,128)}, u32[]{:S(2)}, u32[]{:S(2)}) collective-permute-start(f32[1,2,512,128]{3,2,1,0:T(8,128)} %get-tuple-element.23), channel_id=1, source_target_pairs={{0,2},{2,0},{4,6},{6,4},{8,10},{10,8},{12,14},{14,12},{16,18},{18,... | collective-permute-start | bytes 1572872 | tf_op jit(solution)/shard_map/ppermute | solution.py:393
  15.0 0.7 %collective-permute-start.2 = (f32[1,2,384,128]{3,2,1,0:T(8,128)}, f32[1,2,384,128]{3,2,1,0:T(8,128)S(1)}, u32[]{:S(2)}, u32[]{:S(2)}) collective-permute-start(f32[1,2,384,128]{3,2,1,0:T(8,128)} %get-tuple-element.21), channel_id=1, source_target_pairs={{0,30},{1,31},{2,3},{3,2},{4,5},{5,4},{6,8},{7,9},{8,6},{9,7},{10,... | collective-permute-start | bytes 1179656 | tf_op jit(solution)/shard_map/ppermute | solution.py:394
  15.7 0.0 copy-start.6
  15.7 0.0 copy-start.2
  15.7 0.0 copy-start.4
  15.7 1.4 %dynamic-slice_bitcast_fusion.coarse_operators = f8e4m3fn[1024,1024]{1,0:T(32,128)(4,1)S(1)} fusion(f8e4m3fn[2,1,1024,1024]{3,2,1,0:T(32,128)(4,1)} %constant.22.clone, s32[]{:T(128)S(6)} %select_n.6), kind=kLoop, calls=%fused_computation | loop fusion | bytes 2097156 | tf_op jit(solution)/shard_map/squeeze | solution.py:416
  17.1 0.0 collective-permute-done.4.refs_1_
  17.1 0.0 copy-done.6
  17.1 0.9 %collective-permute-start.1 = (f32[1,2,128,128]{3,2,1,0:T(8,128)S(1)}, f32[1,2,128,128]{3,2,1,0:T(8,128)S(1)}, u32[]{:S(2)}, u32[]{:S(2)}) collective-permute-start(f32[1,2,128,128]{3,2,1,0:T(8,128)S(1)} %copy-done.6), channel_id=1, source_target_pairs={{0,30},{1,31},{2,3},{3,2},{4,5},{5,4},{6,8},{7,9},{8,6},{9,7},{10,... | collective-permute-start | bytes 393224 | tf_op jit(solution)/shard_map/ppermute | solution.py:394
  18.0 1.3 %dynamic-slice_bitcast_fusion.1.high_operators = bf16[1024,512]{1,0:T(8,128)(2,1)S(1)} fusion(bf16[2,1,1024,512]{3,2,1,0:T(8,128)(2,1)} %constant.21.clone, s32[]{:T(128)S(6)} %select_n.6), kind=kLoop, calls=%fused_computation.1 | loop fusion | bytes 2097156 | tf_op jit(solution)/shard_map/squeeze | solution.py:416
  19.3 0.0 collective-permute-done.3.refs_0_
  19.3 0.0 copy-done.2
  19.3 0.0 copy-done.4
  19.3 0.0 copy-start
  19.3 2.0 %near.1 = (f32[2,512,128]{2,1,0:T(8,128)S(1)}, f32[2,512,128]{2,1,0:T(8,128)S(1)}, f32[2,512,128]{2,1,0:T(8,128)S(1)}) custom-call(f32[3,2,512,128]{3,2,1,0:T(8,128)} %velocity.11, f32[2,2,512,128]{3,2,1,0:T(8,128)} %collective-permute-done.3.refs_0_, f32[1,2,512,128]{3,2,1,0:T(8,128)} %collective-permute-done.4.refs_1_, ...), custom_call_target="tpu_custom_call" | custom-call | tf_op jit(solution)/shard_map/near/pallas_call | solution.py:330
  21.4 11.1 %collective-permute-done.5.piece = f32[2,2,512,128]{3,2,1,0:T(8,128)S(1)} collective-permute-done((f32[2,2,512,128]{3,2,1,0:T(8,128)}, f32[2,2,512,128]{3,2,1,0:T(8,128)S(1)}, u32[]{:S(2)}, u32[]{:S(2)}) %collective-permute-start.5) | collective-permute-done | bytes 1048608 | tf_op jit(solution)/shard_map/ppermute | solution.py:394
  32.5 0.0 copy-done
  32.5 1.3 %middle.2 = (f32[2,512,128]{2,1,0:T(8,128)S(1)}, f32[2,512,128]{2,1,0:T(8,128)S(1)}) custom-call(bf16[1024,512]{1,0:T(8,128)(2,1)S(1)} %dynamic-slice_bitcast_fusion.1.high_operators, f8e4m3fn[1024,1024]{1,0:T(32,128)(4,1)S(1)} %dynamic-slice_bitcast_fusion.coarse_operators, f32[3,2,512,128]{3,2,1,0:T(8,128)S(1)} %copy-done, ...), custom_call_target="tpu_custom_call" | custom-call | tf_op jit(solution)/shard_map/middle/pallas_call | solution.py:330
  33.8 2.6 %collective-permute-done.2.piece = f32[1,2,384,128]{3,2,1,0:T(8,128)S(1)} collective-permute-done((f32[1,2,384,128]{3,2,1,0:T(8,128)}, f32[1,2,384,128]{3,2,1,0:T(8,128)S(1)}, u32[]{:S(2)}, u32[]{:S(2)}) %collective-permute-start.2) | collective-permute-done | bytes 393248 | tf_op jit(solution)/shard_map/ppermute | solution.py:394
  36.4 0.7 %middle.3.refs_2_.ahead = f32[2,512,128]{2,1,0:T(8,128)S(1)} custom-call(bf16[1024,512]{1,0:T(8,128)(2,1)S(1)} %dynamic-slice_bitcast_fusion.1.high_operators, f8e4m3fn[1024,1024]{1,0:T(32,128)(4,1)S(1)} %dynamic-slice_bitcast_fusion.coarse_operators, f32[3,2,512,128]{3,2,1,0:T(8,128)S(1)} %copy-done, f32[1,2,384,128]{3,2,1,0:T(8,128)S(1)} %collective-permute-done.2.piece, ...), custom_call_target="tpu_custom_call" | custom-call | tf_op jit(solution)/shard_map/middle/pallas_call | solution.py:330
  37.1 0.6 %collective-permute-done.whole = f32[3,2,512,128]{3,2,1,0:T(8,128)S(1)} collective-permute-done((f32[3,2,512,128]{3,2,1,0:T(8,128)}, f32[3,2,512,128]{3,2,1,0:T(8,128)S(1)}, u32[]{:S(2)}, u32[]{:S(2)}) %collective-permute-start) | collective-permute-done | bytes 1572896 | tf_op jit(solution)/shard_map/ppermute | solution.py:358
  37.8 0.2 first.1
  38.0 0.0 collective-permute-done.1.piece
  38.0 1.2 %last.1 = f32[3,2,512,128]{3,2,1,0:T(8,128)} custom-call(bf16[1024,512]{1,0:T(8,128)(2,1)S(1)} %dynamic-slice_bitcast_fusion.1.high_operators, f8e4m3fn[1024,1024]{1,0:T(32,128)(4,1)S(1)} %dynamic-slice_bitcast_fusion.coarse_operators, f32[3,2,512,128]{3,2,1,0:T(8,128)S(1)} %copy-done, f32[3,2,512,128]{3,2,1,0:T(8,128)S(1)} %collective-permute-done.whole, ...), custom_call_target="tpu_custom_call" | custom-call | tf_op jit(solution)/shard_map/last/pallas_call | solution.py:330
Async XLA Ops:
  0.0 37.8 %collective-permute-start = (f32[3,2,512,128]{3,2,1,0:T(8,128)}, f32[3,2,512,128]{3,2,1,0:T(8,128)S(1)}, u32[]{:S(2)}, u32[]{:S(2)}) collective-permute-start(f32[3,2,512,128]{3,2,1,0:T(8,128)} %velocity.11), channel_id=1, source_target_pairs={{0,1},{1,0},{2,4},{3,5},{4,2},{5,3},{6,7},{7,6},{8,9},{9,8},{10,12... | collective-permute-start | bytes 4718600 | tf_op jit(solution)/shard_map/ppermute | solution.py:358
  8.6 0.8 %copy-start.1 = (f32[2,512,128]{2,1,0:T(8,128)}, f32[2,512,128]{2,1,0:T(8,128)S(1)}, u32[]{:S(2)}) copy-start(f32[2,512,128]{2,1,0:T(8,128)S(1)} %get-tuple-element.25.refs_3_) | copy-start | bytes 1572868
  9.4 0.8 %copy-start.3 = (f32[2,512,128]{2,1,0:T(8,128)}, f32[2,512,128]{2,1,0:T(8,128)S(1)}, u32[]{:S(2)}) copy-start(f32[2,512,128]{2,1,0:T(8,128)S(1)} %get-tuple-element.26.refs_4_) | copy-start | bytes 1572868
  10.2 0.6 %copy-start.5 = (f32[1,2,128,128]{3,2,1,0:T(8,128)}, f32[1,2,128,128]{3,2,1,0:T(8,128)S(1)}, u32[]{:S(2)}) copy-start(f32[1,2,128,128]{3,2,1,0:T(8,128)S(1)} %get-tuple-element.20) | copy-start | bytes 393220
  10.9 8.4 %collective-permute-start.3 = (f32[2,2,512,128]{3,2,1,0:T(8,128)}, f32[2,2,512,128]{3,2,1,0:T(8,128)}, u32[]{:S(2)}, u32[]{:S(2)}) collective-permute-start(f32[2,2,512,128]{3,2,1,0:T(8,128)} %get-tuple-element.22), channel_id=1, source_target_pairs={{0,2},{2,0},{4,6},{6,4},{8,10},{10,8},{12,14},{14,12},{16,18},{18,... | collective-permute-start | bytes 3145736 | tf_op jit(solution)/shard_map/ppermute | solution.py:393
  11.3 21.2 %collective-permute-start.5 = (f32[2,2,512,128]{3,2,1,0:T(8,128)}, f32[2,2,512,128]{3,2,1,0:T(8,128)S(1)}, u32[]{:S(2)}, u32[]{:S(2)}) collective-permute-start(f32[2,2,512,128]{3,2,1,0:T(8,128)} %get-tuple-element.22), channel_id=1, source_target_pairs={{0,30},{1,31},{2,3},{3,2},{4,5},{5,4},{6,8},{7,9},{8,6},{9,7},{10,... | collective-permute-start | bytes 3145736 | tf_op jit(solution)/shard_map/ppermute | solution.py:394
  12.1 5.0 %collective-permute-start.4 = (f32[1,2,512,128]{3,2,1,0:T(8,128)}, f32[1,2,512,128]{3,2,1,0:T(8,128)}, u32[]{:S(2)}, u32[]{:S(2)}) collective-permute-start(f32[1,2,512,128]{3,2,1,0:T(8,128)} %get-tuple-element.23), channel_id=1, source_target_pairs={{0,2},{2,0},{4,6},{6,4},{8,10},{10,8},{12,14},{14,12},{16,18},{18,... | collective-permute-start | bytes 1572872 | tf_op jit(solution)/shard_map/ppermute | solution.py:393
  15.0 21.4 %collective-permute-start.2 = (f32[1,2,384,128]{3,2,1,0:T(8,128)}, f32[1,2,384,128]{3,2,1,0:T(8,128)S(1)}, u32[]{:S(2)}, u32[]{:S(2)}) collective-permute-start(f32[1,2,384,128]{3,2,1,0:T(8,128)} %get-tuple-element.21), channel_id=1, source_target_pairs={{0,30},{1,31},{2,3},{3,2},{4,5},{5,4},{6,8},{7,9},{8,6},{9,7},{10,... | collective-permute-start | bytes 1179656 | tf_op jit(solution)/shard_map/ppermute | solution.py:394
  15.7 1.4 %copy-start.6 = (f32[1,2,128,128]{3,2,1,0:T(8,128)S(1)}, f32[1,2,128,128]{3,2,1,0:T(8,128)}, u32[]{:S(2)}) copy-start(f32[1,2,128,128]{3,2,1,0:T(8,128)} %copy-done.5) | copy-start | bytes 393220
  15.7 3.6 %copy-start.2 = (f32[2,512,128]{2,1,0:T(8,128)S(1)}, f32[2,512,128]{2,1,0:T(8,128)}, u32[]{:S(2)}) copy-start(f32[2,512,128]{2,1,0:T(8,128)} %copy-done.1) | copy-start | bytes 1572868
  15.7 3.6 %copy-start.4 = (f32[2,512,128]{2,1,0:T(8,128)S(1)}, f32[2,512,128]{2,1,0:T(8,128)}, u32[]{:S(2)}) copy-start(f32[2,512,128]{2,1,0:T(8,128)} %copy-done.3) | copy-start | bytes 1572868
  17.1 20.9 %collective-permute-start.1 = (f32[1,2,128,128]{3,2,1,0:T(8,128)S(1)}, f32[1,2,128,128]{3,2,1,0:T(8,128)S(1)}, u32[]{:S(2)}, u32[]{:S(2)}) collective-permute-start(f32[1,2,128,128]{3,2,1,0:T(8,128)S(1)} %copy-done.6), channel_id=1, source_target_pairs={{0,30},{1,31},{2,3},{3,2},{4,5},{5,4},{6,8},{7,9},{8,6},{9,7},{10,... | collective-permute-start | bytes 393224 | tf_op jit(solution)/shard_map/ppermute | solution.py:394
  19.3 13.2 %copy-start = (f32[3,2,512,128]{3,2,1,0:T(8,128)S(1)}, f32[3,2,512,128]{3,2,1,0:T(8,128)}, u32[]{:S(2)}) copy-start(f32[3,2,512,128]{3,2,1,0:T(8,128)} %velocity.11) | copy-start | bytes 4718596

commit v11 on v10

--- a/solution.py
+++ b/solution.py
@@ -298,7 +298,7 @@
             more = wall_rows(undo, operators, field, velocity.at[1], i * half, half, begin)
             for plane in range(2):
                 total[plane, at] += more[plane]
-            stores[2 + i].start()
+            stores[2 + i].start(priority=1)
 
     @pl.when(jnp.logical_not(swapped))
     def _():
@@ -307,7 +307,7 @@
         terms = far_terms(velocity.at[0, :, at])
         add(bases[LAST].at[:, at], total.at[:, at], *terms(piece.at[0]))
         for i in range(2):
-            stores[2 + i].start()
+            stores[2 + i].start(priority=1)
 
     for store in stores:
         store.wait()

time: 39.4 us -> 39.4 us (level)
  no operation moved by 1% of the time
where the time goes in v11:
time: 39.4 us; the launch traced here: 39.2 us
  waiting for transfers between devices  14.4 us (37%)
  Pallas kernels  11.5 us (29%)
  starting transfers between devices  8.25 us (21%)
  local copies, waits for them, and re-layouts  5.01 us (13%)
    ppermute x3, waiting for transfers between devices, shards(): lax.ppermute(parted[cuts.index(piece)], both, seconds)  13.7 us
    pallas_call x6, Pallas kernels, call(): pl.pallas_call(kernel, in_specs=in_specs, out_shape=out_shape, compiler_p...  11.5 us
    ppermute x2, starting transfers between devices, shards(): near = [lax.ppermute(part, 'gx', inward) for part in parted[:len(PIECES)]]  3.3 us
    squeeze x2, local copies, waits for them, and re-layouts, shards(): fixed = (vmem(high[0]), vmem(coarse[0]), vmem(velocity))  2.71 us
    ppermute x1, starting transfers between devices, shards(): first = lax.ppermute(velocity, both, firsts)  2.6 us
    ppermute x3, starting transfers between devices, shards(): lax.ppermute(parted[cuts.index(piece)], both, seconds)  2.35 us
    unnamed x14, local copies, waits for them, and re-layouts  2.29 us
  transfers between devices with their start and end apart: 6, of which 3 were waited for; matrix products, arithmetic and copies ran while one was open for 7% of the time, Pallas kernels for 26%

profile of v11, /device:TPU:1, one launch (start us, length us, event | category | flops | bytes accessed | tf_op | source)
XLA Modules:
  0.0 39.2 jit_solution(2197444301640845145)
XLA Ops:
  0.0 2.6 %collective-permute-start = (f32[3,2,512,128]{3,2,1,0:T(8,128)}, f32[3,2,512,128]{3,2,1,0:T(8,128)S(1)}, u32[]{:S(2)}, u32[]{:S(2)}) collective-permute-start(f32[3,2,512,128]{3,2,1,0:T(8,128)} %velocity.11), channel_id=1, source_target_pairs={{0,1},{1,0},{2,4},{3,5},{4,2},{5,3},{6,7},{7,6},{8,9},{9,8},{10,12... | collective-permute-start | bytes 4718600 | tf_op jit(solution)/shard_map/ppermute | solution.py:358
  2.6 6.0 %local.1 = (f32[2,512,128]{2,1,0:T(8,128)S(1)}, f32[2,512,128]{2,1,0:T(8,128)S(1)}, f32[2,512,128]{2,1,0:T(8,128)S(1)}, f32[2,2,512,128]{3,2,1,0:T(8,128)}, f32[...) custom-call(bf16[2,2,1024,512]{3,2,1,0:T(8,128)(2,1)} %constant.20.clone.blocks, ...), custom_call_target="tpu_custom_call" | custom-call | tf_op jit(solution)/shard_map/local/pallas_call | solution.py:330
  8.6 0.0 copy-start.1
  8.6 0.8 %copy-done.1 = f32[2,512,128]{2,1,0:T(8,128)} copy-done((f32[2,512,128]{2,1,0:T(8,128)}, f32[2,512,128]{2,1,0:T(8,128)S(1)}, u32[]{:S(2)}) %copy-start.1) | copy-done | bytes 524312
  9.4 0.0 copy-start.3
  9.4 0.8 %copy-done.3 = f32[2,512,128]{2,1,0:T(8,128)} copy-done((f32[2,512,128]{2,1,0:T(8,128)}, f32[2,512,128]{2,1,0:T(8,128)S(1)}, u32[]{:S(2)}) %copy-start.3) | copy-done | bytes 524312
  10.2 0.0 copy-start.5
  10.2 0.6 %copy-done.5 = f32[1,2,128,128]{3,2,1,0:T(8,128)} copy-done((f32[1,2,128,128]{3,2,1,0:T(8,128)}, f32[1,2,128,128]{3,2,1,0:T(8,128)S(1)}, u32[]{:S(2)}) %copy-start.5) | copy-done | bytes 131096
  10.9 0.4 %collective-permute-start.3 = (f32[2,2,512,128]{3,2,1,0:T(8,128)}, f32[2,2,512,128]{3,2,1,0:T(8,128)}, u32[]{:S(2)}, u32[]{:S(2)}) collective-permute-start(f32[2,2,512,128]{3,2,1,0:T(8,128)} %get-tuple-element.22), channel_id=1, source_target_pairs={{0,2},{2,0},{4,6},{6,4},{8,10},{10,8},{12,14},{14,12},{16,18},{18,... | collective-permute-start | bytes 3145736 | tf_op jit(solution)/shard_map/ppermute | solution.py:393
  11.3 0.8 %collective-permute-start.5 = (f32[2,2,512,128]{3,2,1,0:T(8,128)}, f32[2,2,512,128]{3,2,1,0:T(8,128)S(1)}, u32[]{:S(2)}, u32[]{:S(2)}) collective-permute-start(f32[2,2,512,128]{3,2,1,0:T(8,128)} %get-tuple-element.22), channel_id=1, source_target_pairs={{0,30},{1,31},{2,3},{3,2},{4,5},{5,4},{6,8},{7,9},{8,6},{9,7},{10,... | collective-permute-start | bytes 3145736 | tf_op jit(solution)/shard_map/ppermute | solution.py:394
  12.1 2.9 %collective-permute-start.4 = (f32[1,2,512,128]{3,2,1,0:T(8,128)}, f32[1,2,512,128]{3,2,1,0:T(8,128)}, u32[]{:S(2)}, u32[]{:S(2)}) collective-permute-start(f32[1,2,512,128]{3,2,1,0:T(8,128)} %get-tuple-element.23), channel_id=1, source_target_pairs={{0,2},{2,0},{4,6},{6,4},{8,10},{10,8},{12,14},{14,12},{16,18},{18,... | collective-permute-start | bytes 1572872 | tf_op jit(solution)/shard_map/ppermute | solution.py:393
  15.0 0.7 %collective-permute-start.2 = (f32[1,2,384,128]{3,2,1,0:T(8,128)}, f32[1,2,384,128]{3,2,1,0:T(8,128)S(1)}, u32[]{:S(2)}, u32[]{:S(2)}) collective-permute-start(f32[1,2,384,128]{3,2,1,0:T(8,128)} %get-tuple-element.21), channel_id=1, source_target_pairs={{0,30},{1,31},{2,3},{3,2},{4,5},{5,4},{6,8},{7,9},{8,6},{9,7},{10,... | collective-permute-start | bytes 1179656 | tf_op jit(solution)/shard_map/ppermute | solution.py:394
  15.7 0.0 copy-start.6
  15.7 0.0 copy-start.2
  15.7 0.0 copy-start.4
  15.7 1.4 %dynamic-slice_bitcast_fusion.coarse_operators = f8e4m3fn[1024,1024]{1,0:T(32,128)(4,1)S(1)} fusion(f8e4m3fn[2,1,1024,1024]{3,2,1,0:T(32,128)(4,1)} %constant.22.clone, s32[]{:T(128)S(6)} %select_n.6), kind=kLoop, calls=%fused_computation | loop fusion | bytes 2097156 | tf_op jit(solution)/shard_map/squeeze | solution.py:416
  17.1 0.0 collective-permute-done.4.refs_1_
  17.1 0.0 copy-done.6
  17.1 0.9 %collective-permute-start.1 = (f32[1,2,128,128]{3,2,1,0:T(8,128)S(1)}, f32[1,2,128,128]{3,2,1,0:T(8,128)S(1)}, u32[]{:S(2)}, u32[]{:S(2)}) collective-permute-start(f32[1,2,128,128]{3,2,1,0:T(8,128)S(1)} %copy-done.6), channel_id=1, source_target_pairs={{0,30},{1,31},{2,3},{3,2},{4,5},{5,4},{6,8},{7,9},{8,6},{9,7},{10,... | collective-permute-start | bytes 393224 | tf_op jit(solution)/shard_map/ppermute | solution.py:394
  18.0 1.3 %dynamic-slice_bitcast_fusion.1.high_operators = bf16[1024,512]{1,0:T(8,128)(2,1)S(1)} fusion(bf16[2,1,1024,512]{3,2,1,0:T(8,128)(2,1)} %constant.21.clone, s32[]{:T(128)S(6)} %select_n.6), kind=kLoop, calls=%fused_computation.1 | loop fusion | bytes 2097156 | tf_op jit(solution)/shard_map/squeeze | solution.py:416
  19.3 0.0 collective-permute-done.3.refs_0_
  19.3 0.0 copy-done.2
  19.3 0.0 copy-done.4
  19.3 0.0 copy-start
  19.3 2.0 %near.1 = (f32[2,512,128]{2,1,0:T(8,128)S(1)}, f32[2,512,128]{2,1,0:T(8,128)S(1)}, f32[2,512,128]{2,1,0:T(8,128)S(1)}) custom-call(f32[3,2,512,128]{3,2,1,0:T(8,128)} %velocity.11, f32[2,2,512,128]{3,2,1,0:T(8,128)} %collective-permute-done.3.refs_0_, f32[1,2,512,128]{3,2,1,0:T(8,128)} %collective-permute-done.4.refs_1_, ...), custom_call_target="tpu_custom_call" | custom-call | tf_op jit(solution)/shard_map/near/pallas_call | solution.py:330
  21.4 11.1 %collective-permute-done.5.piece = f32[2,2,512,128]{3,2,1,0:T(8,128)S(1)} collective-permute-done((f32[2,2,512,128]{3,2,1,0:T(8,128)}, f32[2,2,512,128]{3,2,1,0:T(8,128)S(1)}, u32[]{:S(2)}, u32[]{:S(2)}) %collective-permute-start.5) | collective-permute-done | bytes 1048608 | tf_op jit(solution)/shard_map/ppermute | solution.py:394
  32.5 0.0 copy-done
  32.5 1.3 %middle.2 = (f32[2,512,128]{2,1,0:T(8,128)S(1)}, f32[2,512,128]{2,1,0:T(8,128)S(1)}) custom-call(bf16[1024,512]{1,0:T(8,128)(2,1)S(1)} %dynamic-slice_bitcast_fusion.1.high_operators, f8e4m3fn[1024,1024]{1,0:T(32,128)(4,1)S(1)} %dynamic-slice_bitcast_fusion.coarse_operators, f32[3,2,512,128]{3,2,1,0:T(8,128)S(1)} %copy-done, ...), custom_call_target="tpu_custom_call" | custom-call | tf_op jit(solution)/shard_map/middle/pallas_call | solution.py:330
  33.8 2.6 %collective-permute-done.2.piece = f32[1,2,384,128]{3,2,1,0:T(8,128)S(1)} collective-permute-done((f32[1,2,384,128]{3,2,1,0:T(8,128)}, f32[1,2,384,128]{3,2,1,0:T(8,128)S(1)}, u32[]{:S(2)}, u32[]{:S(2)}) %collective-permute-start.2) | collective-permute-done | bytes 393248 | tf_op jit(solution)/shard_map/ppermute | solution.py:394
  36.4 0.7 %middle.3.refs_2_.ahead = f32[2,512,128]{2,1,0:T(8,128)S(1)} custom-call(bf16[1024,512]{1,0:T(8,128)(2,1)S(1)} %dynamic-slice_bitcast_fusion.1.high_operators, f8e4m3fn[1024,1024]{1,0:T(32,128)(4,1)S(1)} %dynamic-slice_bitcast_fusion.coarse_operators, f32[3,2,512,128]{3,2,1,0:T(8,128)S(1)} %copy-done, f32[1,2,384,128]{3,2,1,0:T(8,128)S(1)} %collective-permute-done.2.piece, ...), custom_call_target="tpu_custom_call" | custom-call | tf_op jit(solution)/shard_map/middle/pallas_call | solution.py:330
  37.1 0.6 %collective-permute-done.whole = f32[3,2,512,128]{3,2,1,0:T(8,128)S(1)} collective-permute-done((f32[3,2,512,128]{3,2,1,0:T(8,128)}, f32[3,2,512,128]{3,2,1,0:T(8,128)S(1)}, u32[]{:S(2)}, u32[]{:S(2)}) %collective-permute-start) | collective-permute-done | bytes 1572896 | tf_op jit(solution)/shard_map/ppermute | solution.py:358
  37.8 0.2 first.1
  38.0 0.0 collective-permute-done.1.piece
  38.0 1.2 %last.1 = f32[3,2,512,128]{3,2,1,0:T(8,128)} custom-call(bf16[1024,512]{1,0:T(8,128)(2,1)S(1)} %dynamic-slice_bitcast_fusion.1.high_operators, f8e4m3fn[1024,1024]{1,0:T(32,128)(4,1)S(1)} %dynamic-slice_bitcast_fusion.coarse_operators, f32[3,2,512,128]{3,2,1,0:T(8,128)S(1)} %copy-done, f32[3,2,512,128]{3,2,1,0:T(8,128)S(1)} %collective-permute-done.whole, ...), custom_call_target="tpu_custom_call" | custom-call | tf_op jit(solution)/shard_map/last/pallas_call | solution.py:330
Async XLA Ops:
  0.0 37.8 %collective-permute-start = (f32[3,2,512,128]{3,2,1,0:T(8,128)}, f32[3,2,512,128]{3,2,1,0:T(8,128)S(1)}, u32[]{:S(2)}, u32[]{:S(2)}) collective-permute-start(f32[3,2,512,128]{3,2,1,0:T(8,128)} %velocity.11), channel_id=1, source_target_pairs={{0,1},{1,0},{2,4},{3,5},{4,2},{5,3},{6,7},{7,6},{8,9},{9,8},{10,12... | collective-permute-start | bytes 4718600 | tf_op jit(solution)/shard_map/ppermute | solution.py:358
  8.6 0.8 %copy-start.1 = (f32[2,512,128]{2,1,0:T(8,128)}, f32[2,512,128]{2,1,0:T(8,128)S(1)}, u32[]{:S(2)}) copy-start(f32[2,512,128]{2,1,0:T(8,128)S(1)} %get-tuple-element.25.refs_3_) | copy-start | bytes 1572868
  9.4 0.8 %copy-start.3 = (f32[2,512,128]{2,1,0:T(8,128)}, f32[2,512,128]{2,1,0:T(8,128)S(1)}, u32[]{:S(2)}) copy-start(f32[2,512,128]{2,1,0:T(8,128)S(1)} %get-tuple-element.26.refs_4_) | copy-start | bytes 1572868
  10.2 0.6 %copy-start.5 = (f32[1,2,128,128]{3,2,1,0:T(8,128)}, f32[1,2,128,128]{3,2,1,0:T(8,128)S(1)}, u32[]{:S(2)}) copy-start(f32[1,2,128,128]{3,2,1,0:T(8,128)S(1)} %get-tuple-element.20) | copy-start | bytes 393220
  10.9 8.4 %collective-permute-start.3 = (f32[2,2,512,128]{3,2,1,0:T(8,128)}, f32[2,2,512,128]{3,2,1,0:T(8,128)}, u32[]{:S(2)}, u32[]{:S(2)}) collective-permute-start(f32[2,2,512,128]{3,2,1,0:T(8,128)} %get-tuple-element.22), channel_id=1, source_target_pairs={{0,2},{2,0},{4,6},{6,4},{8,10},{10,8},{12,14},{14,12},{16,18},{18,... | collective-permute-start | bytes 3145736 | tf_op jit(solution)/shard_map/ppermute | solution.py:393
  11.3 21.2 %collective-permute-start.5 = (f32[2,2,512,128]{3,2,1,0:T(8,128)}, f32[2,2,512,128]{3,2,1,0:T(8,128)S(1)}, u32[]{:S(2)}, u32[]{:S(2)}) collective-permute-start(f32[2,2,512,128]{3,2,1,0:T(8,128)} %get-tuple-element.22), channel_id=1, source_target_pairs={{0,30},{1,31},{2,3},{3,2},{4,5},{5,4},{6,8},{7,9},{8,6},{9,7},{10,... | collective-permute-start | bytes 3145736 | tf_op jit(solution)/shard_map/ppermute | solution.py:394
  12.1 5.0 %collective-permute-start.4 = (f32[1,2,512,128]{3,2,1,0:T(8,128)}, f32[1,2,512,128]{3,2,1,0:T(8,128)}, u32[]{:S(2)}, u32[]{:S(2)}) collective-permute-start(f32[1,2,512,128]{3,2,1,0:T(8,128)} %get-tuple-element.23), channel_id=1, source_target_pairs={{0,2},{2,0},{4,6},{6,4},{8,10},{10,8},{12,14},{14,12},{16,18},{18,... | collective-permute-start | bytes 1572872 | tf_op jit(solution)/shard_map/ppermute | solution.py:393
  15.0 21.4 %collective-permute-start.2 = (f32[1,2,384,128]{3,2,1,0:T(8,128)}, f32[1,2,384,128]{3,2,1,0:T(8,128)S(1)}, u32[]{:S(2)}, u32[]{:S(2)}) collective-permute-start(f32[1,2,384,128]{3,2,1,0:T(8,128)} %get-tuple-element.21), channel_id=1, source_target_pairs={{0,30},{1,31},{2,3},{3,2},{4,5},{5,4},{6,8},{7,9},{8,6},{9,7},{10,... | collective-permute-start | bytes 1179656 | tf_op jit(solution)/shard_map/ppermute | solution.py:394
  15.7 1.4 %copy-start.6 = (f32[1,2,128,128]{3,2,1,0:T(8,128)S(1)}, f32[1,2,128,128]{3,2,1,0:T(8,128)}, u32[]{:S(2)}) copy-start(f32[1,2,128,128]{3,2,1,0:T(8,128)} %copy-done.5) | copy-start | bytes 393220
  15.7 3.6 %copy-start.2 = (f32[2,512,128]{2,1,0:T(8,128)S(1)}, f32[2,512,128]{2,1,0:T(8,128)}, u32[]{:S(2)}) copy-start(f32[2,512,128]{2,1,0:T(8,128)} %copy-done.1) | copy-start | bytes 1572868
  15.7 3.6 %copy-start.4 = (f32[2,512,128]{2,1,0:T(8,128)S(1)}, f32[2,512,128]{2,1,0:T(8,128)}, u32[]{:S(2)}) copy-start(f32[2,512,128]{2,1,0:T(8,128)} %copy-done.3) | copy-start | bytes 1572868
  17.1 20.9 %collective-permute-start.1 = (f32[1,2,128,128]{3,2,1,0:T(8,128)S(1)}, f32[1,2,128,128]{3,2,1,0:T(8,128)S(1)}, u32[]{:S(2)}, u32[]{:S(2)}) collective-permute-start(f32[1,2,128,128]{3,2,1,0:T(8,128)S(1)} %copy-done.6), channel_id=1, source_target_pairs={{0,30},{1,31},{2,3},{3,2},{4,5},{5,4},{6,8},{7,9},{8,6},{9,7},{10,... | collective-permute-start | bytes 393224 | tf_op jit(solution)/shard_map/ppermute | solution.py:394
  19.3 13.2 %copy-start = (f32[3,2,512,128]{3,2,1,0:T(8,128)S(1)}, f32[3,2,512,128]{3,2,1,0:T(8,128)}, u32[]{:S(2)}) copy-start(f32[3,2,512,128]{3,2,1,0:T(8,128)} %velocity.11) | copy-start | bytes 4718596
